TPU v7x, 256 devices: a whole 4x4x8 slice. The times are simulated.
256 devices in a mesh: ctx: 64 (over z, x, core), head: 4 (over y).
Axes of the slice: x: 4, y: 4, z: 8, core: 2. Of those that a mesh axis runs over, the one named last changes fastest.
Arguments:
- queries: bfloat16 [4096, 128, 576], P('ctx', 'head'), may hold values from -40 to 40
- latent: bfloat16 [131072, 576], P('ctx'), may hold values from -8 to 8
- index_queries: bfloat16 [4096, 64, 128], P('ctx', 'head'), may hold values from -6 to 6
- index_weights: bfloat16 [4096, 64], P('ctx', 'head'), may hold values from -0.75 to 0.75
- index_keys: bfloat16 [131072, 128], P('ctx'), may hold values from -6 to 6
- request_tiles: int32 [64, 64, 2], P('ctx'), may hold values from 0 to 15, as said below
- selection: int32 [4096, 16], P('ctx'), may hold values from 0 to 127, as said below
Outputs:
- attended: bfloat16 [4096, 128, 512], P('ctx', 'head')
- index_scores: float32 [4096, 2048], P('ctx', 'head')
Inputs may be any that keep to these rules, and one draw needn't show every extreme that they name: `request_tiles`: entry [r, o, c] is a tile number local to owner o, all different for one r and o. Live slots are a leading run of each owner's slots; all 2 slots of an owner are live unless the owner holds fewer than 2 tiles at or before the tile of device r's last query. `selection`: row q lists 16 different live request slots of device q // 64. Their tiles lie at or before the tile holding position 126976 + q, and that tile is one of them.
All inputs are finite; a program needn't handle non-finite values.
Results may differ from a plain program's by a relative error of at most 0.007.
Values may be sent and summed in bfloat16 or wider, within the bound.
No kernel may reach another device: no remote copies, remote signals or barrier semaphores. Data moves between devices by JAX's collectives and lax.ppermute only.
A program may use at most 128 MiB of HBM per device.

v0:
```python
import math

import jax
import jax.numpy as jnp
from jax import lax
from jax.sharding import PartitionSpec as P

KEY_VALUE_RANK = 512
TILE = 128


score_scale = 192.0 ** (-0.5)


def shards(queries, latent, index_queries, index_weights, index_keys, request_tiles, selection):
    ctx_count = lax.axis_size("ctx")
    query_count, local_heads, latent_width = queries.shape
    key_width = index_keys.shape[1]
    tile_count = latent.shape[0] // TILE
    capacity = request_tiles.shape[2]
    wanted = request_tiles[0]
    latent_tiles = latent.reshape(tile_count, TILE, latent_width)
    key_tiles = index_keys.reshape(tile_count, TILE, key_width)
    asked_tiles = lax.all_to_all(wanted, "ctx", split_axis=0, concat_axis=0, tiled=True)
    fetched = lax.all_to_all(
        latent_tiles[asked_tiles], "ctx", split_axis=0, concat_axis=0, tiled=True
    )
    fetched_keys = lax.all_to_all(
        key_tiles[asked_tiles], "ctx", split_axis=0, concat_axis=0, tiled=True
    )
    slot_total = ctx_count * capacity
    fetched = fetched.reshape(slot_total, TILE, latent_width)
    fetched_keys = fetched_keys.reshape(slot_total, TILE, key_width)
    owner_ids = selection // capacity
    flat_wanted = wanted.reshape(-1)
    matches = selection[:, :, None] == jnp.arange(slot_total, dtype=jnp.int32)[None, None, :]
    local_tile = jnp.sum(jnp.where(matches, flat_wanted[None, None, :], 0), axis=2)
    global_tile = owner_ids * tile_count + local_tile
    key_pos = (
        global_tile[:, :, None] * TILE + jnp.arange(TILE, dtype=jnp.int32)[None, None, :]
    ).reshape(query_count, -1)
    top_total = key_pos.shape[1]
    context = ctx_count * tile_count * TILE
    query_pos = (
        context
        - ctx_count * query_count
        + lax.axis_index("ctx") * query_count
        + jnp.arange(query_count, dtype=jnp.int32)
    )
    visible = key_pos <= query_pos[:, None]
    index_heads_here = index_queries.shape[1]
    block_rows = math.gcd(query_count, 8)
    blocks = query_count // block_rows

    def attend(pieces):
        query_block, index_query_block, iw_block, sel_block, vis_block = pieces
        gathered = fetched[sel_block].reshape(block_rows, top_total, latent_width)
        collected_keys = fetched_keys[sel_block].reshape(block_rows, top_total, key_width)
        scores = (
            jnp.einsum("bhl,bkl->bhk", query_block, gathered, preferred_element_type=jnp.float32)
            * score_scale
        )
        scores = jnp.where(vis_block[:, None, :], scores, -1e30)
        row_peak = jnp.max(scores, axis=2, keepdims=True)
        weights = jnp.exp(scores - row_peak)
        probabilities = (weights / jnp.sum(weights, axis=2, keepdims=True)).astype(jnp.bfloat16)
        attended = jnp.einsum(
            "bhk,bkv->bhv",
            probabilities,
            gathered[:, :, :KEY_VALUE_RANK],
            preferred_element_type=jnp.float32,
        ).astype(jnp.bfloat16)
        key_products = jnp.einsum(
            "urc,ulc->url", index_query_block, collected_keys, preferred_element_type=jnp.float32
        )
        relu_dots = jnp.maximum(key_products, 0.0) * key_width ** (-0.5)
        summed_total = jnp.einsum("bg,bgk->bk", iw_block.astype(jnp.float32), relu_dots)
        return (attended, jnp.where(vis_block, summed_total, 0.0))

    shaped = (
        queries.reshape(blocks, block_rows, local_heads, latent_width),
        index_queries.reshape(blocks, block_rows, index_heads_here, key_width),
        index_weights.reshape(blocks, block_rows, index_heads_here),
        selection.reshape(blocks, block_rows, selection.shape[1]),
        visible.reshape(blocks, block_rows, top_total),
    )
    attended, index_portion = lax.map(attend, shaped)
    attended = attended.reshape(query_count, local_heads, KEY_VALUE_RANK)
    index_portion = index_portion.reshape(query_count, top_total)
    index_scores = lax.psum_scatter(index_portion, "head", scatter_dimension=1, tiled=True)
    return (attended, index_scores)


def solution(mesh):
    return jax.shard_map(
        shards,
        mesh=mesh,
        in_specs=(
            P("ctx", "head", None),
            P("ctx", None),
            P("ctx", "head", None),
            P("ctx", "head"),
            P("ctx", None),
            P("ctx", None, None),
            P("ctx", None),
        ),
        out_specs=(P("ctx", "head", None), P("ctx", "head")),
        check_vma=False,
    )
```

profile of v0, /device:TPU:2, one launch (start us, length us, event | category | flops | bytes accessed | tf_op | source)
XLA Modules:
  0.0 961.6 jit_solution(11475289211068689763)
XLA Ops:
  7.2 1.5 copy.53
  8.7 12.0 %all-to-all-start = ((s32[64,1,2]{2,1,0:T(1,128)}), s32[64,1,2]{2,1,0:T(1,128)S(1)}, u32[]{:S(2)}, u32[]{:S(2)}) async-start(s32[64,1,2]{2,1,0:T(1,128)} %copy.53), calls=%async_computation | async-start | bytes 65536 | tf_op jit(solution)/shard_map/all_to_all | solution.py:24
  20.7 2.0 copy_bitcast_fusion
  22.8 6.5 all-to-all-done
  29.6 10.8 %gather_fusion.2 = bf16[128,128,576]{1,2,0:T(8,128)(2,1)} fusion(bf16[16,128,576]{1,2,0:T(8,128)(2,1)} %copy_bitcast_fusion, s32[1024]{0:T(1024)S(1)} %pad_clamp_fusion.1), kind=kCustom, calls=%fused_computation.2 | custom fusion | bytes 37749248 | tf_op jit(solution)/shard_map/gather | solution.py:26
  40.4 6.9 all-to-all-start.1
  47.3 3.1 gather_fusion.3
  50.4 403.3 %all-to-all-done.1 = bf16[64,2,128,576]{2,3,1,0:T(8,128)(2,1)} async-done(((bf16[64,2,128,576]{2,3,1,0:T(8,128)(2,1)}), bf16[64,2,128,576]{2,3,1,0:T(8,128)(2,1)}, u32[]{:S(2)}, u32[]{:S(2)}) %all-to-all-start.1) | async-done | bytes 18874400 | tf_op jit(solution)/shard_map/all_to_all | solution.py:25
  453.8 20.7 %all-to-all-start.2 = ((bf16[64,2,128,128]{3,2,1,0:T(8,128)(2,1)}), bf16[64,2,128,128]{3,2,1,0:T(8,128)(2,1)}, u32[]{:S(2)}, u32[]{:S(2)}) async-start(bf16[64,2,128,128]{3,2,1,0:T(8,128)(2,1)} %bitcast.93), calls=%async_computation.2 | async-start | bytes 8388608 | tf_op jit(solution)/shard_map/all_to_all | solution.py:28
  475.1 1.3 select_reduce_fusion
  476.9 26.8 %copy.57 = bf16[64,2,128,576]{3,2,1,0:T(8,128)(2,1)} copy(bf16[64,2,128,576]{2,3,1,0:T(8,128)(2,1)} %all-to-all-done.1) | data formatting | bytes 37748736 | tf_op jit(solution)/shard_map/all_to_all | solution.py:25
  503.7 66.8 %all-to-all-done.2 = bf16[64,2,128,128]{3,2,1,0:T(8,128)(2,1)} async-done(((bf16[64,2,128,128]{3,2,1,0:T(8,128)(2,1)}), bf16[64,2,128,128]{3,2,1,0:T(8,128)(2,1)}, u32[]{:S(2)}, u32[]{:S(2)}) %all-to-all-start.2) | async-done | bytes 4194336 | tf_op jit(solution)/shard_map/all_to_all | solution.py:28
  570.6 363.7 %while.12 = (s32[]{:T(128)}, bf16[8,8,32,512]{3,2,1,0:T(8,128)(2,1)}, f32[8,8,2048]{2,1,0:T(8,128)}, pred[8,8,2048]{2,1,0:T(8,128)(4,1)S(1)}, bf16[8,8,32,576]{3...) while((s32[]{:T(128)}, ...), condition=%wide.region_4.5_spmd, body=%wide.region_1.4_spmd.sunk | while | flops 1212831360 | bytes 97367424 | solution.py:87
  570.7 5.3 gather_fusion.1
  576.0 3.5 fusion.67
  579.5 0.6 bitcast_dynamic-update-slice_fusion.2
  580.1 17.0 %gather_fusion = bf16[128,128,576]{2,1,0:T(8,128)(2,1)} fusion(bf16[128,128,576]{2,1,0:T(8,128)(2,1)} %get-tuple-element.166, s32[1024]{0:T(1024)S(1)} %pad_clamp_fusion.3), kind=kCustom, calls=%fused_computation.clone.1 | custom fusion | bytes 37749248 | tf_op jit(solution)/shard_map/while/body/eval_jaxpr/gather | solution.py:57
  597.2 10.4 %fusion.64 = f32[8,32,2048]{2,1,0:T(8,128)S(1)} fusion(bf16[8,2048,576]{2,1,0:T(8,128)(2,1)} %bitcast.87, pred[8,2048]{1,0:T(8,128)(4,1)S(1)} %dynamic-slice_bitcast_fusion.4, bf16[8,8,32,576]{3,2,1,0:T(8,128)(2,1)} %get-tuple-element.164, s32[]{:T(128)S(6)} %copy.76), kind=kOutput, calls=%fused_computation.10.clone.1 | convolution fusion | flops 605028352 | bytes 23412740 | tf_op jit(solution)/shard_map/while/body/eval_jaxpr/bhl,bkl->bhk/dot_general | solution.py:60
  608.1 7.9 fusion.66
  616.1 5.3 gather_fusion.1
  621.4 3.5 fusion.67
  624.9 0.6 bitcast_dynamic-update-slice_fusion.2
  625.6 17.1 %gather_fusion = bf16[128,128,576]{2,1,0:T(8,128)(2,1)} fusion(bf16[128,128,576]{2,1,0:T(8,128)(2,1)} %get-tuple-element.166, s32[1024]{0:T(1024)S(1)} %pad_clamp_fusion.3), kind=kCustom, calls=%fused_computation.clone.1 | custom fusion | bytes 37749248 | tf_op jit(solution)/shard_map/while/body/eval_jaxpr/gather | solution.py:57
  642.6 10.4 %fusion.64 = f32[8,32,2048]{2,1,0:T(8,128)S(1)} fusion(bf16[8,2048,576]{2,1,0:T(8,128)(2,1)} %bitcast.87, pred[8,2048]{1,0:T(8,128)(4,1)S(1)} %dynamic-slice_bitcast_fusion.4, bf16[8,8,32,576]{3,2,1,0:T(8,128)(2,1)} %get-tuple-element.164, s32[]{:T(128)S(6)} %copy.76), kind=kOutput, calls=%fused_computation.10.clone.1 | convolution fusion | flops 605028352 | bytes 23412740 | tf_op jit(solution)/shard_map/while/body/eval_jaxpr/bhl,bkl->bhk/dot_general | solution.py:60
  653.1 0.5 fusion.65
  653.5 7.9 fusion.66
  661.6 5.3 gather_fusion.1
  666.9 3.5 fusion.67
  670.4 0.6 bitcast_dynamic-update-slice_fusion.2
  671.0 17.1 %gather_fusion = bf16[128,128,576]{2,1,0:T(8,128)(2,1)} fusion(bf16[128,128,576]{2,1,0:T(8,128)(2,1)} %get-tuple-element.166, s32[1024]{0:T(1024)S(1)} %pad_clamp_fusion.3), kind=kCustom, calls=%fused_computation.clone.1 | custom fusion | bytes 37749248 | tf_op jit(solution)/shard_map/while/body/eval_jaxpr/gather | solution.py:57
  688.1 10.4 %fusion.64 = f32[8,32,2048]{2,1,0:T(8,128)S(1)} fusion(bf16[8,2048,576]{2,1,0:T(8,128)(2,1)} %bitcast.87, pred[8,2048]{1,0:T(8,128)(4,1)S(1)} %dynamic-slice_bitcast_fusion.4, bf16[8,8,32,576]{3,2,1,0:T(8,128)(2,1)} %get-tuple-element.164, s32[]{:T(128)S(6)} %copy.76), kind=kOutput, calls=%fused_computation.10.clone.1 | convolution fusion | flops 605028352 | bytes 23412740 | tf_op jit(solution)/shard_map/while/body/eval_jaxpr/bhl,bkl->bhk/dot_general | solution.py:60
  699.0 7.9 fusion.66
  707.1 5.3 gather_fusion.1
  712.3 3.5 fusion.67
  715.9 0.7 bitcast_dynamic-update-slice_fusion.2
  716.5 17.1 %gather_fusion = bf16[128,128,576]{2,1,0:T(8,128)(2,1)} fusion(bf16[128,128,576]{2,1,0:T(8,128)(2,1)} %get-tuple-element.166, s32[1024]{0:T(1024)S(1)} %pad_clamp_fusion.3), kind=kCustom, calls=%fused_computation.clone.1 | custom fusion | bytes 37749248 | tf_op jit(solution)/shard_map/while/body/eval_jaxpr/gather | solution.py:57
  733.6 10.4 %fusion.64 = f32[8,32,2048]{2,1,0:T(8,128)S(1)} fusion(bf16[8,2048,576]{2,1,0:T(8,128)(2,1)} %bitcast.87, pred[8,2048]{1,0:T(8,128)(4,1)S(1)} %dynamic-slice_bitcast_fusion.4, bf16[8,8,32,576]{3,2,1,0:T(8,128)(2,1)} %get-tuple-element.164, s32[]{:T(128)S(6)} %copy.76), kind=kOutput, calls=%fused_computation.10.clone.1 | convolution fusion | flops 605028352 | bytes 23412740 | tf_op jit(solution)/shard_map/while/body/eval_jaxpr/bhl,bkl->bhk/dot_general | solution.py:60
  744.0 0.5 fusion.65
  744.5 7.9 fusion.66
  752.5 5.3 gather_fusion.1
  757.8 3.5 fusion.67
  761.3 0.7 bitcast_dynamic-update-slice_fusion.2
  762.0 17.0 %gather_fusion = bf16[128,128,576]{2,1,0:T(8,128)(2,1)} fusion(bf16[128,128,576]{2,1,0:T(8,128)(2,1)} %get-tuple-element.166, s32[1024]{0:T(1024)S(1)} %pad_clamp_fusion.3), kind=kCustom, calls=%fused_computation.clone.1 | custom fusion | bytes 37749248 | tf_op jit(solution)/shard_map/while/body/eval_jaxpr/gather | solution.py:57
  779.0 10.4 %fusion.64 = f32[8,32,2048]{2,1,0:T(8,128)S(1)} fusion(bf16[8,2048,576]{2,1,0:T(8,128)(2,1)} %bitcast.87, pred[8,2048]{1,0:T(8,128)(4,1)S(1)} %dynamic-slice_bitcast_fusion.4, bf16[8,8,32,576]{3,2,1,0:T(8,128)(2,1)} %get-tuple-element.164, s32[]{:T(128)S(6)} %copy.76), kind=kOutput, calls=%fused_computation.10.clone.1 | convolution fusion | flops 605028352 | bytes 23412740 | tf_op jit(solution)/shard_map/while/body/eval_jaxpr/bhl,bkl->bhk/dot_general | solution.py:60
  789.9 7.9 fusion.66
  798.0 5.3 gather_fusion.1
  803.2 3.5 fusion.67
  806.8 0.7 bitcast_dynamic-update-slice_fusion.2
  807.4 17.0 %gather_fusion = bf16[128,128,576]{2,1,0:T(8,128)(2,1)} fusion(bf16[128,128,576]{2,1,0:T(8,128)(2,1)} %get-tuple-element.166, s32[1024]{0:T(1024)S(1)} %pad_clamp_fusion.3), kind=kCustom, calls=%fused_computation.clone.1 | custom fusion | bytes 37749248 | tf_op jit(solution)/shard_map/while/body/eval_jaxpr/gather | solution.py:57
  824.5 10.4 %fusion.64 = f32[8,32,2048]{2,1,0:T(8,128)S(1)} fusion(bf16[8,2048,576]{2,1,0:T(8,128)(2,1)} %bitcast.87, pred[8,2048]{1,0:T(8,128)(4,1)S(1)} %dynamic-slice_bitcast_fusion.4, bf16[8,8,32,576]{3,2,1,0:T(8,128)(2,1)} %get-tuple-element.164, s32[]{:T(128)S(6)} %copy.76), kind=kOutput, calls=%fused_computation.10.clone.1 | convolution fusion | flops 605028352 | bytes 23412740 | tf_op jit(solution)/shard_map/while/body/eval_jaxpr/bhl,bkl->bhk/dot_general | solution.py:60
  835.4 7.9 fusion.66
  843.4 5.3 gather_fusion.1
  848.7 3.5 fusion.67
  852.2 0.6 bitcast_dynamic-update-slice_fusion.2
  852.9 17.1 %gather_fusion = bf16[128,128,576]{2,1,0:T(8,128)(2,1)} fusion(bf16[128,128,576]{2,1,0:T(8,128)(2,1)} %get-tuple-element.166, s32[1024]{0:T(1024)S(1)} %pad_clamp_fusion.3), kind=kCustom, calls=%fused_computation.clone.1 | custom fusion | bytes 37749248 | tf_op jit(solution)/shard_map/while/body/eval_jaxpr/gather | solution.py:57
  869.9 10.4 %fusion.64 = f32[8,32,2048]{2,1,0:T(8,128)S(1)} fusion(bf16[8,2048,576]{2,1,0:T(8,128)(2,1)} %bitcast.87, pred[8,2048]{1,0:T(8,128)(4,1)S(1)} %dynamic-slice_bitcast_fusion.4, bf16[8,8,32,576]{3,2,1,0:T(8,128)(2,1)} %get-tuple-element.164, s32[]{:T(128)S(6)} %copy.76), kind=kOutput, calls=%fused_computation.10.clone.1 | convolution fusion | flops 605028352 | bytes 23412740 | tf_op jit(solution)/shard_map/while/body/eval_jaxpr/bhl,bkl->bhk/dot_general | solution.py:60
  880.8 7.9 fusion.66
  888.9 5.3 gather_fusion.1
  894.2 3.5 fusion.67
  897.7 0.6 bitcast_dynamic-update-slice_fusion.2
  898.3 17.1 %gather_fusion = bf16[128,128,576]{2,1,0:T(8,128)(2,1)} fusion(bf16[128,128,576]{2,1,0:T(8,128)(2,1)} %get-tuple-element.166, s32[1024]{0:T(1024)S(1)} %pad_clamp_fusion.3), kind=kCustom, calls=%fused_computation.clone.1 | custom fusion | bytes 37749248 | tf_op jit(solution)/shard_map/while/body/eval_jaxpr/gather | solution.py:57
  915.4 10.4 %fusion.64 = f32[8,32,2048]{2,1,0:T(8,128)S(1)} fusion(bf16[8,2048,576]{2,1,0:T(8,128)(2,1)} %bitcast.87, pred[8,2048]{1,0:T(8,128)(4,1)S(1)} %dynamic-slice_bitcast_fusion.4, bf16[8,8,32,576]{3,2,1,0:T(8,128)(2,1)} %get-tuple-element.164, s32[]{:T(128)S(6)} %copy.76), kind=kOutput, calls=%fused_computation.10.clone.1 | convolution fusion | flops 605028352 | bytes 23412740 | tf_op jit(solution)/shard_map/while/body/eval_jaxpr/bhl,bkl->bhk/dot_general | solution.py:60
  926.3 7.9 fusion.66
  934.3 20.5 %reduce-scatter.2.cloned.1.call-done = f32[64,512]{1,0:T(8,128)} async-done(((f32[64,2048]{1,0:T(8,128)}), f32[64,512]{1,0:T(8,128)}) %reduce-scatter.2.cloned.1.call-update) | async-done | bytes 131088 | tf_op jit(solution)/shard_map/reduce_scatter | solution.py:90
  (77 shorter events, 5.0 us)
Async XLA Ops:
  7.2 13.6 %copy-start = (bf16[2048,576]{0,1:T(8,128)(2,1)S(1)}, bf16[2048,576]{0,1:T(8,128)(2,1)}, u32[]{:S(2)}) copy-start(bf16[2048,576]{0,1:T(8,128)(2,1)} %param.10) | copy-start | bytes 7077892
  8.7 20.5 %all-to-all-start = ((s32[64,1,2]{2,1,0:T(1,128)}), s32[64,1,2]{2,1,0:T(1,128)S(1)}, u32[]{:S(2)}, u32[]{:S(2)}) async-start(s32[64,1,2]{2,1,0:T(1,128)} %copy.53), calls=%async_computation | async-start | bytes 65536 | tf_op jit(solution)/shard_map/all_to_all | solution.py:24
  40.4 6.9 copy-start.2
  40.4 413.3 %all-to-all-start.1 = ((bf16[64,2,128,576]{2,3,1,0:T(8,128)(2,1)}), bf16[64,2,128,576]{2,3,1,0:T(8,128)(2,1)}, u32[]{:S(2)}, u32[]{:S(2)}) async-start(bf16[64,2,128,576]{2,3,1,0:T(8,128)(2,1)} %bitcast.91), calls=%async_computation.1 | async-start | bytes 37748736 | tf_op jit(solution)/shard_map/all_to_all | solution.py:25
  453.8 20.9 %copy-start.5 = (s32[1,64,2]{1,2,0:T(2,128)S(1)}, s32[1,64,2]{1,2,0:T(2,128)}, u32[]{:S(2)}) copy-start(s32[1,64,2]{1,2,0:T(2,128)} %param.14) | copy-start | bytes 1540
  453.8 21.0 %copy-start.4 = (bf16[64,16]{0,1:T(8,128)(2,1)S(1)}, bf16[64,16]{0,1:T(8,128)(2,1)}, u32[]{:S(2)}) copy-start(bf16[64,16]{0,1:T(8,128)(2,1)} %param.12) | copy-start | bytes 6148
  453.8 21.1 %copy-start.3 = (s32[64,16]{0,1:T(8,128)S(1)}, s32[64,16]{0,1:T(8,128)}, u32[]{:S(2)}) copy-start(s32[64,16]{0,1:T(8,128)} %param.15) | copy-start | bytes 12292
  453.8 116.8 %all-to-all-start.2 = ((bf16[64,2,128,128]{3,2,1,0:T(8,128)(2,1)}), bf16[64,2,128,128]{3,2,1,0:T(8,128)(2,1)}, u32[]{:S(2)}, u32[]{:S(2)}) async-start(bf16[64,2,128,128]{3,2,1,0:T(8,128)(2,1)} %bitcast.93), calls=%async_computation.2 | async-start | bytes 8388608 | tf_op jit(solution)/shard_map/all_to_all | solution.py:28
  474.4 480.3 %reduce-scatter.2.cloned.1.call-start = ((), (), s32[]{:S(2)}) async-start(), calls=%async_computation.4 | async-start | bytes 655360 | tf_op jit(solution)/shard_map/reduce_scatter | solution.py:90
  934.2 20.5 %copy-start.1 = (bf16[2048,576]{0,1:T(8,128)(2,1)S(1)}, bf16[2048,576]{0,1:T(8,128)(2,1)}, u32[]{:S(2)}) copy-start(bf16[2048,576]{0,1:T(8,128)(2,1)} %param.10) | copy-start | bytes 7077892
Sparse Core Ops, SparseCore 0:
  934.4 20.3 reduce-scatter.1
where the time goes:
time: 963 us; the launch traced here: 962 us
  waiting for transfers between devices  497 us (52%)
  local copies, waits for them, and re-layouts  225 us (23%)
  matrix products  175 us (18%)
  starting transfers between devices  39.8 us (4%)
  between operations  14.2 us (1%)
  other arithmetic  10.4 us (1%)
    all_to_all x1, waiting for transfers between devices, shards(): lax.all_to_all(latent_tiles[asked_tiles], 'ctx', split_axis=0, concat_axi...  403 us
    gather x8, local copies, waits for them, and re-layouts, attend(): gathered = fetched[sel_block].reshape(block_rows, top_total, latent_width)  136 us
    dot_general x8, matrix products, attend(): jnp.einsum('bhl,bkl->bhk', query_block, gathered, preferred_element_type=...  83.5 us
    all_to_all x1, waiting for transfers between devices, shards(): lax.all_to_all(key_tiles[asked_tiles], 'ctx', split_axis=0, concat_axis=0...  66.8 us
    dot_general x8, matrix products, attend(): jnp.einsum('bhk,bkv->bhv', probabilities, gathered[:, :, :KEY_VALUE_RANK]...  63.5 us
    gather x8, local copies, waits for them, and re-layouts, attend(): fetched_keys[sel_block].reshape(block_rows, top_total, key_width)  42.2 us
    dot_general x8, matrix products, attend(): jnp.einsum('bg,bgk->bk', iw_block.astype(jnp.float32), relu_dots)  28.2 us
    all_to_all x1, local copies, waits for them, and re-layouts, shards(): lax.all_to_all(latent_tiles[asked_tiles], 'ctx', split_axis=0, concat_axi...  26.8 us
  transfers between devices with their start and end apart: 4, of which 4 were waited for; matrix products, arithmetic and copies ran while one was open for 4% of the time, Pallas kernels for 0%

commit v1 on v0

v1 whole, which is shorter than its diff:
```python
import functools

import jax
import jax.numpy as jnp
from jax import lax
from jax.experimental import pallas as pl
from jax.experimental.pallas import tpu as pltpu
from jax.sharding import Mesh, PartitionSpec as P

KEY_VALUE_RANK = 512
LATENT = 576
INDEX_AT = 640
WIDTH = 768
TILE = 128
CAP = 2
GROUP = 8
SCALE = 192.0 ** -0.5
LOG2_E = 1.4426950408889634
MASKED = -1e30


def attend_kernel(sel, q, iq, weight_t, lim, *refs):
    fetched, (out, lse, index_out, rows, picked_a, picked_b, sems) = refs[:-7], refs[-7:]
    step = pl.program_id(0)
    part = rows.shape[0] // (sel.shape[1] * 8)
    picks = sel.shape[1]
    heads = q.shape[0] * q.shape[2]
    index_heads = iq.shape[0] * iq.shape[2]

    @pl.when(step == 0)
    def _():
        copies, at = [], 0
        for i, ref in enumerate(fetched):
            size = ref.shape[0]
            copies.append(pltpu.make_async_copy(ref, rows.at[pl.ds(at, size)], sems.at[i]))
            at += size
        for copy in copies:
            copy.start()
        for copy in copies:
            copy.wait()

    lane = lax.broadcasted_iota(jnp.int32, (heads, 128), 1)
    weight_lane = lax.broadcasted_iota(jnp.int32, weight_t.shape, 1)
    lse_columns = jnp.zeros((heads, 128), jnp.float32)
    for i in range(GROUP):
        picked = (picked_a, picked_b)[i % 2]
        query = step * GROUP + i
        for k in range(picks):
            start = pl.multiple_of(sel[query, k] * part, part)
            picked[pl.ds(k * part, part), :] = rows[pl.ds(start, part), :]
        visible = lim[pl.ds(i, 1), :] >= 0
        scores = lax.dot_general(
            q[:, i].reshape(heads, LATENT),
            picked[:, :LATENT],
            (((1,), (1,)), ((), ())),
            preferred_element_type=jnp.float32,
        )
        scores = jnp.where(visible, scores * (SCALE * LOG2_E), MASKED)
        peak = jnp.max(scores, axis=1, keepdims=True)
        probs = jnp.exp2(scores - peak)
        total = jnp.sum(probs, axis=1, keepdims=True)
        summed = jnp.dot(
            probs.astype(jnp.bfloat16), picked[:, :KEY_VALUE_RANK], preferred_element_type=jnp.float32
        )
        summed = (summed * (1.0 / total)).astype(jnp.bfloat16)
        out[:, i] = summed.reshape(q.shape[0], q.shape[2], KEY_VALUE_RANK)
        lse_columns = jnp.where(lane == i, peak + jnp.log2(total), lse_columns)
        dots = lax.dot_general(
            iq[:, i].reshape(index_heads, iq.shape[3]),
            picked[:, INDEX_AT:],
            (((1,), (1,)), ((), ())),
            preferred_element_type=jnp.float32,
        )
        weight = jnp.sum(jnp.where(weight_lane == query, weight_t[...], 0.0), axis=1, keepdims=True)
        index_row = jnp.sum(jnp.maximum(dots, 0.0) * weight, axis=0, keepdims=True)
        index_out[pl.ds(i, 1), :] = jnp.where(visible, index_row, 0.0)
    lse[...] = jnp.transpose(lse_columns)[:GROUP]


def attend(sel, q, iq, weight_t, lim, fetched):
    ways, queries, heads, width = q.shape
    picks = sel.shape[1]
    part = lim.shape[1] // picks
    slots = sum(f.shape[0] for f in fetched) // part
    grid = queries // GROUP
    spec = pltpu.PrefetchScalarGridSpec(
        num_scalar_prefetch=1,
        grid=(grid,),
        in_specs=[
            pl.BlockSpec((ways, GROUP, heads, width), lambda i, s: (0, i, 0, 0)),
            pl.BlockSpec((ways, GROUP) + iq.shape[2:], lambda i, s: (0, i, 0, 0)),
            pl.BlockSpec(weight_t.shape, lambda i, s: (0, 0)),
            pl.BlockSpec((GROUP, lim.shape[1]), lambda i, s: (i, 0)),
        ]
        + [pl.BlockSpec(memory_space=pl.ANY)] * len(fetched),
        out_specs=[
            pl.BlockSpec((ways, GROUP, heads, KEY_VALUE_RANK), lambda i, s: (0, i, 0, 0)),
            pl.BlockSpec((GROUP, ways * heads), lambda i, s: (i, 0)),
            pl.BlockSpec((GROUP, lim.shape[1]), lambda i, s: (i, 0)),
        ],
        scratch_shapes=[
            pltpu.VMEM((slots * part, WIDTH), jnp.bfloat16),
            pltpu.VMEM((picks * part, WIDTH), jnp.bfloat16),
            pltpu.VMEM((picks * part, WIDTH), jnp.bfloat16),
            pltpu.SemaphoreType.DMA((len(fetched),)),
        ],
    )
    return pl.pallas_call(
        attend_kernel,
        grid_spec=spec,
        out_shape=[
            jax.ShapeDtypeStruct((ways, queries, heads, KEY_VALUE_RANK), jnp.bfloat16),
            jax.ShapeDtypeStruct((queries, ways * heads), jnp.float32),
            jax.ShapeDtypeStruct((queries, lim.shape[1]), jnp.float32),
        ],
        compiler_params=pltpu.CompilerParams(vmem_limit_bytes=48 * 1024 * 1024),
        name="attend",
    )(sel, q, iq, weight_t, lim, *fetched)


def ring_blocks(block, axis, size):
    forward = [(i, (i + 1) % size) for i in range(size)]
    backward = [(i, (i - 1) % size) for i in range(size)]
    up = down = block
    got = {0: block}
    for d in range(1, size // 2):
        up = lax.ppermute(up, axis, forward)
        down = lax.ppermute(down, axis, backward)
        got[size - d], got[d] = up, down
    half = block.shape[0] // 2
    got[size // 2] = jnp.concatenate(
        [lax.ppermute(up[:half], axis, forward), lax.ppermute(down[half:], axis, backward)]
    )
    return got


def rounds_of(size):
    rounds = [[0, 1, size - 1]]
    rounds += [[d, size - d] for d in range(2, size // 2)]
    return rounds + [[size // 2]]


def shards(queries, latent, index_queries, index_weights, index_keys, request_tiles, selection):
    z_count, x_count, c_count, y_count = (lax.axis_size(a) for a in ("z", "x", "c", "y"))
    z, x, c, y = (lax.axis_index(a) for a in ("z", "x", "c", "y"))
    plane = x_count * c_count
    here = x * c_count + c
    query_count, local_heads, _ = queries.shape
    tile_count = latent.shape[0] // TILE
    part = TILE // y_count
    picks = selection.shape[1]

    own_rows = lax.dynamic_index_in_dim(latent.reshape(tile_count, y_count, part, LATENT), y, 1, False)
    own_keys = lax.dynamic_index_in_dim(index_keys.reshape(tile_count, y_count, part, -1), y, 1, False)
    padding = jnp.zeros((tile_count, part, INDEX_AT - LATENT), own_rows.dtype)
    own = jnp.concatenate([own_rows, padding, own_keys], axis=2)

    all_queries = lax.all_gather(queries, "y")
    all_index_queries = lax.all_gather(index_queries, "y")
    all_index_weights = lax.all_gather(index_weights, "y")

    wanted = request_tiles[0]
    plans = lax.all_gather(wanted, ("x", "c")).reshape(plane, z_count, plane, CAP)
    plans = lax.dynamic_index_in_dim(plans, here, 2, False)

    blocks = ring_blocks(own, "z", z_count)
    fetched = []
    place = {}
    base = 0
    for distances in rounds_of(z_count):
        found = []
        for p, d in enumerate(distances):
            asked = lax.dynamic_index_in_dim(plans, (z + d) % z_count, 1, False)
            found.append(blocks[d][asked])
            place[d] = (base + p * CAP, len(distances) * CAP)
        found = jnp.stack(found, axis=1).reshape(plane, -1, WIDTH)
        moved = lax.all_to_all(found, ("x", "c"), split_axis=0, concat_axis=0, tiled=True)
        fetched.append(moved.reshape(-1, WIDTH))
        base += plane * len(distances) * CAP

    owner = selection // CAP
    distance = (owner // plane - z) % z_count
    first = sum(jnp.where(distance == d, place[d][0], 0) for d in place)
    stride = sum(jnp.where(distance == d, place[d][1], 0) for d in place)
    rows_at = first + (owner % plane) * stride + selection % CAP

    flat_wanted = wanted.reshape(-1)
    matches = selection[:, :, None] == jnp.arange(flat_wanted.shape[0], dtype=jnp.int32)
    local_tile = jnp.sum(jnp.where(matches, flat_wanted, 0), axis=2)
    tile_start = (owner * tile_count + local_tile) * TILE + y * part
    ctx_count = z_count * plane
    context = ctx_count * tile_count * TILE
    query_pos = (
        context
        - ctx_count * query_count
        + (z * plane + here) * query_count
        + jnp.arange(query_count, dtype=jnp.int32)
    )
    lim = (query_pos[:, None] - tile_start)[:, :, None] - jnp.arange(part, dtype=jnp.int32)
    lim = lim.reshape(query_count, picks * part)

    key_scale = index_keys.shape[1] ** -0.5
    weight_t = jnp.transpose(all_index_weights.astype(jnp.float32), (0, 2, 1)).reshape(-1, query_count) * key_scale

    partial, lse, index_part = attend(rows_at, all_queries, all_index_queries, weight_t, lim, fetched)

    lse = jnp.transpose(lse.reshape(query_count, y_count, local_heads), (1, 0, 2))
    index_part = jnp.transpose(index_part.reshape(query_count, y_count, -1), (1, 0, 2))
    small = jnp.concatenate([lse, index_part], axis=2)
    small = lax.all_to_all(small, "y", split_axis=0, concat_axis=0, tiled=True)
    partial = lax.all_to_all(partial, "y", split_axis=0, concat_axis=0, tiled=True)
    lse, index_part = small[:, :, :local_heads], small[:, :, local_heads:]
    share = jnp.exp2(lse - jnp.max(lse, axis=0))
    share = share / jnp.sum(share, axis=0)
    attended = jnp.sum(partial.astype(jnp.float32) * share[..., None], axis=0).astype(jnp.bfloat16)
    index_scores = jnp.transpose(
        index_part.reshape(y_count, query_count, picks // y_count, part), (1, 2, 0, 3)
    ).reshape(query_count, -1)
    return attended, index_scores


def solution(mesh):
    ctx, head = mesh.devices.shape
    x_count, c_count = 4, 2
    grid = Mesh(
        mesh.devices.reshape(ctx // (x_count * c_count), x_count, c_count, head), ("z", "x", "c", "y")
    )
    ctx_axes = ("z", "x", "c")
    return jax.shard_map(
        shards,
        mesh=grid,
        in_specs=(
            P(ctx_axes, "y", None),
            P(ctx_axes, None),
            P(ctx_axes, "y", None),
            P(ctx_axes, "y"),
            P(ctx_axes, None),
            P(ctx_axes, None, None),
            P(ctx_axes, None),
        ),
        out_specs=(P(ctx_axes, "y", None), P(ctx_axes, "y")),
        check_vma=False,
    )
```

time: 963 us -> 326 us (0.34)
  waiting for transfers between devices: 497 us -> 152 us
  local copies, waits for them, and re-layouts: 225 us -> 32 us
  matrix products: 175 us -> 0 us
  Pallas kernels: 0 us -> 40.5 us
  blocking collectives: 0 us -> 32 us
    all_to_all x3 -> x5, waiting for transfers between devices: 477 us -> 100 us  [the longest x1 91.4 us: shards(): lax.all_to_all(partial, 'y', split_axis=0, concat_axis=0, tiled=True)]
    gather x18 -> x8, local copies, waits for them, and re-layouts: 193 us -> 13.1 us  [shards(): found.append(blocks[d][asked])]
    dot_general x24 -> x0, matrix products: 175 us -> none  [the longest x8 83.5 us: attend(): jnp.einsum('bhl,bkl->bhk', query_block, gathered, preferred_element_type=...]
    ppermute x0 -> x8, waiting for transfers between devices: none -> 50.1 us  [the longest x3 42.6 us: ring_blocks(): up = lax.ppermute(up, axis, forward)]
    pallas_call x0 -> x1, Pallas kernels: none -> 40.5 us  [attend(): pl.pallas_call(attend_kernel, grid_spec=spec, out_shape=[jax.ShapeDtypeSt...]
    all_to_all x3 -> x0, local copies, waits for them, and re-layouts: 28.4 us -> none  [the longest x1 26.8 us: shards(): lax.all_to_all(latent_tiles[asked_tiles], 'ctx', split_axis=0, concat_axi...]
    all_gather x0 -> x2, blocking collectives: none -> 21.2 us  [the longest x1 12.5 us: shards(): all_index_weights = lax.all_gather(index_weights, 'y')]
    reduce_scatter x1 -> x0, waiting for transfers between devices: 20.5 us -> none  [shards(): lax.psum_scatter(index_portion, 'head', scatter_dimension=1, tiled=True)]
  transfers between devices with their start and end apart: 4 -> 15, of which waited for: 4 -> 9; matrix products, arithmetic and copies ran while one was open for 4% -> 9% of each run, Pallas kernels for 0% -> 0%
where the time goes in v1:
time: 326 us; the launch traced here: 324 us
  waiting for transfers between devices  152 us (47%)
  starting transfers between devices  41.1 us (13%)
  Pallas kernels  40.5 us (12%)
  local copies, waits for them, and re-layouts  32 us (10%)
  blocking collectives  32 us (10%)
  between operations  14.4 us (4%)
  other arithmetic  11.6 us (4%)
    all_to_all x1, waiting for transfers between devices, shards(): lax.all_to_all(partial, 'y', split_axis=0, concat_axis=0, tiled=True)  91.4 us
    ppermute x3, waiting for transfers between devices, ring_blocks(): up = lax.ppermute(up, axis, forward)  42.6 us
    pallas_call x1, Pallas kernels, attend(): pl.pallas_call(attend_kernel, grid_spec=spec, out_shape=[jax.ShapeDtypeSt...  40.5 us
    all_to_all x4, starting transfers between devices, shards(): lax.all_to_all(found, ('x', 'c'), split_axis=0, concat_axis=0, tiled=True)  19.6 us
    gather x8, local copies, waits for them, and re-layouts, shards(): found.append(blocks[d][asked])  13.1 us
    all_gather x1, blocking collectives, shards(): all_index_weights = lax.all_gather(index_weights, 'y')  12.5 us
    all_to_all x1, blocking collectives, shards(): small = lax.all_to_all(small, 'y', split_axis=0, concat_axis=0, tiled=True)  10.8 us
    unnamed x27, local copies, waits for them, and re-layouts  10.6 us
  transfers between devices with their start and end apart: 15, of which 9 were waited for; matrix products, arithmetic and copies ran while one was open for 9% of the time, Pallas kernels for 0%

profile of v1, /device:TPU:2, one launch (start us, length us, event | category | flops | bytes accessed | tf_op | source)
XLA Modules:
  0.0 323.5 jit_solution(1715038188791505226)
XLA Ops:
  7.2 0.7 all-gather.9.cloned.1.call-update
  8.0 0.7 all-gather.7.cloned.1.call-update
  8.7 3.1 copy.150
  12.0 0.2 pad_maximum_fusion.3
  12.1 2.0 collective-permute-start.1
  14.1 4.0 %collective-permute-start = (bf16[16,32,768]{2,1,0:T(8,128)(2,1)S(1)}, bf16[16,32,768]{2,1,0:T(8,128)(2,1)}, u32[]{:S(2)}, u32[]{:S(2)}) collective-permute-start(bf16[16,32,768]{2,1,0:T(8,128)(2,1)S(1)} %pad_maximum_fusion.3), channel_id=1, source_target_pairs={{0,224},{32,0},{64,32},{96,64},{128,96},{160,128},{192,160},{224,1... | collective-permute-start | bytes 2359304 | tf_op jit(solution)/shard_map/ppermute | solution.py:128
  18.2 8.7 %all_gather.27 = s32[8,64,2]{1,2,0:T(2,128)S(1)} all-gather(s32[1,64,2]{1,2,0:T(2,128)S(1)} %copy-done.10), channel_id=1, replica_groups=mesh['z'=8,'x'=4,'c'=2,'y'=4] {'x','c'}, dimensions={0}, use_global_device_ids=true | all-gather | bytes 4608 | tf_op jit(solution)/shard_map/all_gather | solution.py:163
  26.8 0.1 copy.177
  27.0 0.1 copy.157
  27.5 0.6 gather_fusion
  28.1 7.5 %collective-permute-done.1 = bf16[16,32,768]{2,1,0:T(8,128)(2,1)S(1)} collective-permute-done((bf16[16,32,768]{2,1,0:T(8,128)(2,1)S(1)}, bf16[16,32,768]{2,1,0:T(8,128)(2,1)S(1)}, u32[]{:S(2)}, u32[]{:S(2)}) %collective-permute-start.1) | collective-permute-done | bytes 786464 | tf_op jit(solution)/shard_map/ppermute | solution.py:127
  35.6 0.6 gather_fusion.2
  36.2 1.7 gather_fusion.1
  38.0 0.3 pad_maximum_fusion
  38.2 1.7 copy.158
  39.9 4.8 %all-to-all-start = ((bf16[8,192,768]{2,1,0:T(8,128)(2,1)}), bf16[8,192,768]{2,1,0:T(8,128)(2,1)S(1)}, u32[]{:S(2)}, u32[]{:S(2)}) async-start(bf16[8,192,768]{2,1,0:T(8,128)(2,1)} %bitcast.101), calls=%async_computation | async-start | bytes 4718592 | tf_op jit(solution)/shard_map/all_to_all | solution.py:177
  44.8 3.2 collective-permute-start.2
  48.3 17.3 %collective-permute-done.3 = bf16[16,32,768]{2,1,0:T(8,128)(2,1)} collective-permute-done((bf16[16,32,768]{2,1,0:T(8,128)(2,1)S(1)}, bf16[16,32,768]{2,1,0:T(8,128)(2,1)}, u32[]{:S(2)}, u32[]{:S(2)}) %collective-permute-start.3) | collective-permute-done | bytes 786464 | tf_op jit(solution)/shard_map/ppermute | solution.py:127
  65.7 1.7 gather_fusion.4
  67.4 2.6 gather_fusion.3
  70.0 1.3 pad_maximum_fusion.1
  71.3 1.3 copy.163
  72.6 0.7 all-to-all-done
  73.3 1.4 copy-done.5
  74.7 5.0 %all-to-all-start.1 = ((bf16[8,128,768]{2,1,0:T(8,128)(2,1)}), bf16[8,128,768]{2,1,0:T(8,128)(2,1)S(1)}, u32[]{:S(2)}, u32[]{:S(2)}) async-start(bf16[8,128,768]{2,1,0:T(8,128)(2,1)} %bitcast.103), calls=%async_computation.1 | async-start | bytes 3145728 | tf_op jit(solution)/shard_map/all_to_all | solution.py:177
  79.7 3.2 collective-permute-start.4
  82.9 17.8 %collective-permute-done.5 = bf16[16,32,768]{2,1,0:T(8,128)(2,1)S(1)} collective-permute-done((bf16[16,32,768]{2,1,0:T(8,128)(2,1)}, bf16[16,32,768]{2,1,0:T(8,128)(2,1)S(1)}, u32[]{:S(2)}, u32[]{:S(2)}) %collective-permute-start.5) | collective-permute-done | bytes 786464 | tf_op jit(solution)/shard_map/ppermute | solution.py:127
  100.7 0.9 copy-done.6
  101.6 0.1 collective-permute-start.6
  101.7 0.9 copy-done.7
  102.6 3.3 %collective-permute-start.7 = (bf16[8,32,768]{2,1,0:T(8,128)(2,1)S(1)}, bf16[8,32,768]{2,1,0:T(8,128)(2,1)S(1)}, u32[]{:S(2)}, u32[]{:S(2)}) collective-permute-start(bf16[8,32,768]{2,1,0:T(8,128)(2,1)S(1)} %slice.33), channel_id=1, source_target_pairs={{0,224},{32,0},{64,32},{96,64},{128,96},{160,128},{192,160},{224,1... | collective-permute-start | bytes 1179656 | tf_op jit(solution)/shard_map/ppermute | solution.py:132
  106.1 7.3 %collective-permute-done.6 = bf16[8,32,768]{2,1,0:T(8,128)(2,1)S(1)} collective-permute-done((bf16[8,32,768]{2,1,0:T(8,128)(2,1)S(1)}, bf16[8,32,768]{2,1,0:T(8,128)(2,1)S(1)}, u32[]{:S(2)}, u32[]{:S(2)}) %collective-permute-start.6) | collective-permute-done | bytes 393248 | tf_op jit(solution)/shard_map/ppermute | solution.py:132
  113.3 0.3 collective-permute-done.7
  113.7 1.5 gather_fusion.7
  115.2 4.8 %all-to-all-start.3 = ((bf16[8,64,768]{2,1,0:T(8,128)(2,1)}), bf16[8,64,768]{2,1,0:T(8,128)(2,1)S(1)}, u32[]{:S(2)}, u32[]{:S(2)}) async-start(bf16[8,64,768]{2,1,0:T(8,128)(2,1)} %bitcast.32), calls=%async_computation.3 | async-start | bytes 1572864 | tf_op jit(solution)/shard_map/all_to_all | solution.py:177
  120.4 1.7 gather_fusion.6
  122.1 2.6 gather_fusion.5
  124.7 1.3 pad_maximum_fusion.2
  126.0 1.3 copy.168
  127.3 4.4 %all-to-all-done.3 = bf16[8,64,768]{2,1,0:T(8,128)(2,1)S(1)} async-done(((bf16[8,64,768]{2,1,0:T(8,128)(2,1)}), bf16[8,64,768]{2,1,0:T(8,128)(2,1)S(1)}, u32[]{:S(2)}, u32[]{:S(2)}) %all-to-all-start.3) | async-done | bytes 786464 | tf_op jit(solution)/shard_map/all_to_all | solution.py:177
  131.7 0.9 copy-done.2
  132.6 5.0 %all-to-all-start.2 = ((bf16[8,128,768]{2,1,0:T(8,128)(2,1)}), bf16[8,128,768]{2,1,0:T(8,128)(2,1)S(1)}, u32[]{:S(2)}, u32[]{:S(2)}) async-start(bf16[8,128,768]{2,1,0:T(8,128)(2,1)} %bitcast.102), calls=%async_computation.2 | async-start | bytes 3145728 | tf_op jit(solution)/shard_map/all_to_all | solution.py:177
  137.6 0.1 copy.146
  137.7 0.1 copy.141
  137.8 0.1 reshape_squeeze.3
  138.0 1.3 select_reduce_fusion
  139.3 0.1 add_subtract_fusion
  139.5 0.7 sub.58
  140.2 1.1 copy.149
  141.3 12.5 %all-gather.3 = bf16[4,64,16]{1,2,0:T(8,128)(2,1)S(1)} all-gather(bf16[1,64,16]{1,2,0:T(8,128)(2,1)S(1)} %bitcast.117), channel_id=4, replica_groups=mesh['z'=8,'x'=4,'c'=2,'y'=4] {'y'}, dimensions={0}, use_global_device_ids=true | all-gather | bytes 10240 | tf_op jit(solution)/shard_map/all_gather | solution.py:160
  153.9 3.8 %all-to-all-done.2 = bf16[8,128,768]{2,1,0:T(8,128)(2,1)S(1)} async-done(((bf16[8,128,768]{2,1,0:T(8,128)(2,1)}), bf16[8,128,768]{2,1,0:T(8,128)(2,1)S(1)}, u32[]{:S(2)}, u32[]{:S(2)}) %all-to-all-start.2) | async-done | bytes 1572896 | tf_op jit(solution)/shard_map/all_to_all | solution.py:177
  157.7 1.1 copy-done.3
  158.9 1.2 copy-done.4
  160.1 40.5 %attend.1 = (bf16[4,64,32,512]{3,2,1,0:T(8,128)(2,1)}, f32[64,128]{1,0:T(8,128)S(1)}, f32[64,512]{1,0:T(8,128)S(1)}) custom-call(s32[64,16]{1,0:T(8,128)S(1)} %get-tuple-element.25.sel, bf16[4,64,32,576]{3,2,1,0:T(8,128)(2,1)} %bitcast.99, bf16[4,64,16,128]{3,2,1,0:T(8,128)(2,1)S(1)} %bitcast.97, f32[64,64]{1,0:T(8,128)S(1)} %bitcast.98, ...), custom_call_target="tpu_custom_call" | custom-call | tf_op jit(solution)/shard_map/attend/pallas_call | solution.py:108
  200.5 0.1 copy.171
  200.6 0.1 copy.173
  200.8 0.1 pad_maximum_fusion.5
  200.9 10.8 %all_to_all.30 = f32[4,64,160]{2,1,0:T(8,128)S(1)} all-to-all(f32[4,64,160]{2,1,0:T(8,128)S(1)} %pad_maximum_fusion.5), channel_id=1, replica_groups=mesh['z'=8,'x'=4,'c'=2,'y'=4] {'y'}, dimensions={0} | all-to-all | bytes 327680 | tf_op jit(solution)/shard_map/all_to_all | solution.py:210
  211.7 5.6 %all-to-all-start.4 = ((bf16[4,64,32,512]{3,2,1,0:T(8,128)(2,1)}), bf16[4,64,32,512]{3,2,1,0:T(8,128)(2,1)}, u32[]{:S(2)}, u32[]{:S(2)}) async-start(bf16[4,64,32,512]{3,2,1,0:T(8,128)(2,1)} %get-tuple-element.5), calls=%async_computation.4 | async-start | bytes 16777216 | tf_op jit(solution)/shard_map/all_to_all | solution.py:211
  217.4 0.1 slice.35
  217.5 0.1 copy.179
  217.6 0.8 copy.176
  218.5 91.4 %all-to-all-done.4 = bf16[4,64,32,512]{3,2,1,0:T(8,128)(2,1)} async-done(((bf16[4,64,32,512]{3,2,1,0:T(8,128)(2,1)}), bf16[4,64,32,512]{3,2,1,0:T(8,128)(2,1)}, u32[]{:S(2)}, u32[]{:S(2)}) %all-to-all-start.4) | async-done | bytes 8388640 | tf_op jit(solution)/shard_map/all_to_all | solution.py:211
  309.9 6.8 %multiply_reduce_fusion = bf16[64,32,512]{2,1,0:T(8,128)(2,1)} fusion(bf16[4,64,32,512]{3,2,1,0:T(8,128)(2,1)} %all-to-all-done.4, f32[4,64,32]{2,1,0:T(8,128)S(1)} %fusion), kind=kLoop, calls=%fused_computation.8 | loop fusion | flops 11534336 | bytes 10518528 | tf_op jit(solution)/shard_map/reduce_sum | solution.py:215
  (68 shorter events, 2.0 us)
Async XLA Ops:
  7.2 4.7 %copy-start = (bf16[2048,128]{1,0:T(8,128)(2,1)S(1)}, bf16[2048,128]{1,0:T(8,128)(2,1)}, u32[]{:S(2)}) copy-start(bf16[2048,128]{1,0:T(8,128)(2,1)} %param.11) | copy-start | bytes 1572868
  7.2 146.7 %all-gather.9.cloned.1.call-start = ((), (), s32[]{:S(2)}) async-start(), calls=%async_computation.7 | async-start | bytes 1310720 | tf_op jit(solution)/shard_map/all_gather | solution.py:159
  7.9 149.8 %all-gather.7.cloned.1.call-start = ((), (), s32[]{:S(2)}) async-start(), calls=%async_computation.6 | async-start | bytes 13107200 | tf_op jit(solution)/shard_map/all_gather | solution.py:158
  11.8 6.4 %copy-start.10 = (s32[1,64,2]{1,2,0:T(2,128)S(1)}, s32[1,64,2]{1,2,0:T(2,128)}, u32[]{:S(2)}) copy-start(s32[1,64,2]{1,2,0:T(2,128)} %param.12) | copy-start | bytes 1540
  12.1 23.5 %collective-permute-start.1 = (bf16[16,32,768]{2,1,0:T(8,128)(2,1)S(1)}, bf16[16,32,768]{2,1,0:T(8,128)(2,1)S(1)}, u32[]{:S(2)}, u32[]{:S(2)}) collective-permute-start(bf16[16,32,768]{2,1,0:T(8,128)(2,1)S(1)} %pad_maximum_fusion.3), channel_id=1, source_target_pairs={{0,32},{32,64},{64,96},{96,128},{128,160},{160,192},{192,224},{224... | collective-permute-start | bytes 2359304 | tf_op jit(solution)/shard_map/ppermute | solution.py:127
  14.1 22.1 %collective-permute-start = (bf16[16,32,768]{2,1,0:T(8,128)(2,1)S(1)}, bf16[16,32,768]{2,1,0:T(8,128)(2,1)}, u32[]{:S(2)}, u32[]{:S(2)}) collective-permute-start(bf16[16,32,768]{2,1,0:T(8,128)(2,1)S(1)} %pad_maximum_fusion.3), channel_id=1, source_target_pairs={{0,224},{32,0},{64,32},{96,64},{128,96},{160,128},{192,160},{224,1... | collective-permute-start | bytes 2359304 | tf_op jit(solution)/shard_map/ppermute | solution.py:128
  39.9 33.4 %all-to-all-start = ((bf16[8,192,768]{2,1,0:T(8,128)(2,1)}), bf16[8,192,768]{2,1,0:T(8,128)(2,1)S(1)}, u32[]{:S(2)}, u32[]{:S(2)}) async-start(bf16[8,192,768]{2,1,0:T(8,128)(2,1)} %bitcast.101), calls=%async_computation | async-start | bytes 4718592 | tf_op jit(solution)/shard_map/all_to_all | solution.py:177
  44.7 20.9 %collective-permute-start.3 = (bf16[16,32,768]{2,1,0:T(8,128)(2,1)S(1)}, bf16[16,32,768]{2,1,0:T(8,128)(2,1)}, u32[]{:S(2)}, u32[]{:S(2)}) collective-permute-start(bf16[16,32,768]{2,1,0:T(8,128)(2,1)S(1)} %collective-permute-done.1), channel_id=1, source_target_pairs={{0,32},{32,64},{64,96},{96,128},{128,160},{160,192},{192,224},{224... | collective-permute-start | bytes 2359304 | tf_op jit(solution)/shard_map/ppermute | solution.py:127
  44.8 22.6 %collective-permute-start.2 = (bf16[16,32,768]{2,1,0:T(8,128)(2,1)}, bf16[16,32,768]{2,1,0:T(8,128)(2,1)}, u32[]{:S(2)}, u32[]{:S(2)}) collective-permute-start(bf16[16,32,768]{2,1,0:T(8,128)(2,1)} %collective-permute-done), channel_id=1, source_target_pairs={{0,224},{32,0},{64,32},{96,64},{128,96},{160,128},{192,160},{224,1... | collective-permute-start | bytes 2359304 | tf_op jit(solution)/shard_map/ppermute | solution.py:128
  73.3 1.4 copy-start.5
  74.7 40.5 %all-to-all-start.1 = ((bf16[8,128,768]{2,1,0:T(8,128)(2,1)}), bf16[8,128,768]{2,1,0:T(8,128)(2,1)S(1)}, u32[]{:S(2)}, u32[]{:S(2)}) async-start(bf16[8,128,768]{2,1,0:T(8,128)(2,1)} %bitcast.103), calls=%async_computation.1 | async-start | bytes 3145728 | tf_op jit(solution)/shard_map/all_to_all | solution.py:177
  79.7 21.0 %collective-permute-start.5 = (bf16[16,32,768]{2,1,0:T(8,128)(2,1)}, bf16[16,32,768]{2,1,0:T(8,128)(2,1)S(1)}, u32[]{:S(2)}, u32[]{:S(2)}) collective-permute-start(bf16[16,32,768]{2,1,0:T(8,128)(2,1)} %collective-permute-done.3), channel_id=1, source_target_pairs={{0,32},{32,64},{64,96},{96,128},{128,160},{160,192},{192,224},{224... | collective-permute-start | bytes 2359304 | tf_op jit(solution)/shard_map/ppermute | solution.py:127
  79.7 22.0 %collective-permute-start.4 = (bf16[16,32,768]{2,1,0:T(8,128)(2,1)}, bf16[16,32,768]{2,1,0:T(8,128)(2,1)S(1)}, u32[]{:S(2)}, u32[]{:S(2)}) collective-permute-start(bf16[16,32,768]{2,1,0:T(8,128)(2,1)} %collective-permute-done.2), channel_id=1, source_target_pairs={{0,224},{32,0},{64,32},{96,64},{128,96},{160,128},{192,160},{224,1... | collective-permute-start | bytes 2359304 | tf_op jit(solution)/shard_map/ppermute | solution.py:128
  100.7 0.9 copy-start.6
  101.6 11.7 %collective-permute-start.6 = (bf16[8,32,768]{2,1,0:T(8,128)(2,1)S(1)}, bf16[8,32,768]{2,1,0:T(8,128)(2,1)S(1)}, u32[]{:S(2)}, u32[]{:S(2)}) collective-permute-start(bf16[8,32,768]{2,1,0:T(8,128)(2,1)S(1)} %slice.32), channel_id=1, source_target_pairs={{0,32},{32,64},{64,96},{96,128},{128,160},{160,192},{192,224},{224... | collective-permute-start | bytes 1179656 | tf_op jit(solution)/shard_map/ppermute | solution.py:132
  101.7 0.9 copy-start.7
  102.6 11.0 %collective-permute-start.7 = (bf16[8,32,768]{2,1,0:T(8,128)(2,1)S(1)}, bf16[8,32,768]{2,1,0:T(8,128)(2,1)S(1)}, u32[]{:S(2)}, u32[]{:S(2)}) collective-permute-start(bf16[8,32,768]{2,1,0:T(8,128)(2,1)S(1)} %slice.33), channel_id=1, source_target_pairs={{0,224},{32,0},{64,32},{96,64},{128,96},{160,128},{192,160},{224,1... | collective-permute-start | bytes 1179656 | tf_op jit(solution)/shard_map/ppermute | solution.py:132
  115.2 16.5 %all-to-all-start.3 = ((bf16[8,64,768]{2,1,0:T(8,128)(2,1)}), bf16[8,64,768]{2,1,0:T(8,128)(2,1)S(1)}, u32[]{:S(2)}, u32[]{:S(2)}) async-start(bf16[8,64,768]{2,1,0:T(8,128)(2,1)} %bitcast.32), calls=%async_computation.3 | async-start | bytes 1572864 | tf_op jit(solution)/shard_map/all_to_all | solution.py:177
  127.3 10.5 %copy-start.8 = (s32[64,16]{0,1:T(8,128)S(1)}, s32[64,16]{0,1:T(8,128)}, u32[]{:S(2)}) copy-start(s32[64,16]{0,1:T(8,128)} %param.13) | copy-start | bytes 12292
  127.3 14.0 %copy-start.9 = (bf16[64,16]{0,1:T(8,128)(2,1)S(1)}, bf16[64,16]{0,1:T(8,128)(2,1)}, u32[]{:S(2)}) copy-start(bf16[64,16]{0,1:T(8,128)(2,1)} %param.10) | copy-start | bytes 6148
  131.7 0.9 copy-start.2
  132.6 25.1 %all-to-all-start.2 = ((bf16[8,128,768]{2,1,0:T(8,128)(2,1)}), bf16[8,128,768]{2,1,0:T(8,128)(2,1)S(1)}, u32[]{:S(2)}, u32[]{:S(2)}) async-start(bf16[8,128,768]{2,1,0:T(8,128)(2,1)} %bitcast.102), calls=%async_computation.2 | async-start | bytes 3145728 | tf_op jit(solution)/shard_map/all_to_all | solution.py:177
  157.7 1.1 copy-start.3
  158.8 1.2 copy-start.4
  211.7 98.2 %all-to-all-start.4 = ((bf16[4,64,32,512]{3,2,1,0:T(8,128)(2,1)}), bf16[4,64,32,512]{3,2,1,0:T(8,128)(2,1)}, u32[]{:S(2)}, u32[]{:S(2)}) async-start(bf16[4,64,32,512]{3,2,1,0:T(8,128)(2,1)} %get-tuple-element.5), calls=%async_computation.4 | async-start | bytes 16777216 | tf_op jit(solution)/shard_map/all_to_all | solution.py:211
  309.9 6.8 %copy-start.1 = (bf16[2048,128]{1,0:T(8,128)(2,1)S(1)}, bf16[2048,128]{1,0:T(8,128)(2,1)}, u32[]{:S(2)}) copy-start(bf16[2048,128]{1,0:T(8,128)(2,1)} %param.11) | copy-start | bytes 1572868
Sparse Core Ops, SparseCore 0:
  9.8 29.4 all-gather.8
  41.2 103.7 all-gather.6

commit v2 on v1

v2 whole, which is shorter than its diff:
```python
import jax
import jax.numpy as jnp
from jax import lax
from jax.experimental import pallas as pl
from jax.experimental.pallas import tpu as pltpu
from jax.sharding import Mesh, PartitionSpec as P

KEY_VALUE_RANK = 512
LATENT = 576
ROTARY = LATENT - KEY_VALUE_RANK
LANES = 128
COLUMNS = KEY_VALUE_RANK // LANES
WIDE = KEY_VALUE_RANK + LANES
TILE = 128
CAP = 2
GROUP = 8
BATCH = 4
SCALE = 192.0 ** -0.5
LOG2_E = 1.4426950408889634
MASKED = -1e30


def lines_of(part):
    latent = COLUMNS * part
    return latent, latent + part // 2, latent + part // 2 + part


def attend_kernel(sel, lim, quarters, q_own, q_pair, *refs):
    own_fetched, pair_fetched = refs[: len(refs) // 2 - 3], refs[len(refs) // 2 - 3 : -6]
    out_own, out_pair, lse, rows, rotary, sems = refs[-6:]
    step = pl.program_id(0)
    slots, half, _ = rows.shape
    part = half // 2
    latent, packed, _ = lines_of(part)
    picks = sel.shape[1]
    heads = q_own.shape[1] + q_pair.shape[1]

    @pl.when(step == 0)
    def _():
        copies = []
        for side, fetched in enumerate((own_fetched, pair_fetched)):
            at = 0
            for ref in fetched:
                count = ref.shape[0]
                for j in range(COLUMNS):
                    copies.append(
                        pltpu.make_async_copy(
                            ref.at[:, pl.ds(j * part, part), :],
                            rows.at[pl.ds(at, count), pl.ds(side * part, part), pl.ds(j * LANES, LANES)],
                            sems.at[len(copies)],
                        )
                    )
                copies.append(
                    pltpu.make_async_copy(
                        ref.at[:, pl.ds(latent, packed - latent), :],
                        rotary.at[pl.ds(at, count), pl.ds(side * (part // 2), part // 2), :],
                        sems.at[len(copies)],
                    )
                )
                at += count
        for copy in copies:
            copy.start()
        for copy in copies:
            copy.wait()

        @pl.loop(0, slots)
        def _(slot):
            for side in range(2):
                pairs = rotary[slot, pl.ds(side * (part // 2), part // 2), :]
                turned = jnp.concatenate([pairs[:, ROTARY:], pairs[:, :ROTARY]], axis=1)
                rows[slot, pl.ds(side * part, part), pl.ds(KEY_VALUE_RANK, LANES)] = jnp.concatenate(
                    [pairs, turned], axis=0
                )

    row = lax.broadcasted_iota(jnp.int32, (half, heads), 0)
    place = jnp.where(row < part, row + quarters[0] * part, row - part + quarters[1] * part)
    per = 256 // half

    def keys(query, n, width):
        return jnp.concatenate([rows[sel[query, n * per + j], :, :width] for j in range(per)], axis=0)

    def scores_of(i):
        query = step * GROUP + i
        here = jnp.concatenate([q_own[i], q_pair[i]], axis=0)
        found = []
        for n in range(picks // per):
            block = lax.dot_general(
                keys(query, n, LATENT), here, (((1,), (1,)), ((), ())), preferred_element_type=jnp.float32
            )
            block = block * (SCALE * LOG2_E)
            found += [
                jnp.where(place <= lim[query, n * per + j], block[j * half : (j + 1) * half], MASKED)
                for j in range(per)
            ]
        return jnp.concatenate(found, axis=0)

    for first in range(0, GROUP, BATCH):
        batch = range(first, first + BATCH)
        scores = [scores_of(i) for i in batch]
        probs = []
        for i, s in zip(batch, scores):
            peak = jnp.max(s, axis=0, keepdims=True)
            p = jnp.exp2(s - peak)
            total = jnp.sum(p, axis=0, keepdims=True)
            probs.append((p * (1.0 / total)).astype(jnp.bfloat16))
            lse[pl.ds(i, 1), pl.ds(0, heads)] = peak + jnp.log2(total)
        for i, p in zip(batch, probs):
            summed = 0.0
            for n in range(picks // per):
                summed = summed + lax.dot_general(
                    p[n * 256 : (n + 1) * 256],
                    keys(step * GROUP + i, n, KEY_VALUE_RANK),
                    (((0,), (0,)), ((), ())),
                    preferred_element_type=jnp.float32,
                )
            summed = summed.astype(jnp.bfloat16)
            out_own[i] = summed[: heads // 2]
            out_pair[i] = summed[heads // 2 :]


def attend(sel, lim, quarters, q_own, q_pair, own_fetched, pair_fetched, first, count):
    _, heads, width = q_own.shape
    slots = sum(f.shape[0] for f in own_fetched)
    part = 2 * pair_fetched[0].shape[1] // (2 * COLUMNS + 1)
    at = first // GROUP
    spec = pltpu.PrefetchScalarGridSpec(
        num_scalar_prefetch=3,
        grid=(count // GROUP,),
        in_specs=[pl.BlockSpec((GROUP, heads, width), lambda i, *_: (at + i, 0, 0))] * 2
        + [pl.BlockSpec(memory_space=pl.ANY)] * (2 * len(own_fetched)),
        out_specs=[pl.BlockSpec((GROUP, heads, KEY_VALUE_RANK), lambda i, *_: (i, 0, 0))] * 2
        + [pl.BlockSpec((GROUP, LANES), lambda i, *_: (i, 0))],
        scratch_shapes=[
            pltpu.VMEM((slots, 2 * part, WIDE), jnp.bfloat16),
            pltpu.VMEM((slots, part, LANES), jnp.bfloat16),
            pltpu.SemaphoreType.DMA((2 * len(own_fetched) * (COLUMNS + 1),)),
        ],
    )
    return pl.pallas_call(
        attend_kernel,
        grid_spec=spec,
        out_shape=[jax.ShapeDtypeStruct((count, heads, KEY_VALUE_RANK), jnp.bfloat16)] * 2
        + [jax.ShapeDtypeStruct((count, LANES), jnp.float32)],
        compiler_params=pltpu.CompilerParams(vmem_limit_bytes=40 * 1024 * 1024),
        name="attend",
    )(sel[first : first + count], lim[first : first + count], quarters, q_own, q_pair, *own_fetched, *pair_fetched)


def index_kernel(sel, iq, weight_t, lim, *refs):
    fetched, (index_out, keys, sems) = refs[:-3], refs[-3:]
    step = pl.program_id(0)
    part = keys.shape[1]
    _, packed, lines = lines_of(part)
    picks = sel.shape[1]
    heads = iq.shape[0] * iq.shape[2]

    @pl.when(step == 0)
    def _():
        copies, at = [], 0
        for i, ref in enumerate(fetched):
            count = ref.shape[0]
            copies.append(
                pltpu.make_async_copy(
                    ref.at[:, pl.ds(packed, lines - packed), :], keys.at[pl.ds(at, count)], sems.at[i]
                )
            )
            at += count
        for copy in copies:
            copy.start()
        for copy in copies:
            copy.wait()

    weight_lane = lax.broadcasted_iota(jnp.int32, weight_t.shape, 1)
    for i in range(GROUP):
        query = step * GROUP + i
        picked = jnp.concatenate([keys[sel[query, k]] for k in range(picks)], axis=0)
        dots = lax.dot_general(
            iq[:, i].reshape(heads, iq.shape[3]),
            picked,
            (((1,), (1,)), ((), ())),
            preferred_element_type=jnp.float32,
        )
        weight = jnp.sum(jnp.where(weight_lane == query, weight_t[...], 0.0), axis=1, keepdims=True)
        index_row = jnp.sum(jnp.maximum(dots, 0.0) * weight, axis=0, keepdims=True)
        index_out[pl.ds(i, 1), :] = jnp.where(lim[pl.ds(i, 1), :] >= 0, index_row, 0.0)


def index(sel, iq, weight_t, lim, fetched):
    queries, picks = sel.shape
    part = lim.shape[1] // picks
    slots = sum(f.shape[0] for f in fetched)
    spec = pltpu.PrefetchScalarGridSpec(
        num_scalar_prefetch=1,
        grid=(queries // GROUP,),
        in_specs=[
            pl.BlockSpec((iq.shape[0], GROUP) + iq.shape[2:], lambda i, s: (0, i, 0, 0)),
            pl.BlockSpec(weight_t.shape, lambda i, s: (0, 0)),
            pl.BlockSpec((GROUP, lim.shape[1]), lambda i, s: (i, 0)),
        ]
        + [pl.BlockSpec(memory_space=pl.ANY)] * len(fetched),
        out_specs=pl.BlockSpec((GROUP, lim.shape[1]), lambda i, s: (i, 0)),
        scratch_shapes=[
            pltpu.VMEM((slots, part, LANES), jnp.bfloat16),
            pltpu.SemaphoreType.DMA((len(fetched),)),
        ],
    )
    return pl.pallas_call(
        index_kernel,
        grid_spec=spec,
        out_shape=jax.ShapeDtypeStruct(lim.shape, jnp.float32),
        compiler_params=pltpu.CompilerParams(vmem_limit_bytes=16 * 1024 * 1024),
        name="index",
    )(sel, iq, weight_t, lim, *fetched)


def ring_blocks(block, axis, size):
    forward = [(i, (i + 1) % size) for i in range(size)]
    backward = [(i, (i - 1) % size) for i in range(size)]
    up = down = block
    got = {0: block}
    for d in range(1, size // 2):
        up = lax.ppermute(up, axis, forward)
        down = lax.ppermute(down, axis, backward)
        got[size - d], got[d] = up, down
    half = block.shape[0] // 2
    got[size // 2] = jnp.concatenate(
        [lax.ppermute(up[:half], axis, forward), lax.ppermute(down[half:], axis, backward)]
    )
    return got


def rounds_of(size):
    rounds = [[0, 1, size - 1]]
    rounds += [[d, size - d] for d in range(2, size // 2)]
    return rounds + [[size // 2]]


def pairings():
    near, far = (lambda y: y ^ 1), (lambda y: 3 - y)
    rows = [(4 * c + y, 4 * c + (near, far)[c](y)) for c in range(2) for y in range(4)]
    heads = [(4 * c + y, 4 * c + (far, near)[c](y)) for c in range(2) for y in range(4)]
    return rows, heads


def shards(queries, latent, index_queries, index_weights, index_keys, request_tiles, selection):
    z_count, x_count, c_count, y_count = (lax.axis_size(a) for a in ("z", "x", "c", "y"))
    z, x, c, y = (lax.axis_index(a) for a in ("z", "x", "c", "y"))
    plane = x_count * c_count
    here = x * c_count + c
    query_count, local_heads, _ = queries.shape
    index_heads = index_queries.shape[1]
    tile_count = latent.shape[0] // TILE
    part = TILE // y_count
    picks = selection.shape[1]
    _, packed, lines = lines_of(part)
    row_pairs, head_pairs = pairings()

    def quarter(a):
        return lax.dynamic_index_in_dim(a.reshape(tile_count, y_count, part, a.shape[1]), y, 1, False)

    own_rows, own_keys = quarter(latent), quarter(index_keys)
    rotary = own_rows[:, :, KEY_VALUE_RANK:]
    own = jnp.concatenate(
        [own_rows[:, :, j * LANES : (j + 1) * LANES] for j in range(COLUMNS)]
        + [jnp.concatenate([rotary[:, : part // 2], rotary[:, part // 2 :]], axis=2), own_keys],
        axis=1,
    )

    q_pair = lax.ppermute(queries, ("c", "y"), head_pairs)
    weight_rows = jnp.pad(index_weights, ((0, 0), (0, LANES - index_heads)))
    joined = jnp.concatenate([index_queries, weight_rows.reshape(-1, index_heads, LANES)], axis=0)
    joined = lax.all_gather(joined, "y")
    weights = joined[:, query_count:].reshape(y_count, query_count, LANES)[:, :, :index_heads]
    key_scale = index_keys.shape[1] ** -0.5
    weight_t = jnp.transpose(weights.astype(jnp.float32), (0, 2, 1)).reshape(-1, query_count) * key_scale

    wanted = request_tiles[0]
    plans = lax.all_gather(wanted, ("x", "c")).reshape(plane, z_count, plane, CAP)
    plans = lax.dynamic_index_in_dim(plans, here, 2, False)

    blocks = ring_blocks(own, "z", z_count)
    own_fetched, pair_fetched = [], []
    place = {}
    base = 0
    for distances in rounds_of(z_count):
        found = []
        for p, d in enumerate(distances):
            asked = lax.dynamic_index_in_dim(plans, (z + d) % z_count, 1, False)
            found.append(blocks[d][asked])
            place[d] = (base + p * CAP, len(distances) * CAP)
        found = jnp.concatenate(found, axis=1).reshape(plane, -1, LANES)
        moved = lax.all_to_all(found, ("x", "c"), split_axis=0, concat_axis=0, tiled=True)
        moved = moved.reshape(-1, lines, LANES)
        own_fetched.append(moved)
        pair_fetched.append(lax.ppermute(moved[:, :packed], ("c", "y"), row_pairs))
        base += plane * len(distances) * CAP

    owner = selection // CAP
    distance = (owner // plane - z) % z_count
    first = sum(jnp.where(distance == d, place[d][0], 0) for d in place)
    stride = sum(jnp.where(distance == d, place[d][1], 0) for d in place)
    rows_at = first + (owner % plane) * stride + selection % CAP

    flat_wanted = wanted.reshape(-1)
    matches = selection[:, :, None] == jnp.arange(flat_wanted.shape[0], dtype=jnp.int32)
    local_tile = jnp.sum(jnp.where(matches, flat_wanted, 0), axis=2)
    tile_start = (owner * tile_count + local_tile) * TILE
    ctx_count = z_count * plane
    context = ctx_count * tile_count * TILE
    query_pos = (
        context
        - ctx_count * query_count
        + (z * plane + here) * query_count
        + jnp.arange(query_count, dtype=jnp.int32)
    )
    lim = query_pos[:, None] - tile_start
    own_lim = (lim - y * part)[:, :, None] - jnp.arange(part, dtype=jnp.int32)
    own_lim = own_lim.reshape(query_count, picks * part)
    partner = jnp.where(c == 0, y ^ 1, 3 - y)

    index_part = index(rows_at, joined, weight_t, own_lim, own_fetched)
    index_part = lax.all_gather(index_part, "y").reshape(y_count, query_count, y_count, -1, part)
    index_part = lax.dynamic_index_in_dim(index_part, y, 2, False)
    index_scores = jnp.transpose(index_part, (1, 2, 0, 3)).reshape(query_count, -1)

    quarters = jnp.stack([y, partner])
    attended = []
    split = query_count * 3 // 4
    for first_query, count in ((0, split), (split, query_count - split)):
        mine, other, lse = attend(
            rows_at, lim, quarters, queries, q_pair, own_fetched, pair_fetched, first_query, count
        )
        other = lax.ppermute(other, ("c", "y"), head_pairs)
        other_lse = lax.ppermute(lse[:, local_heads : 2 * local_heads], ("c", "y"), head_pairs)
        share = 1.0 / (1.0 + jnp.exp2(other_lse - lse[:, :local_heads]))[..., None]
        other_share = 1.0 / (1.0 + jnp.exp2(lse[:, :local_heads] - other_lse))[..., None]
        merged = mine.astype(jnp.float32) * share + other.astype(jnp.float32) * other_share
        attended.append(merged.astype(jnp.bfloat16))
    return jnp.concatenate(attended, axis=0), index_scores


def solution(mesh):
    ctx, head = mesh.devices.shape
    x_count, c_count = 4, 2
    grid = Mesh(
        mesh.devices.reshape(ctx // (x_count * c_count), x_count, c_count, head), ("z", "x", "c", "y")
    )
    ctx_axes = ("z", "x", "c")
    return jax.shard_map(
        shards,
        mesh=grid,
        in_specs=(
            P(ctx_axes, "y", None),
            P(ctx_axes, None),
            P(ctx_axes, "y", None),
            P(ctx_axes, "y"),
            P(ctx_axes, None),
            P(ctx_axes, None, None),
            P(ctx_axes, None),
        ),
        out_specs=(P(ctx_axes, "y", None), P(ctx_axes, "y")),
        check_vma=False,
    )
```

time: 326 us -> 331 us (1.015)
  waiting for transfers between devices: 152 us -> 103 us
  Pallas kernels: 40.5 us -> 72.3 us
  local copies, waits for them, and re-layouts: 32 us -> 50.9 us
  blocking collectives: 32 us -> 22.5 us
  other arithmetic: 11.6 us -> 18.4 us
  starting transfers between devices: 41.1 us -> 47.7 us
    all_to_all x1 -> x0, waiting for transfers between devices: 91.4 us -> none  [shards(): lax.all_to_all(partial, 'y', split_axis=0, concat_axis=0, tiled=True)]
    ppermute x0 -> x9, waiting for transfers between devices: none -> 51.2 us  [the longest x1 24.2 us: shards(): q_pair = lax.ppermute(queries, ('c', 'y'), head_pairs)]
    pallas_call x1 -> x2, Pallas kernels: 40.5 us -> 65.7 us  [attend(): pl.pallas_call(attend_kernel, grid_spec=spec, out_shape=[jax.ShapeDtypeSt...]
    ppermute x0 -> x9, starting transfers between devices: none -> 12.9 us  [the longest x2 3.79 us: shards(): other = lax.ppermute(other, ('c', 'y'), head_pairs)]
    all_to_all x1 -> x0, blocking collectives: 10.8 us -> none  [shards(): small = lax.all_to_all(small, 'y', split_axis=0, concat_axis=0, tiled=True)]
    slice x1 -> x12, local copies, waits for them, and re-layouts: 0.09 us -> 9.9 us  [the longest x4 6.96 us: shards(): pair_fetched.append(lax.ppermute(moved[:, :packed], ('c', 'y'), row_pairs))]
    concatenate x2 -> x5, other arithmetic: 0.29 us -> 8.56 us  [the longest x3 6.32 us: shards(): found = jnp.concatenate(found, axis=1).reshape(plane, -1, LANES)]
    reduce_sum x2 -> x0, other arithmetic: 6.81 us -> none  [the longest x1 6.78 us: shards(): jnp.sum(partial.astype(jnp.float32) * share[..., None], axis=0)]
  transfers between devices with their start and end apart: 15 -> 22, of which waited for: 9 -> 11; matrix products, arithmetic and copies ran while one was open for 9% -> 15% of each run, Pallas kernels for 0% -> 22%
where the time goes in v2:
time: 331 us; the launch traced here: 330 us
  waiting for transfers between devices  103 us (31%)
  Pallas kernels  72.3 us (22%)
  local copies, waits for them, and re-layouts  50.9 us (15%)
  starting transfers between devices  47.7 us (14%)
  blocking collectives  22.5 us (7%)
  other arithmetic  18.4 us (6%)
  between operations  14.5 us (4%)
    pallas_call x2, Pallas kernels, attend(): pl.pallas_call(attend_kernel, grid_spec=spec, out_shape=[jax.ShapeDtypeSt...  65.7 us
    ppermute x3, waiting for transfers between devices, ring_blocks(): up = lax.ppermute(up, axis, forward)  38 us
    ppermute x1, waiting for transfers between devices, shards(): q_pair = lax.ppermute(queries, ('c', 'y'), head_pairs)  24.2 us
    ppermute x4, waiting for transfers between devices, shards(): pair_fetched.append(lax.ppermute(moved[:, :packed], ('c', 'y'), row_pairs))  22 us
    all_to_all x4, starting transfers between devices, shards(): lax.all_to_all(found, ('x', 'c'), split_axis=0, concat_axis=0, tiled=True)  20.1 us
    all_gather x1, blocking collectives, shards(): lax.all_gather(index_part, 'y')  13.8 us
    unnamed x40, local copies, waits for them, and re-layouts  13.6 us
    gather x8, local copies, waits for them, and re-layouts, shards(): found.append(blocks[d][asked])  13.5 us
  transfers between devices with their start and end apart: 22, of which 11 were waited for; matrix products, arithmetic and copies ran while one was open for 15% of the time, Pallas kernels for 22%

profile of v2, /device:TPU:2, one launch (start us, length us, event | category | flops | bytes accessed | tf_op | source)
XLA Modules:
  0.0 329.6 jit_solution(5092763789561931306)
XLA Ops:
  7.2 3.1 copy.103
  10.7 0.9 bitcast_dynamic-update-slice_fusion
  11.6 2.0 collective-permute-start.2
  13.6 4.0 %collective-permute-start.1 = (bf16[16,176,128]{2,1,0:T(8,128)(2,1)S(1)}, bf16[16,176,128]{2,1,0:T(8,128)(2,1)}, u32[]{:S(2)}, u32[]{:S(2)}) collective-permute-start(bf16[16,176,128]{2,1,0:T(8,128)(2,1)S(1)} %bitcast_dynamic-update-slice_fusion), channel_id=1, source_target_pairs={{0,224},{32,0},{64,32},{96,64},{128,96},{160,128},{192,160},{224,1... | collective-permute-start | bytes 2162696 | tf_op jit(solution)/shard_map/ppermute | solution.py:223
  17.6 8.7 %all_gather.15 = s32[8,64,2]{1,2,0:T(2,128)S(1)} all-gather(s32[1,64,2]{1,2,0:T(2,128)S(1)} %copy-done.14), channel_id=1, replica_groups=mesh['z'=8,'x'=4,'c'=2,'y'=4] {'x','c'}, dimensions={0}, use_global_device_ids=true | all-gather | bytes 4608 | tf_op jit(solution)/shard_map/all_gather | solution.py:278
  27.7 5.9 %collective-permute-done.2 = bf16[16,176,128]{2,1,0:T(8,128)(2,1)S(1)} collective-permute-done((bf16[16,176,128]{2,1,0:T(8,128)(2,1)S(1)}, bf16[16,176,128]{2,1,0:T(8,128)(2,1)S(1)}, u32[]{:S(2)}, u32[]{:S(2)}) %collective-permute-start.2) | collective-permute-done | bytes 720928 | tf_op jit(solution)/shard_map/ppermute | solution.py:222
  34.4 1.8 gather_fusion.1
  36.2 1.6 pad_maximum_fusion
  37.8 4.8 %all-to-all-start = ((bf16[8,1056,128]{2,1,0:T(8,128)(2,1)}), bf16[8,1056,128]{2,1,0:T(8,128)(2,1)S(1)}, u32[]{:S(2)}, u32[]{:S(2)}) async-start(bf16[8,1056,128]{2,1,0:T(8,128)(2,1)} %bitcast.100), calls=%async_computation | async-start | bytes 4325376 | tf_op jit(solution)/shard_map/all_to_all | solution.py:292
  42.6 3.2 collective-permute-start.3
  46.2 15.9 %collective-permute-done.4 = bf16[16,176,128]{2,1,0:T(8,128)(2,1)} collective-permute-done((bf16[16,176,128]{2,1,0:T(8,128)(2,1)S(1)}, bf16[16,176,128]{2,1,0:T(8,128)(2,1)}, u32[]{:S(2)}, u32[]{:S(2)}) %collective-permute-start.4) | collective-permute-done | bytes 720928 | tf_op jit(solution)/shard_map/ppermute | solution.py:222
  62.1 1.8 gather_fusion.4
  63.9 2.6 gather_fusion.3
  66.5 2.3 pad_maximum_fusion.2
  69.0 5.7 %all-to-all-start.1 = ((bf16[8,704,128]{2,1,0:T(8,128)(2,1)}), bf16[8,704,128]{2,1,0:T(8,128)(2,1)}, u32[]{:S(2)}, u32[]{:S(2)}) async-start(bf16[8,704,128]{2,1,0:T(8,128)(2,1)} %bitcast.102), calls=%async_computation.1 | async-start | bytes 2883584 | tf_op jit(solution)/shard_map/all_to_all | solution.py:292
  74.7 3.2 collective-permute-start.5
  78.3 16.1 %collective-permute-done.6 = bf16[16,176,128]{2,1,0:T(8,128)(2,1)} collective-permute-done((bf16[16,176,128]{2,1,0:T(8,128)(2,1)}, bf16[16,176,128]{2,1,0:T(8,128)(2,1)}, u32[]{:S(2)}, u32[]{:S(2)}) %collective-permute-start.6) | collective-permute-done | bytes 720928 | tf_op jit(solution)/shard_map/ppermute | solution.py:222
  94.4 1.8 gather_fusion.6
  96.2 2.6 gather_fusion.5
  98.8 2.4 pad_maximum_fusion.3
  101.2 4.8 %all-to-all-start.2 = ((bf16[8,704,128]{2,1,0:T(8,128)(2,1)}), bf16[8,704,128]{2,1,0:T(8,128)(2,1)}, u32[]{:S(2)}, u32[]{:S(2)}) async-start(bf16[8,704,128]{2,1,0:T(8,128)(2,1)} %bitcast.101), calls=%async_computation.2 | async-start | bytes 2883584 | tf_op jit(solution)/shard_map/all_to_all | solution.py:292
  106.1 3.0 collective-permute-start
  109.1 1.3 slice.119
  110.5 1.0 slice.118
  111.6 1.3 collective-permute-start.8
  112.9 1.0 slice.117
  113.9 0.9 collective-permute-start.7
  115.8 6.3 %collective-permute-done.8 = bf16[8,176,128]{2,1,0:T(8,128)(2,1)S(1)} collective-permute-done((bf16[8,176,128]{2,1,0:T(8,128)(2,1)S(1)}, bf16[8,176,128]{2,1,0:T(8,128)(2,1)S(1)}, u32[]{:S(2)}, u32[]{:S(2)}) %collective-permute-start.8) | collective-permute-done | bytes 360480 | tf_op jit(solution)/shard_map/ppermute | solution.py:227
  122.1 3.4 %collective-permute-done.7 = bf16[8,176,128]{2,1,0:T(8,128)(2,1)} collective-permute-done((bf16[8,176,128]{2,1,0:T(8,128)(2,1)S(1)}, bf16[8,176,128]{2,1,0:T(8,128)(2,1)}, u32[]{:S(2)}, u32[]{:S(2)}) %collective-permute-start.7) | collective-permute-done | bytes 360480 | tf_op jit(solution)/shard_map/ppermute | solution.py:227
  125.5 1.1 pad_maximum_fusion.4
  126.6 1.5 gather_fusion.7
  128.1 4.8 %all-to-all-start.3 = ((bf16[8,352,128]{2,1,0:T(8,128)(2,1)}), bf16[8,352,128]{2,1,0:T(8,128)(2,1)S(1)}, u32[]{:S(2)}, u32[]{:S(2)}) async-start(bf16[8,352,128]{2,1,0:T(8,128)(2,1)} %bitcast.104), calls=%async_computation.3 | async-start | bytes 1441792 | tf_op jit(solution)/shard_map/all_to_all | solution.py:292
  132.9 2.4 slice.120
  135.9 2.4 slice.121
  138.3 1.4 collective-permute-start.11
  139.7 4.2 %all-to-all-done.3 = bf16[8,352,128]{2,1,0:T(8,128)(2,1)S(1)} async-done(((bf16[8,352,128]{2,1,0:T(8,128)(2,1)}), bf16[8,352,128]{2,1,0:T(8,128)(2,1)S(1)}, u32[]{:S(2)}, u32[]{:S(2)}) %all-to-all-start.3) | async-done | bytes 720928 | tf_op jit(solution)/shard_map/all_to_all | solution.py:292
  143.9 0.9 slice.122
  146.3 1.3 select_reduce_fusion
  147.7 1.5 broadcast_subtract_fusion.1
  150.4 24.2 %collective-permute-done.q_pair = bf16[64,32,576]{2,1,0:T(8,128)(2,1)} collective-permute-done((bf16[64,32,576]{2,1,0:T(8,128)(2,1)}, bf16[64,32,576]{2,1,0:T(8,128)(2,1)}, u32[]{:S(2)}, u32[]{:S(2)}) %collective-permute-start) | collective-permute-done | bytes 2359328 | tf_op jit(solution)/shard_map/ppermute | solution.py:269
  174.6 22.0 %collective-permute-done.12.refs_7_ = bf16[16,144,128]{2,1,0:T(8,128)(2,1)S(1)} collective-permute-done((bf16[16,144,128]{2,1,0:T(8,128)(2,1)}, bf16[16,144,128]{2,1,0:T(8,128)(2,1)S(1)}, u32[]{:S(2)}, u32[]{:S(2)}) %collective-permute-start.12) | collective-permute-done | bytes 589856 | tf_op jit(solution)/shard_map/ppermute | solution.py:295
  197.4 41.8 %attend.2 = (bf16[48,32,512]{2,1,0:T(8,128)(2,1)S(1)}, bf16[48,32,512]{2,1,0:T(8,128)(2,1)}, f32[48,128]{1,0:T(8,128)S(1)}) custom-call(s32[48,16]{1,0:T(8,128)S(1)} %slice.109.sel, s32[48,16]{1,0:T(8,128)S(1)} %copy-done.6, s32[2]{0:T(128)S(1)} %pad_add_fusion.quarters, bf16[64,32,576]{2,1,0:T(8,128)(2,1)} %q_own.3, ...), custom_call_target="tpu_custom_call" | custom-call | tf_op jit(solution)/shard_map/attend/pallas_call | solution.py:139
  239.2 1.1 copy-done.1
  240.3 3.0 collective-permute-start.14
  244.0 0.8 copy.123
  245.6 1.7 copy.124
  247.9 1.6 broadcast_subtract_fusion.lim
  249.5 1.5 slice.125
  250.9 1.5 copy.132
  253.2 1.2 copy-done.3
  254.4 0.9 copy-done.4
  255.3 6.7 %index.1 = f32[64,512]{1,0:T(8,128)S(1)} custom-call(s32[64,16]{1,0:T(8,128)S(1)} %get-tuple-element.34.sel, bf16[4,68,16,128]{3,2,1,0:T(8,128)(2,1)S(1)} %bitcast.98, f32[64,64]{1,0:T(8,128)S(1)} %bitcast.99, s32[64,512]{1,0:T(8,128)S(1)} %copy-done.4, bf16[48,176,128]{2,1,0:T(8,128)(2,1)S(1)} %bitcast.91, bf16[32,176,128]{2,1,0:T(8,128)(2,1)} %bitcast.20.refs_1_, ...), custom_call_target="tpu_custom_call" | custom-call | tf_op jit(solution)/shard_map/index/pallas_call | solution.py:207
  262.0 13.8 %all-gather.1 = f32[256,512]{1,0:T(8,128)} all-gather(f32[64,512]{1,0:T(8,128)S(1)} %index.1), channel_id=3, replica_groups=mesh['z'=8,'x'=4,'c'=2,'y'=4] {'y'}, dimensions={0}, use_global_device_ids=true | all-gather | bytes 655360 | tf_op jit(solution)/shard_map/all_gather | solution.py:322
  275.8 2.0 copy.125
  277.9 2.5 reshape.322
  280.4 1.7 copy-done
  282.1 23.9 %attend.3 = (bf16[16,32,512]{2,1,0:T(8,128)(2,1)S(1)}, bf16[16,32,512]{2,1,0:T(8,128)(2,1)}, f32[16,128]{1,0:T(8,128)S(1)}) custom-call(s32[16,16]{1,0:T(8,128)S(1)} %slice.123.sel, s32[16,16]{1,0:T(8,128)S(1)} %slice.124.lim, s32[2]{0:T(128)S(1)} %copy-done.8, bf16[64,32,576]{2,1,0:T(8,128)(2,1)S(1)} %copy-done, ...), custom_call_target="tpu_custom_call" | custom-call | tf_op jit(solution)/shard_map/attend/pallas_call | solution.py:139
  307.7 2.5 collective-permute-start.15
  310.2 1.0 constant_dynamic-slice_fusion
  312.0 0.8 collective-permute-start.13
  312.8 4.7 %collective-permute-done.15 = f32[16,32]{1,0:T(8,128)S(1)} collective-permute-done((f32[16,32]{1,0:T(8,128)S(1)}, f32[16,32]{1,0:T(8,128)S(1)}, u32[]{:S(2)}, u32[]{:S(2)}) %collective-permute-start.15) | collective-permute-done | bytes 2080 | tf_op jit(solution)/shard_map/ppermute | solution.py:334
  317.8 1.3 add_convert_fusion.1
  319.2 2.1 add_convert_fusion
  321.3 1.5 pad_maximum_fusion.1
  (104 shorter events, 14.3 us)
Async XLA Ops:
  10.3 7.4 %copy-start.14 = (s32[1,64,2]{1,2,0:T(2,128)S(1)}, s32[1,64,2]{1,2,0:T(2,128)}, u32[]{:S(2)}) copy-start(s32[1,64,2]{1,2,0:T(2,128)} %param.12) | copy-start | bytes 1540
  11.6 22.1 %collective-permute-start.2 = (bf16[16,176,128]{2,1,0:T(8,128)(2,1)S(1)}, bf16[16,176,128]{2,1,0:T(8,128)(2,1)S(1)}, u32[]{:S(2)}, u32[]{:S(2)}) collective-permute-start(bf16[16,176,128]{2,1,0:T(8,128)(2,1)S(1)} %bitcast_dynamic-update-slice_fusion), channel_id=1, source_target_pairs={{0,32},{32,64},{64,96},{96,128},{128,160},{160,192},{192,224},{224... | collective-permute-start | bytes 2162696 | tf_op jit(solution)/shard_map/ppermute | solution.py:222
  13.6 20.8 %collective-permute-start.1 = (bf16[16,176,128]{2,1,0:T(8,128)(2,1)S(1)}, bf16[16,176,128]{2,1,0:T(8,128)(2,1)}, u32[]{:S(2)}, u32[]{:S(2)}) collective-permute-start(bf16[16,176,128]{2,1,0:T(8,128)(2,1)S(1)} %bitcast_dynamic-update-slice_fusion), channel_id=1, source_target_pairs={{0,224},{32,0},{64,32},{96,64},{128,96},{160,128},{192,160},{224,1... | collective-permute-start | bytes 2162696 | tf_op jit(solution)/shard_map/ppermute | solution.py:223
  37.8 31.3 %all-to-all-start = ((bf16[8,1056,128]{2,1,0:T(8,128)(2,1)}), bf16[8,1056,128]{2,1,0:T(8,128)(2,1)S(1)}, u32[]{:S(2)}, u32[]{:S(2)}) async-start(bf16[8,1056,128]{2,1,0:T(8,128)(2,1)} %bitcast.100), calls=%async_computation | async-start | bytes 4325376 | tf_op jit(solution)/shard_map/all_to_all | solution.py:292
  42.6 19.5 %collective-permute-start.4 = (bf16[16,176,128]{2,1,0:T(8,128)(2,1)S(1)}, bf16[16,176,128]{2,1,0:T(8,128)(2,1)}, u32[]{:S(2)}, u32[]{:S(2)}) collective-permute-start(bf16[16,176,128]{2,1,0:T(8,128)(2,1)S(1)} %collective-permute-done.2), channel_id=1, source_target_pairs={{0,32},{32,64},{64,96},{96,128},{128,160},{160,192},{192,224},{224... | collective-permute-start | bytes 2162696 | tf_op jit(solution)/shard_map/ppermute | solution.py:222
  42.6 21.3 %collective-permute-start.3 = (bf16[16,176,128]{2,1,0:T(8,128)(2,1)}, bf16[16,176,128]{2,1,0:T(8,128)(2,1)}, u32[]{:S(2)}, u32[]{:S(2)}) collective-permute-start(bf16[16,176,128]{2,1,0:T(8,128)(2,1)} %collective-permute-done.1), channel_id=1, source_target_pairs={{0,224},{32,0},{64,32},{96,64},{128,96},{160,128},{192,160},{224,1... | collective-permute-start | bytes 2162696 | tf_op jit(solution)/shard_map/ppermute | solution.py:223
  69.0 32.2 %all-to-all-start.1 = ((bf16[8,704,128]{2,1,0:T(8,128)(2,1)}), bf16[8,704,128]{2,1,0:T(8,128)(2,1)}, u32[]{:S(2)}, u32[]{:S(2)}) async-start(bf16[8,704,128]{2,1,0:T(8,128)(2,1)} %bitcast.102), calls=%async_computation.1 | async-start | bytes 2883584 | tf_op jit(solution)/shard_map/all_to_all | solution.py:292
  74.7 19.7 %collective-permute-start.6 = (bf16[16,176,128]{2,1,0:T(8,128)(2,1)}, bf16[16,176,128]{2,1,0:T(8,128)(2,1)}, u32[]{:S(2)}, u32[]{:S(2)}) collective-permute-start(bf16[16,176,128]{2,1,0:T(8,128)(2,1)} %collective-permute-done.4), channel_id=1, source_target_pairs={{0,32},{32,64},{64,96},{96,128},{128,160},{160,192},{192,224},{224... | collective-permute-start | bytes 2162696 | tf_op jit(solution)/shard_map/ppermute | solution.py:222
  74.7 21.5 %collective-permute-start.5 = (bf16[16,176,128]{2,1,0:T(8,128)(2,1)}, bf16[16,176,128]{2,1,0:T(8,128)(2,1)}, u32[]{:S(2)}, u32[]{:S(2)}) collective-permute-start(bf16[16,176,128]{2,1,0:T(8,128)(2,1)} %collective-permute-done.3), channel_id=1, source_target_pairs={{0,224},{32,0},{64,32},{96,64},{128,96},{160,128},{192,160},{224,1... | collective-permute-start | bytes 2162696 | tf_op jit(solution)/shard_map/ppermute | solution.py:223
  101.2 26.8 %all-to-all-start.2 = ((bf16[8,704,128]{2,1,0:T(8,128)(2,1)}), bf16[8,704,128]{2,1,0:T(8,128)(2,1)}, u32[]{:S(2)}, u32[]{:S(2)}) async-start(bf16[8,704,128]{2,1,0:T(8,128)(2,1)} %bitcast.101), calls=%async_computation.2 | async-start | bytes 2883584 | tf_op jit(solution)/shard_map/all_to_all | solution.py:292
  106.1 143.4 %all-gather.4.cloned.1.call-start = ((), (), s32[]{:S(2)}) async-start(), calls=%async_computation.4 | async-start | bytes 1392640 | tf_op jit(solution)/shard_map/all_gather | solution.py:272
  106.1 68.6 %collective-permute-start = (bf16[64,32,576]{2,1,0:T(8,128)(2,1)}, bf16[64,32,576]{2,1,0:T(8,128)(2,1)}, u32[]{:S(2)}, u32[]{:S(2)}) collective-permute-start(bf16[64,32,576]{2,1,0:T(8,128)(2,1)} %q_own.3), channel_id=1, source_target_pairs={{0,3},{1,2},{2,1},{3,0},{4,5},{5,4},{6,7},{7,6},{8,11},{9,10},{10,... | collective-permute-start | bytes 7077896 | tf_op jit(solution)/shard_map/ppermute | solution.py:269
  109.1 5.7 %copy-start.13 = (bf16[64,16]{0,1:T(8,128)(2,1)S(1)}, bf16[64,16]{0,1:T(8,128)(2,1)}, u32[]{:S(2)}) copy-start(bf16[64,16]{0,1:T(8,128)(2,1)} %param.10) | copy-start | bytes 6148
  109.1 5.8 %copy-start.10 = (bf16[64,16,128]{2,1,0:T(8,128)(2,1)S(1)}, bf16[64,16,128]{2,1,0:T(8,128)(2,1)}, u32[]{:S(2)}) copy-start(bf16[64,16,128]{2,1,0:T(8,128)(2,1)} %param.9) | copy-start | bytes 786436
  110.4 86.2 %collective-permute-start.9 = (bf16[48,144,128]{2,1,0:T(8,128)(2,1)}, bf16[48,144,128]{2,1,0:T(8,128)(2,1)}, u32[]{:S(2)}, u32[]{:S(2)}) collective-permute-start(bf16[48,144,128]{2,1,0:T(8,128)(2,1)} %slice.119), channel_id=1, source_target_pairs={{0,1},{1,0},{2,3},{3,2},{4,7},{5,6},{6,5},{7,4},{8,9},{9,8},{10,11... | collective-permute-start | bytes 5308424 | tf_op jit(solution)/shard_map/ppermute | solution.py:295
  111.6 10.6 %collective-permute-start.8 = (bf16[8,176,128]{2,1,0:T(8,128)(2,1)S(1)}, bf16[8,176,128]{2,1,0:T(8,128)(2,1)S(1)}, u32[]{:S(2)}, u32[]{:S(2)}) collective-permute-start(bf16[8,176,128]{2,1,0:T(8,128)(2,1)S(1)} %slice.118), channel_id=1, source_target_pairs={{0,224},{32,0},{64,32},{96,64},{128,96},{160,128},{192,160},{224,1... | collective-permute-start | bytes 1081352 | tf_op jit(solution)/shard_map/ppermute | solution.py:227
  113.9 11.6 %collective-permute-start.7 = (bf16[8,176,128]{2,1,0:T(8,128)(2,1)S(1)}, bf16[8,176,128]{2,1,0:T(8,128)(2,1)}, u32[]{:S(2)}, u32[]{:S(2)}) collective-permute-start(bf16[8,176,128]{2,1,0:T(8,128)(2,1)S(1)} %slice.117), channel_id=1, source_target_pairs={{0,32},{32,64},{64,96},{96,128},{128,160},{160,192},{192,224},{224... | collective-permute-start | bytes 1081352 | tf_op jit(solution)/shard_map/ppermute | solution.py:227
  128.1 15.8 %all-to-all-start.3 = ((bf16[8,352,128]{2,1,0:T(8,128)(2,1)}), bf16[8,352,128]{2,1,0:T(8,128)(2,1)S(1)}, u32[]{:S(2)}, u32[]{:S(2)}) async-start(bf16[8,352,128]{2,1,0:T(8,128)(2,1)} %bitcast.104), calls=%async_computation.3 | async-start | bytes 1441792 | tf_op jit(solution)/shard_map/all_to_all | solution.py:292
  135.3 61.4 %collective-permute-start.10 = (bf16[32,144,128]{2,1,0:T(8,128)(2,1)}, bf16[32,144,128]{2,1,0:T(8,128)(2,1)}, u32[]{:S(2)}, u32[]{:S(2)}) collective-permute-start(bf16[32,144,128]{2,1,0:T(8,128)(2,1)} %slice.120), channel_id=1, source_target_pairs={{0,1},{1,0},{2,3},{3,2},{4,7},{5,6},{6,5},{7,4},{8,9},{9,8},{10,11... | collective-permute-start | bytes 3538952 | tf_op jit(solution)/shard_map/ppermute | solution.py:295
  135.9 9.7 %copy-start.12 = (s32[64,16]{0,1:T(8,128)S(1)}, s32[64,16]{0,1:T(8,128)}, u32[]{:S(2)}) copy-start(s32[64,16]{0,1:T(8,128)} %param.13) | copy-start | bytes 12292
  138.3 58.3 %collective-permute-start.11 = (bf16[32,144,128]{2,1,0:T(8,128)(2,1)}, bf16[32,144,128]{2,1,0:T(8,128)(2,1)}, u32[]{:S(2)}, u32[]{:S(2)}) collective-permute-start(bf16[32,144,128]{2,1,0:T(8,128)(2,1)} %slice.121), channel_id=1, source_target_pairs={{0,1},{1,0},{2,3},{3,2},{4,7},{5,6},{6,5},{7,4},{8,9},{9,8},{10,11... | collective-permute-start | bytes 3538952 | tf_op jit(solution)/shard_map/ppermute | solution.py:295
  144.7 51.9 %collective-permute-start.12 = (bf16[16,144,128]{2,1,0:T(8,128)(2,1)}, bf16[16,144,128]{2,1,0:T(8,128)(2,1)S(1)}, u32[]{:S(2)}, u32[]{:S(2)}) collective-permute-start(bf16[16,144,128]{2,1,0:T(8,128)(2,1)} %slice.122), channel_id=1, source_target_pairs={{0,1},{1,0},{2,3},{3,2},{4,7},{5,6},{6,5},{7,4},{8,9},{9,8},{10,11... | collective-permute-start | bytes 1769480 | tf_op jit(solution)/shard_map/ppermute | solution.py:295
  145.7 0.6 copy-start.9
  149.1 0.6 copy-start.11
  150.4 88.7 %copy-start.7 = (s32[2]{0:T(128)}, s32[2]{0:T(128)S(1)}, u32[]{:S(2)}) copy-start(s32[2]{0:T(128)S(1)} %pad_add_fusion.quarters) | copy-start | bytes 28
  196.6 0.7 copy-start.6
  239.1 1.1 copy-start.1
  240.3 78.9 %collective-permute-start.14 = (bf16[48,32,512]{2,1,0:T(8,128)(2,1)}, bf16[48,32,512]{2,1,0:T(8,128)(2,1)}, u32[]{:S(2)}, u32[]{:S(2)}) collective-permute-start(bf16[48,32,512]{2,1,0:T(8,128)(2,1)} %get-tuple-element.10), channel_id=1, source_target_pairs={{0,3},{1,2},{2,1},{3,0},{4,5},{5,4},{6,7},{7,6},{8,11},{9,10},{10,... | collective-permute-start | bytes 4718600 | tf_op jit(solution)/shard_map/ppermute | solution.py:333
  253.2 1.2 copy-start.3
  254.4 0.9 copy-start.4
  262.0 18.4 %copy-start.8 = (s32[2]{0:T(128)S(1)}, s32[2]{0:T(128)}, u32[]{:S(2)}) copy-start(s32[2]{0:T(128)} %copy-done.7) | copy-start | bytes 28
  280.4 1.7 copy-start
  306.0 0.8 copy-start.5
  306.8 12.4 %copy-start.2 = (bf16[48,32,512]{2,1,0:T(8,128)(2,1)S(1)}, bf16[48,32,512]{2,1,0:T(8,128)(2,1)}, u32[]{:S(2)}) copy-start(bf16[48,32,512]{2,1,0:T(8,128)(2,1)} %copy-done.1) | copy-start | bytes 4718596
  306.8 11.0 %collective-permute-start.16 = (bf16[16,32,512]{2,1,0:T(8,128)(2,1)}, bf16[16,32,512]{2,1,0:T(8,128)(2,1)S(1)}, u32[]{:S(2)}, u32[]{:S(2)}) collective-permute-start(bf16[16,32,512]{2,1,0:T(8,128)(2,1)} %get-tuple-element.13), channel_id=1, source_target_pairs={{0,3},{1,2},{2,1},{3,0},{4,5},{5,4},{6,7},{7,6},{8,11},{9,10},{10,... | collective-permute-start | bytes 1572872 | tf_op jit(solution)/shard_map/ppermute | solution.py:333
  307.7 9.8 %collective-permute-start.15 = (f32[16,32]{1,0:T(8,128)S(1)}, f32[16,32]{1,0:T(8,128)S(1)}, u32[]{:S(2)}, u32[]{:S(2)}) collective-permute-start(f32[16,32]{1,0:T(8,128)S(1)} %slice.89), channel_id=1, source_target_pairs={{0,3},{1,2},{2,1},{3,0},{4,5},{5,4},{6,7},{7,6},{8,11},{9,10},{10,... | collective-permute-start | bytes 6152 | tf_op jit(solution)/shard_map/ppermute | solution.py:334
  312.0 5.8 %collective-permute-start.13 = (f32[48,32]{1,0:T(8,128)S(1)}, f32[48,32]{1,0:T(8,128)S(1)}, u32[]{:S(2)}, u32[]{:S(2)}) collective-permute-start(f32[48,32]{1,0:T(8,128)S(1)} %slice.85), channel_id=1, source_target_pairs={{0,3},{1,2},{2,1},{3,0},{4,5},{5,4},{6,7},{7,6},{8,11},{9,10},{10,... | collective-permute-start | bytes 18440 | tf_op jit(solution)/shard_map/ppermute | solution.py:334
Sparse Core Ops, SparseCore 0:
  115.7 33.1 all-gather.3

commit v3 on v2

--- a/solution.py
+++ b/solution.py
@@ -6,11 +6,8 @@
 from jax.sharding import Mesh, PartitionSpec as P
 
 KEY_VALUE_RANK = 512
-LATENT = 576
-ROTARY = LATENT - KEY_VALUE_RANK
 LANES = 128
 COLUMNS = KEY_VALUE_RANK // LANES
-WIDE = KEY_VALUE_RANK + LANES
 TILE = 128
 CAP = 2
 GROUP = 8
@@ -27,101 +24,118 @@
 
 def attend_kernel(sel, lim, quarters, q_own, q_pair, *refs):
     own_fetched, pair_fetched = refs[: len(refs) // 2 - 3], refs[len(refs) // 2 - 3 : -6]
-    out_own, out_pair, lse, rows, rotary, sems = refs[-6:]
+    out_own, out_pair, lse, own, pair, sems = refs[-6:]
     step = pl.program_id(0)
-    slots, half, _ = rows.shape
-    part = half // 2
-    latent, packed, _ = lines_of(part)
+    part = 2 * own.shape[1] // (2 * COLUMNS + 3)
+    low = part // 2
     picks = sel.shape[1]
-    heads = q_own.shape[1] + q_pair.shape[1]
+    half_heads = q_own.shape[1]
+    heads = 2 * half_heads
 
     @pl.when(step == 0)
     def _():
         copies = []
-        for side, fetched in enumerate((own_fetched, pair_fetched)):
+        for rows, fetched in ((own, own_fetched), (pair, pair_fetched)):
             at = 0
             for ref in fetched:
-                count = ref.shape[0]
-                for j in range(COLUMNS):
-                    copies.append(
-                        pltpu.make_async_copy(
-                            ref.at[:, pl.ds(j * part, part), :],
-                            rows.at[pl.ds(at, count), pl.ds(side * part, part), pl.ds(j * LANES, LANES)],
-                            sems.at[len(copies)],
-                        )
-                    )
                 copies.append(
-                    pltpu.make_async_copy(
-                        ref.at[:, pl.ds(latent, packed - latent), :],
-                        rotary.at[pl.ds(at, count), pl.ds(side * (part // 2), part // 2), :],
-                        sems.at[len(copies)],
-                    )
+                    pltpu.make_async_copy(ref, rows.at[pl.ds(at, ref.shape[0])], sems.at[len(copies)])
                 )
-                at += count
+                at += ref.shape[0]
         for copy in copies:
             copy.start()
         for copy in copies:
             copy.wait()
 
-        @pl.loop(0, slots)
-        def _(slot):
-            for side in range(2):
-                pairs = rotary[slot, pl.ds(side * (part // 2), part // 2), :]
-                turned = jnp.concatenate([pairs[:, ROTARY:], pairs[:, :ROTARY]], axis=1)
-                rows[slot, pl.ds(side * part, part), pl.ds(KEY_VALUE_RANK, LANES)] = jnp.concatenate(
-                    [pairs, turned], axis=0
-                )
-
-    row = lax.broadcasted_iota(jnp.int32, (half, heads), 0)
-    place = jnp.where(row < part, row + quarters[0] * part, row - part + quarters[1] * part)
-    per = 256 // half
-
-    def keys(query, n, width):
-        return jnp.concatenate([rows[sel[query, n * per + j], :, :width] for j in range(per)], axis=0)
+    row = lax.broadcasted_iota(jnp.int32, (low, 2 * heads), 0)
+    lane = lax.broadcasted_iota(jnp.int32, (low, 2 * heads), 1)
+    row = jnp.where(lane < heads, row, row + low)
+    places = [row + quarters[side] * part for side in range(2)]
+    sides = (own, pair)
+    per = 256 // (2 * low)
+    blocks = range(0, picks, per)
+
+    def half_rows(ref, slot, upper):
+        return jnp.concatenate(
+            [ref[slot, pl.ds(j * part + upper * low, low), :] for j in range(COLUMNS)], axis=1
+        )
 
     def scores_of(i):
         query = step * GROUP + i
         here = jnp.concatenate([q_own[i], q_pair[i]], axis=0)
+        value, rotary = here[:, :KEY_VALUE_RANK], here[:, KEY_VALUE_RANK:]
+        no_value, no_rotary = jnp.zeros_like(value), jnp.zeros_like(rotary)
+        weights = jnp.concatenate(
+            [
+                jnp.concatenate([value, no_value, rotary, no_rotary], axis=1),
+                jnp.concatenate([no_value, value, no_rotary, rotary], axis=1),
+            ],
+            axis=0,
+        )
         found = []
-        for n in range(picks // per):
+        for n in blocks:
+            lines = []
+            for k in range(n, n + per):
+                slot = sel[query, k]
+                for ref in sides:
+                    lines.append(
+                        jnp.concatenate(
+                            [
+                                half_rows(ref, slot, 0),
+                                half_rows(ref, slot, 1),
+                                ref[slot, pl.ds(COLUMNS * part, low), :],
+                            ],
+                            axis=1,
+                        )
+                    )
             block = lax.dot_general(
-                keys(query, n, LATENT), here, (((1,), (1,)), ((), ())), preferred_element_type=jnp.float32
+                jnp.concatenate(lines, axis=0),
+                weights,
+                (((1,), (1,)), ((), ())),
+                preferred_element_type=jnp.float32,
             )
             block = block * (SCALE * LOG2_E)
-            found += [
-                jnp.where(place <= lim[query, n * per + j], block[j * half : (j + 1) * half], MASKED)
-                for j in range(per)
-            ]
+            for k in range(n, n + per):
+                for side in range(2):
+                    at = ((k - n) * 2 + side) * low
+                    found.append(jnp.where(places[side] <= lim[query, k], block[at : at + low], MASKED))
         return jnp.concatenate(found, axis=0)
+
+    def both(row, op):
+        return op(row, jnp.concatenate([row[:, heads:], row[:, :heads]], axis=1))
 
     for first in range(0, GROUP, BATCH):
         batch = range(first, first + BATCH)
         scores = [scores_of(i) for i in batch]
         probs = []
         for i, s in zip(batch, scores):
-            peak = jnp.max(s, axis=0, keepdims=True)
+            peak = both(jnp.max(s, axis=0, keepdims=True), jnp.maximum)
             p = jnp.exp2(s - peak)
-            total = jnp.sum(p, axis=0, keepdims=True)
-            probs.append((p * (1.0 / total)).astype(jnp.bfloat16))
-            lse[pl.ds(i, 1), pl.ds(0, heads)] = peak + jnp.log2(total)
+            total = both(jnp.sum(p, axis=0, keepdims=True), jnp.add)
+            lse[pl.ds(i, 1), :] = peak + jnp.log2(total)
+            probs.append(jnp.transpose((p * (1.0 / total)).astype(jnp.bfloat16)))
         for i, p in zip(batch, probs):
+            query = step * GROUP + i
             summed = 0.0
-            for n in range(picks // per):
-                summed = summed + lax.dot_general(
-                    p[n * 256 : (n + 1) * 256],
-                    keys(step * GROUP + i, n, KEY_VALUE_RANK),
-                    (((0,), (0,)), ((), ())),
-                    preferred_element_type=jnp.float32,
-                )
+            for n in blocks:
+                for upper in range(2):
+                    values = jnp.concatenate(
+                        [half_rows(ref, sel[query, k], upper) for k in range(n, n + per) for ref in sides], axis=0
+                    )
+                    summed = summed + jnp.dot(
+                        p[upper * heads : (upper + 1) * heads, n * 2 * low : (n + per) * 2 * low],
+                        values,
+                        preferred_element_type=jnp.float32,
+                    )
             summed = summed.astype(jnp.bfloat16)
-            out_own[i] = summed[: heads // 2]
-            out_pair[i] = summed[heads // 2 :]
+            out_own[i] = summed[:half_heads]
+            out_pair[i] = summed[half_heads:]
 
 
 def attend(sel, lim, quarters, q_own, q_pair, own_fetched, pair_fetched, first, count):
     _, heads, width = q_own.shape
     slots = sum(f.shape[0] for f in own_fetched)
-    part = 2 * pair_fetched[0].shape[1] // (2 * COLUMNS + 1)
+    lines = own_fetched[0].shape[1]
     at = first // GROUP
     spec = pltpu.PrefetchScalarGridSpec(
         num_scalar_prefetch=3,
@@ -131,9 +145,9 @@
         out_specs=[pl.BlockSpec((GROUP, heads, KEY_VALUE_RANK), lambda i, *_: (i, 0, 0))] * 2
         + [pl.BlockSpec((GROUP, LANES), lambda i, *_: (i, 0))],
         scratch_shapes=[
-            pltpu.VMEM((slots, 2 * part, WIDE), jnp.bfloat16),
-            pltpu.VMEM((slots, part, LANES), jnp.bfloat16),
-            pltpu.SemaphoreType.DMA((2 * len(own_fetched) * (COLUMNS + 1),)),
+            pltpu.VMEM((slots, lines, LANES), jnp.bfloat16),
+            pltpu.VMEM((slots, lines, LANES), jnp.bfloat16),
+            pltpu.SemaphoreType.DMA((2 * len(own_fetched),)),
         ],
     )
     return pl.pallas_call(
@@ -142,8 +156,33 @@
         out_shape=[jax.ShapeDtypeStruct((count, heads, KEY_VALUE_RANK), jnp.bfloat16)] * 2
         + [jax.ShapeDtypeStruct((count, LANES), jnp.float32)],
         compiler_params=pltpu.CompilerParams(vmem_limit_bytes=40 * 1024 * 1024),
+        cost_estimate=pl.CostEstimate(
+            flops=count * 400_000_000, bytes_accessed=12_000_000, transcendentals=count * 65536
+        ),
         name="attend",
     )(sel[first : first + count], lim[first : first + count], quarters, q_own, q_pair, *own_fetched, *pair_fetched)
+
+
+def take_kernel(asked, *refs):
+    blocks, found = refs[:-1], refs[-1]
+    for to in range(found.shape[0]):
+        for p, block in enumerate(blocks):
+            for slot in range(CAP):
+                found[to, p * CAP + slot] = block[asked[p, to, slot]]
+
+
+def take(asked, blocks):
+    count, plane, _ = asked.shape
+    tile = blocks[0].shape[1:]
+    return pl.pallas_call(
+        take_kernel,
+        in_specs=[pl.BlockSpec(memory_space=pltpu.SMEM)] + [pl.BlockSpec(memory_space=pltpu.VMEM)] * count,
+        out_specs=pl.BlockSpec(memory_space=pltpu.VMEM),
+        out_shape=jax.ShapeDtypeStruct((plane, count * CAP) + tile, blocks[0].dtype),
+        compiler_params=pltpu.CompilerParams(vmem_limit_bytes=16 * 1024 * 1024),
+        cost_estimate=pl.CostEstimate(flops=0, bytes_accessed=count * 1_500_000, transcendentals=0),
+        name="take",
+    )(asked, *blocks)
 
 
 def index_kernel(sel, iq, weight_t, lim, *refs):
@@ -230,9 +269,7 @@
 
 
 def rounds_of(size):
-    rounds = [[0, 1, size - 1]]
-    rounds += [[d, size - d] for d in range(2, size // 2)]
-    return rounds + [[size // 2]]
+    return [[0]] + [[d, size - d] for d in range(1, size // 2)] + [[size // 2]]
 
 
 def pairings():
@@ -252,7 +289,7 @@
     tile_count = latent.shape[0] // TILE
     part = TILE // y_count
     picks = selection.shape[1]
-    _, packed, lines = lines_of(part)
+    _, _, lines = lines_of(part)
     row_pairs, head_pairs = pairings()
 
     def quarter(a):
@@ -282,17 +319,21 @@
     own_fetched, pair_fetched = [], []
     place = {}
     base = 0
-    for distances in rounds_of(z_count):
-        found = []
+    for r, distances in enumerate(rounds_of(z_count)):
+        asked = jnp.stack(
+            [lax.dynamic_index_in_dim(plans, (z + d) % z_count, 1, False) for d in distances]
+        )
+        found = take(asked, [blocks[d] for d in distances])
         for p, d in enumerate(distances):
-            asked = lax.dynamic_index_in_dim(plans, (z + d) % z_count, 1, False)
-            found.append(blocks[d][asked])
             place[d] = (base + p * CAP, len(distances) * CAP)
-        found = jnp.concatenate(found, axis=1).reshape(plane, -1, LANES)
-        moved = lax.all_to_all(found, ("x", "c"), split_axis=0, concat_axis=0, tiled=True)
+        if r == 2:
+            found, q_pair = lax.optimization_barrier((found, q_pair))
+        if r >= 2:
+            found, pair_fetched[r - 2] = lax.optimization_barrier((found, pair_fetched[r - 2]))
+        moved = lax.all_to_all(found.reshape(plane, -1, LANES), ("x", "c"), split_axis=0, concat_axis=0, tiled=True)
         moved = moved.reshape(-1, lines, LANES)
         own_fetched.append(moved)
-        pair_fetched.append(lax.ppermute(moved[:, :packed], ("c", "y"), row_pairs))
+        pair_fetched.append(lax.ppermute(moved, ("c", "y"), row_pairs))
         base += plane * len(distances) * CAP
 
     owner = selection // CAP
@@ -319,9 +360,21 @@
     partner = jnp.where(c == 0, y ^ 1, 3 - y)
 
     index_part = index(rows_at, joined, weight_t, own_lim, own_fetched)
-    index_part = lax.all_gather(index_part, "y").reshape(y_count, query_count, y_count, -1, part)
-    index_part = lax.dynamic_index_in_dim(index_part, y, 2, False)
-    index_scores = jnp.transpose(index_part, (1, 2, 0, 3)).reshape(query_count, -1)
+    rows_at, index_part = lax.optimization_barrier((rows_at, index_part))
+    index_part = index_part.reshape(query_count, y_count, -1)
+    from_quarter = []
+    for d in range(y_count):
+        piece = lax.dynamic_index_in_dim(index_part, (y + d) % y_count, 1, False)
+        if d:
+            piece = lax.ppermute(piece, "y", [(i, (i + d) % y_count) for i in range(y_count)])
+        from_quarter.append(piece.reshape(query_count, -1, part))
+    index_scores = jnp.concatenate(
+        [
+            sum(jnp.where((y - d) % y_count == j, from_quarter[d], 0.0) for d in range(y_count))[:, :, None]
+            for j in range(y_count)
+        ],
+        axis=2,
+    ).reshape(query_count, -1)
 
     quarters = jnp.stack([y, partner])
     attended = []

time: 331 us -> 243 us (0.73)
  waiting for transfers between devices: 103 us -> 71.5 us
  local copies, waits for them, and re-layouts: 50.9 us -> 23.1 us
  blocking collectives: 22.5 us -> 8.67 us
  Pallas kernels: 72.3 us -> 60.2 us
  other arithmetic: 18.4 us -> 7.65 us
  starting transfers between devices: 47.7 us -> 56 us
    ppermute x3, waiting for transfers between devices: 38 us -> 4.18 us  [ring_blocks(): up = lax.ppermute(up, axis, forward)]
    all_to_all x4 -> x5, waiting for transfers between devices: 4.35 us -> 31.7 us  [shards(): lax.all_to_all(found.reshape(plane, -1, LANES), ('x', 'c'), split_axis=0,...]
    ppermute x1, waiting for transfers between devices: 24.2 us -> 0.01 us  [shards(): q_pair = lax.ppermute(queries, ('c', 'y'), head_pairs)]
    pallas_call x2, Pallas kernels: 65.7 us -> 47.5 us  [attend(): pl.pallas_call(attend_kernel, grid_spec=spec, out_shape=[jax.ShapeDtypeSt...]
    ppermute x4 -> x8, waiting for transfers between devices: 22 us -> 5.8 us  [the longest x3 5.79 us: shards(): lax.ppermute(piece, 'y', [(i, (i + d) % y_count) for i in range(y_count)])]
    ppermute x3, waiting for transfers between devices: 0.01 us -> 15.5 us  [ring_blocks(): down = lax.ppermute(down, axis, backward)]
    all_gather x1 -> x0, blocking collectives: 13.8 us -> none  [shards(): lax.all_gather(index_part, 'y')]
    gather x8 -> x0, local copies, waits for them, and re-layouts: 13.5 us -> none  [shards(): found.append(blocks[d][asked])]
  transfers between devices with their start and end apart: 22 -> 27, of which waited for: 11 -> 14; matrix products, arithmetic and copies ran while one was open for 15% -> 7% of each run, Pallas kernels for 22% -> 11%
where the time goes in v3:
time: 243 us; the launch traced here: 242 us
  waiting for transfers between devices  71.5 us (29%)
  Pallas kernels  60.2 us (25%)
  starting transfers between devices  56 us (23%)
  local copies, waits for them, and re-layouts  23.1 us (10%)
  between operations  14.7 us (6%)
  blocking collectives  8.67 us (4%)
  other arithmetic  7.65 us (3%)
    pallas_call x2, Pallas kernels, attend(): pl.pallas_call(attend_kernel, grid_spec=spec, out_shape=[jax.ShapeDtypeSt...  47.5 us
    all_to_all x5, waiting for transfers between devices, shards(): lax.all_to_all(found.reshape(plane, -1, LANES), ('x', 'c'), split_axis=0,...  31.7 us
    all_to_all x5, starting transfers between devices, shards(): lax.all_to_all(found.reshape(plane, -1, LANES), ('x', 'c'), split_axis=0,...  26.7 us
    ppermute x3, waiting for transfers between devices, ring_blocks(): down = lax.ppermute(down, axis, backward)  15.5 us
    unnamed x41, local copies, waits for them, and re-layouts  15 us
    ppermute x3, starting transfers between devices, ring_blocks(): down = lax.ppermute(down, axis, backward)  10 us
    all_gather x1, blocking collectives, shards(): lax.all_gather(wanted, ('x', 'c')).reshape(plane, z_count, plane, CAP)  8.67 us
    pallas_call x1, Pallas kernels, index(): pl.pallas_call(index_kernel, grid_spec=spec, out_shape=jax.ShapeDtypeStru...  6.67 us
  transfers between devices with their start and end apart: 27, of which 14 were waited for; matrix products, arithmetic and copies ran while one was open for 7% of the time, Pallas kernels for 11%

profile of v3, /device:TPU:2, one launch (start us, length us, event | category | flops | bytes accessed | tf_op | source)
XLA Modules:
  0.0 241.8 jit_solution(13737043355837314328)
XLA Ops:
  7.2 3.1 %collective-permute-start.4 = (bf16[64,32,576]{2,1,0:T(8,128)(2,1)}, bf16[64,32,576]{2,1,0:T(8,128)(2,1)}, u32[]{:S(2)}, u32[]{:S(2)}) collective-permute-start(bf16[64,32,576]{2,1,0:T(8,128)(2,1)} %q_own.3), channel_id=1, source_target_pairs={{0,3},{1,2},{2,1},{3,0},{4,5},{5,4},{6,7},{7,6},{8,11},{9,10},{10,... | collective-permute-start | bytes 7077896 | tf_op jit(solution)/shard_map/ppermute | solution.py:306
  10.3 3.1 %copy.115 = bf16[2048,576]{1,0:T(8,128)(2,1)S(1)} copy(bf16[2048,576]{0,1:T(8,128)(2,1)} %param.8) | data formatting | bytes 4718592 | tf_op args[1]
  13.7 0.9 bitcast_dynamic-update-slice_fusion.refs_0_
  14.7 5.9 %collective-permute-start = (bf16[16,176,128]{2,1,0:T(8,128)(2,1)S(1)}, bf16[16,176,128]{2,1,0:T(8,128)(2,1)S(1)}, u32[]{:S(2)}, u32[]{:S(2)}) collective-permute-start(bf16[16,176,128]{2,1,0:T(8,128)(2,1)S(1)} %bitcast_dynamic-update-slice_fusion.refs_0_), channel_id=1, source_target_pairs={{0,224},{32,0},{64,32},{96,64},{128,96},{160,128},{192,160},{224,1... | collective-permute-start | bytes 2162696 | tf_op jit(solution)/shard_map/ppermute | solution.py:262
  20.6 8.7 %all_gather.11 = s32[8,64,2]{1,2,0:T(2,128)S(1)} all-gather(s32[1,64,2]{1,2,0:T(2,128)S(1)} %copy-done.14), channel_id=1, replica_groups=mesh['z'=8,'x'=4,'c'=2,'y'=4] {'x','c'}, dimensions={0}, use_global_device_ids=true | all-gather | bytes 4608 | tf_op jit(solution)/shard_map/all_gather | solution.py:315
  29.6 1.5 take.5
  31.1 6.5 %all-to-all-start = ((bf16[8,352,128]{2,1,0:T(8,128)(2,1)}), bf16[8,352,128]{2,1,0:T(8,128)(2,1)}, u32[]{:S(2)}, u32[]{:S(2)}) async-start(bf16[8,352,128]{2,1,0:T(8,128)(2,1)} %bitcast.12), calls=%async_computation | async-start | bytes 1441792 | tf_op jit(solution)/shard_map/all_to_all | solution.py:333
  37.7 0.9 copy-done.7
  38.6 1.1 copy-done.8
  39.7 1.2 take.6
  40.9 1.1 copy-done.1
  42.0 6.7 %all-to-all-done = bf16[8,352,128]{2,1,0:T(8,128)(2,1)} async-done(((bf16[8,352,128]{2,1,0:T(8,128)(2,1)}), bf16[8,352,128]{2,1,0:T(8,128)(2,1)}, u32[]{:S(2)}, u32[]{:S(2)}) %all-to-all-start) | async-done | bytes 720928 | tf_op jit(solution)/shard_map/all_to_all | solution.py:333
  48.7 4.9 %all-to-all-start.1 = ((bf16[8,704,128]{2,1,0:T(8,128)(2,1)}), bf16[8,704,128]{2,1,0:T(8,128)(2,1)S(1)}, u32[]{:S(2)}, u32[]{:S(2)}) async-start(bf16[8,704,128]{2,1,0:T(8,128)(2,1)} %bitcast.74), calls=%async_computation.1 | async-start | bytes 2883584 | tf_op jit(solution)/shard_map/all_to_all | solution.py:333
  53.7 3.2 %collective-permute-start.2 = (bf16[16,176,128]{2,1,0:T(8,128)(2,1)S(1)}, bf16[16,176,128]{2,1,0:T(8,128)(2,1)S(1)}, u32[]{:S(2)}, u32[]{:S(2)}) collective-permute-start(bf16[16,176,128]{2,1,0:T(8,128)(2,1)S(1)} %copy-done.8), channel_id=1, source_target_pairs={{0,224},{32,0},{64,32},{96,64},{128,96},{160,128},{192,160},{224,1... | collective-permute-start | bytes 2162696 | tf_op jit(solution)/shard_map/ppermute | solution.py:262
  57.1 15.5 %collective-permute-done.2.refs_0_ = bf16[16,176,128]{2,1,0:T(8,128)(2,1)S(1)} collective-permute-done((bf16[16,176,128]{2,1,0:T(8,128)(2,1)S(1)}, bf16[16,176,128]{2,1,0:T(8,128)(2,1)S(1)}, u32[]{:S(2)}, u32[]{:S(2)}) %collective-permute-start.2) | collective-permute-done | bytes 720928 | tf_op jit(solution)/shard_map/ppermute | solution.py:262
  72.6 0.9 copy-done.9
  73.5 2.9 %collective-permute-done.3.refs_1_ = bf16[16,176,128]{2,1,0:T(8,128)(2,1)} collective-permute-done((bf16[16,176,128]{2,1,0:T(8,128)(2,1)}, bf16[16,176,128]{2,1,0:T(8,128)(2,1)}, u32[]{:S(2)}, u32[]{:S(2)}) %collective-permute-start.3) | collective-permute-done | bytes 720928 | tf_op jit(solution)/shard_map/ppermute | solution.py:261
  76.3 1.1 copy-done.10
  77.4 1.2 take.7
  78.7 1.1 copy-done.2
  79.8 4.8 %all-to-all-start.2 = ((bf16[8,704,128]{2,1,0:T(8,128)(2,1)}), bf16[8,704,128]{2,1,0:T(8,128)(2,1)S(1)}, u32[]{:S(2)}, u32[]{:S(2)}) async-start(bf16[8,704,128]{2,1,0:T(8,128)(2,1)} %bitcast.75), calls=%async_computation.2 | async-start | bytes 2883584 | tf_op jit(solution)/shard_map/all_to_all | solution.py:333
  84.8 0.8 collective-permute-start.6
  85.6 1.2 collective-permute-start.7
  86.8 16.6 %all-to-all-done.2 = bf16[8,704,128]{2,1,0:T(8,128)(2,1)S(1)} async-done(((bf16[8,704,128]{2,1,0:T(8,128)(2,1)}), bf16[8,704,128]{2,1,0:T(8,128)(2,1)S(1)}, u32[]{:S(2)}, u32[]{:S(2)}) %all-to-all-start.2) | async-done | bytes 1441824 | tf_op jit(solution)/shard_map/all_to_all | solution.py:333
  103.6 1.3 collective-permute-done.7.refs_1_
  104.9 1.4 take.8
  106.3 1.1 copy-done
  107.4 4.9 %all-to-all-start.3 = ((bf16[8,704,128]{2,1,0:T(8,128)(2,1)}), bf16[8,704,128]{2,1,0:T(8,128)(2,1)}, u32[]{:S(2)}, u32[]{:S(2)}) async-start(bf16[8,704,128]{2,1,0:T(8,128)(2,1)} %bitcast.73), calls=%async_computation.3 | async-start | bytes 2883584 | tf_op jit(solution)/shard_map/all_to_all | solution.py:333
  112.5 0.7 pad_maximum_fusion.2
  113.3 1.0 slice.86
  114.7 1.7 slice.85
  116.4 1.7 collective-permute-start.9
  118.5 1.3 select_reduce_fusion
  119.8 5.1 %collective-permute-done.10 = bf16[8,176,128]{2,1,0:T(8,128)(2,1)} collective-permute-done((bf16[8,176,128]{2,1,0:T(8,128)(2,1)S(1)}, bf16[8,176,128]{2,1,0:T(8,128)(2,1)}, u32[]{:S(2)}, u32[]{:S(2)}) %collective-permute-start.10) | collective-permute-done | bytes 360480 | tf_op jit(solution)/shard_map/ppermute | solution.py:266
  124.9 3.2 %collective-permute-done.9 = bf16[8,176,128]{2,1,0:T(8,128)(2,1)} collective-permute-done((bf16[8,176,128]{2,1,0:T(8,128)(2,1)}, bf16[8,176,128]{2,1,0:T(8,128)(2,1)}, u32[]{:S(2)}, u32[]{:S(2)}) %collective-permute-start.9) | collective-permute-done | bytes 360480 | tf_op jit(solution)/shard_map/ppermute | solution.py:266
  128.1 1.2 pad_maximum_fusion.1.refs_0_
  129.3 0.7 take.9
  130.0 0.9 copy-done.3
  131.2 5.5 %all-to-all-start.4 = ((bf16[8,352,128]{2,1,0:T(8,128)(2,1)}), bf16[8,352,128]{2,1,0:T(8,128)(2,1)}, u32[]{:S(2)}, u32[]{:S(2)}) async-start(bf16[8,352,128]{2,1,0:T(8,128)(2,1)} %bitcast.76), calls=%async_computation.4 | async-start | bytes 1441792 | tf_op jit(solution)/shard_map/all_to_all | solution.py:333
  137.7 0.8 slice.77
  138.6 1.2 collective-permute-start.12
  139.9 8.0 %all-to-all-done.4 = bf16[8,352,128]{2,1,0:T(8,128)(2,1)} async-done(((bf16[8,352,128]{2,1,0:T(8,128)(2,1)}), bf16[8,352,128]{2,1,0:T(8,128)(2,1)}, u32[]{:S(2)}, u32[]{:S(2)}) %all-to-all-start.4) | async-done | bytes 720928 | tf_op jit(solution)/shard_map/all_to_all | solution.py:333
  147.9 1.4 collective-permute-start.13
  149.3 1.2 copy-done.6
  150.5 6.7 %index.1 = f32[64,512]{1,0:T(8,128)S(1)} custom-call(s32[64,16]{1,0:T(8,128)S(1)} %get-tuple-element.22.sel, bf16[4,68,16,128]{3,2,1,0:T(8,128)(2,1)S(1)} %bitcast.78, f32[64,64]{1,0:T(8,128)S(1)} %bitcast.79, s32[64,512]{1,0:T(8,128)S(1)} %broadcast_subtract_fusion.lim, bf16[16,176,128]{2,1,0:T(8,128)(2,1)} %bitcast.13.refs_0_, ...), custom_call_target="tpu_custom_call" | custom-call | tf_op jit(solution)/shard_map/index/pallas_call | solution.py:246
  157.4 0.7 copy.132
  158.1 1.1 collective-permute-start.20
  159.2 0.7 copy.131
  160.0 1.6 collective-permute-start.19
  161.7 0.7 copy.130
  162.4 0.6 collective-permute-start.18
  163.0 4.8 %collective-permute-done.20 = f32[64,128]{0,1:T(8,128)S(1)} collective-permute-done((f32[64,128]{0,1:T(8,128)}, f32[64,128]{0,1:T(8,128)S(1)}, u32[]{:S(2)}, u32[]{:S(2)}) %collective-permute-start.20) | collective-permute-done | bytes 32800 | tf_op jit(solution)/shard_map/ppermute | solution.py:369
  167.7 1.0 collective-permute-done.19
  168.9 32.5 %attend.2 = (bf16[48,32,512]{2,1,0:T(8,128)(2,1)S(1)}, bf16[48,32,512]{2,1,0:T(8,128)(2,1)}, f32[48,128]{1,0:T(8,128)S(1)}) custom-call(s32[48,16]{1,0:T(8,128)S(1)} %slice.69.sel, s32[48,16]{1,0:T(8,128)S(1)} %slice.87.lim, s32[2]{0:T(128)S(1)} %pad_add_fusion.3.quarters, bf16[64,32,576]{2,1,0:T(8,128)(2,1)} %q_own.3, ...), custom_call_target="tpu_custom_call" | custom-call | flops 19200000000 | bytes 12000000 | tf_op jit(solution)/shard_map/attend/pallas_call | solution.py:153
  201.4 1.2 copy-done.4
  202.6 2.3 collective-permute-start.15
  205.0 15.0 %attend.3 = (bf16[16,32,512]{2,1,0:T(8,128)(2,1)S(1)}, bf16[16,32,512]{2,1,0:T(8,128)(2,1)}, f32[16,128]{1,0:T(8,128)S(1)}) custom-call(s32[16,16]{1,0:T(8,128)S(1)} %slice.73.sel, s32[16,16]{1,0:T(8,128)S(1)} %slice.88.lim, s32[2]{0:T(128)S(1)} %pad_add_fusion.3.quarters, bf16[64,32,576]{2,1,0:T(8,128)(2,1)} %q_own.3, ...), custom_call_target="tpu_custom_call" | custom-call | flops 6400000000 | bytes 12000000 | tf_op jit(solution)/shard_map/attend/pallas_call | solution.py:153
  220.0 1.0 collective-permute-start.17
  221.1 2.3 collective-permute-start.16
  223.4 0.8 copy.134
  224.3 1.0 collective-permute-start.14
  225.2 5.5 %collective-permute-done.16 = f32[16,32]{1,0:T(8,128)S(1)} collective-permute-done((f32[16,32]{1,0:T(8,128)S(1)}, f32[16,32]{1,0:T(8,128)S(1)}, u32[]{:S(2)}, u32[]{:S(2)}) %collective-permute-start.16) | collective-permute-done | bytes 2080 | tf_op jit(solution)/shard_map/ppermute | solution.py:387
  231.4 2.1 add_convert_fusion
  233.5 1.5 pad_maximum_fusion
  (97 shorter events, 4.7 us)
Async XLA Ops:
  7.2 72.6 %collective-permute-start.4 = (bf16[64,32,576]{2,1,0:T(8,128)(2,1)}, bf16[64,32,576]{2,1,0:T(8,128)(2,1)}, u32[]{:S(2)}, u32[]{:S(2)}) collective-permute-start(bf16[64,32,576]{2,1,0:T(8,128)(2,1)} %q_own.3), channel_id=1, source_target_pairs={{0,3},{1,2},{2,1},{3,0},{4,5},{5,4},{6,7},{7,6},{8,11},{9,10},{10,... | collective-permute-start | bytes 7077896 | tf_op jit(solution)/shard_map/ppermute | solution.py:306
  13.4 7.3 %copy-start.14 = (s32[1,64,2]{1,2,0:T(2,128)S(1)}, s32[1,64,2]{1,2,0:T(2,128)}, u32[]{:S(2)}) copy-start(s32[1,64,2]{1,2,0:T(2,128)} %param.12) | copy-start | bytes 1540
  14.7 23.0 %collective-permute-start = (bf16[16,176,128]{2,1,0:T(8,128)(2,1)S(1)}, bf16[16,176,128]{2,1,0:T(8,128)(2,1)S(1)}, u32[]{:S(2)}, u32[]{:S(2)}) collective-permute-start(bf16[16,176,128]{2,1,0:T(8,128)(2,1)S(1)} %bitcast_dynamic-update-slice_fusion.refs_0_), channel_id=1, source_target_pairs={{0,224},{32,0},{64,32},{96,64},{128,96},{160,128},{192,160},{224,1... | collective-permute-start | bytes 2162696 | tf_op jit(solution)/shard_map/ppermute | solution.py:262
  20.6 17.9 %collective-permute-start.1 = (bf16[16,176,128]{2,1,0:T(8,128)(2,1)S(1)}, bf16[16,176,128]{2,1,0:T(8,128)(2,1)}, u32[]{:S(2)}, u32[]{:S(2)}) collective-permute-start(bf16[16,176,128]{2,1,0:T(8,128)(2,1)S(1)} %bitcast_dynamic-update-slice_fusion.refs_0_), channel_id=1, source_target_pairs={{0,32},{32,64},{64,96},{96,128},{128,160},{160,192},{192,224},{224... | collective-permute-start | bytes 2162696 | tf_op jit(solution)/shard_map/ppermute | solution.py:261
  31.1 17.6 %all-to-all-start = ((bf16[8,352,128]{2,1,0:T(8,128)(2,1)}), bf16[8,352,128]{2,1,0:T(8,128)(2,1)}, u32[]{:S(2)}, u32[]{:S(2)}) async-start(bf16[8,352,128]{2,1,0:T(8,128)(2,1)} %bitcast.12), calls=%async_computation | async-start | bytes 1441792 | tf_op jit(solution)/shard_map/all_to_all | solution.py:333
  37.7 0.9 copy-start.7
  38.6 1.1 copy-start.8
  40.9 1.1 copy-start.1
  48.7 31.1 %all-to-all-start.1 = ((bf16[8,704,128]{2,1,0:T(8,128)(2,1)}), bf16[8,704,128]{2,1,0:T(8,128)(2,1)S(1)}, u32[]{:S(2)}, u32[]{:S(2)}) async-start(bf16[8,704,128]{2,1,0:T(8,128)(2,1)} %bitcast.74), calls=%async_computation.1 | async-start | bytes 2883584 | tf_op jit(solution)/shard_map/all_to_all | solution.py:333
  53.7 18.9 %collective-permute-start.2 = (bf16[16,176,128]{2,1,0:T(8,128)(2,1)S(1)}, bf16[16,176,128]{2,1,0:T(8,128)(2,1)S(1)}, u32[]{:S(2)}, u32[]{:S(2)}) collective-permute-start(bf16[16,176,128]{2,1,0:T(8,128)(2,1)S(1)} %copy-done.8), channel_id=1, source_target_pairs={{0,224},{32,0},{64,32},{96,64},{128,96},{160,128},{192,160},{224,1... | collective-permute-start | bytes 2162696 | tf_op jit(solution)/shard_map/ppermute | solution.py:262
  56.9 19.4 %collective-permute-start.3 = (bf16[16,176,128]{2,1,0:T(8,128)(2,1)}, bf16[16,176,128]{2,1,0:T(8,128)(2,1)}, u32[]{:S(2)}, u32[]{:S(2)}) collective-permute-start(bf16[16,176,128]{2,1,0:T(8,128)(2,1)} %collective-permute-done.1.refs_1_), channel_id=1, source_target_pairs={{0,32},{32,64},{64,96},{96,128},{128,160},{160,192},{192,224},{224... | collective-permute-start | bytes 2162696 | tf_op jit(solution)/shard_map/ppermute | solution.py:261
  56.9 22.9 %collective-permute-start.5 = (bf16[16,176,128]{2,1,0:T(8,128)(2,1)}, bf16[16,176,128]{2,1,0:T(8,128)(2,1)}, u32[]{:S(2)}, u32[]{:S(2)}) collective-permute-start(bf16[16,176,128]{2,1,0:T(8,128)(2,1)} %bitcast.13.refs_0_), channel_id=1, source_target_pairs={{0,1},{1,0},{2,3},{3,2},{4,7},{5,6},{6,5},{7,4},{8,9},{9,8},{10,11... | collective-permute-start | bytes 2162696 | tf_op jit(solution)/shard_map/ppermute | solution.py:336
  72.6 0.9 copy-start.9
  76.3 1.1 copy-start.10
  78.7 1.1 copy-start.2
  79.8 23.6 %all-to-all-start.2 = ((bf16[8,704,128]{2,1,0:T(8,128)(2,1)}), bf16[8,704,128]{2,1,0:T(8,128)(2,1)S(1)}, u32[]{:S(2)}, u32[]{:S(2)}) async-start(bf16[8,704,128]{2,1,0:T(8,128)(2,1)} %bitcast.75), calls=%async_computation.2 | async-start | bytes 2883584 | tf_op jit(solution)/shard_map/all_to_all | solution.py:333
  84.6 22.8 %collective-permute-start.8 = (bf16[32,176,128]{2,1,0:T(8,128)(2,1)S(1)}, bf16[32,176,128]{2,1,0:T(8,128)(2,1)}, u32[]{:S(2)}, u32[]{:S(2)}) collective-permute-start(bf16[32,176,128]{2,1,0:T(8,128)(2,1)S(1)} %bitcast.65), channel_id=1, source_target_pairs={{0,1},{1,0},{2,3},{3,2},{4,7},{5,6},{6,5},{7,4},{8,9},{9,8},{10,11... | collective-permute-start | bytes 4325384 | tf_op jit(solution)/shard_map/ppermute | solution.py:336
  84.8 18.8 %collective-permute-start.6 = (bf16[16,176,128]{2,1,0:T(8,128)(2,1)}, bf16[16,176,128]{2,1,0:T(8,128)(2,1)}, u32[]{:S(2)}, u32[]{:S(2)}) collective-permute-start(bf16[16,176,128]{2,1,0:T(8,128)(2,1)} %copy-done.9), channel_id=1, source_target_pairs={{0,224},{32,0},{64,32},{96,64},{128,96},{160,128},{192,160},{224,1... | collective-permute-start | bytes 2162696 | tf_op jit(solution)/shard_map/ppermute | solution.py:262
  85.6 19.3 %collective-permute-start.7 = (bf16[16,176,128]{2,1,0:T(8,128)(2,1)}, bf16[16,176,128]{2,1,0:T(8,128)(2,1)}, u32[]{:S(2)}, u32[]{:S(2)}) collective-permute-start(bf16[16,176,128]{2,1,0:T(8,128)(2,1)} %collective-permute-done.3.refs_1_), channel_id=1, source_target_pairs={{0,32},{32,64},{64,96},{96,128},{128,160},{160,192},{192,224},{224... | collective-permute-start | bytes 2162696 | tf_op jit(solution)/shard_map/ppermute | solution.py:261
  103.3 27.5 %collective-permute-start.11 = (bf16[32,176,128]{2,1,0:T(8,128)(2,1)S(1)}, bf16[32,176,128]{2,1,0:T(8,128)(2,1)}, u32[]{:S(2)}, u32[]{:S(2)}) collective-permute-start(bf16[32,176,128]{2,1,0:T(8,128)(2,1)S(1)} %bitcast.69), channel_id=1, source_target_pairs={{0,1},{1,0},{2,3},{3,2},{4,7},{5,6},{6,5},{7,4},{8,9},{9,8},{10,11... | collective-permute-start | bytes 4325384 | tf_op jit(solution)/shard_map/ppermute | solution.py:336
  106.3 1.1 copy-start
  107.4 5.0 %copy-start.13 = (bf16[64,16]{0,1:T(8,128)(2,1)S(1)}, bf16[64,16]{0,1:T(8,128)(2,1)}, u32[]{:S(2)}) copy-start(bf16[64,16]{0,1:T(8,128)(2,1)} %param.10) | copy-start | bytes 6148
  107.4 5.1 %copy-start.11 = (bf16[64,16,128]{2,1,0:T(8,128)(2,1)S(1)}, bf16[64,16,128]{2,1,0:T(8,128)(2,1)}, u32[]{:S(2)}) copy-start(bf16[64,16,128]{2,1,0:T(8,128)(2,1)} %param.9) | copy-start | bytes 786436
  107.4 23.8 %all-to-all-start.3 = ((bf16[8,704,128]{2,1,0:T(8,128)(2,1)}), bf16[8,704,128]{2,1,0:T(8,128)(2,1)}, u32[]{:S(2)}, u32[]{:S(2)}) async-start(bf16[8,704,128]{2,1,0:T(8,128)(2,1)} %bitcast.73), calls=%async_computation.3 | async-start | bytes 2883584 | tf_op jit(solution)/shard_map/all_to_all | solution.py:333
  112.4 6.0 %copy-start.12 = (s32[64,16]{0,1:T(8,128)S(1)}, s32[64,16]{0,1:T(8,128)}, u32[]{:S(2)}) copy-start(s32[64,16]{0,1:T(8,128)} %param.13) | copy-start | bytes 12292
  112.4 25.3 %all-gather.3.cloned.1.call-start = ((), (), s32[]{:S(2)}) async-start(), calls=%async_computation.5 | async-start | bytes 1392640 | tf_op jit(solution)/shard_map/all_gather | solution.py:309
  114.3 10.7 %collective-permute-start.10 = (bf16[8,176,128]{2,1,0:T(8,128)(2,1)S(1)}, bf16[8,176,128]{2,1,0:T(8,128)(2,1)}, u32[]{:S(2)}, u32[]{:S(2)}) collective-permute-start(bf16[8,176,128]{2,1,0:T(8,128)(2,1)S(1)} %slice.86), channel_id=1, source_target_pairs={{0,224},{32,0},{64,32},{96,64},{128,96},{160,128},{192,160},{224,1... | collective-permute-start | bytes 1081352 | tf_op jit(solution)/shard_map/ppermute | solution.py:266
  116.4 11.7 %collective-permute-start.9 = (bf16[8,176,128]{2,1,0:T(8,128)(2,1)}, bf16[8,176,128]{2,1,0:T(8,128)(2,1)}, u32[]{:S(2)}, u32[]{:S(2)}) collective-permute-start(bf16[8,176,128]{2,1,0:T(8,128)(2,1)} %slice.85), channel_id=1, source_target_pairs={{0,32},{32,64},{64,96},{96,128},{128,160},{160,192},{192,224},{224... | collective-permute-start | bytes 1081352 | tf_op jit(solution)/shard_map/ppermute | solution.py:266
  130.0 0.9 copy-start.3
  131.2 16.7 %all-to-all-start.4 = ((bf16[8,352,128]{2,1,0:T(8,128)(2,1)}), bf16[8,352,128]{2,1,0:T(8,128)(2,1)}, u32[]{:S(2)}, u32[]{:S(2)}) async-start(bf16[8,352,128]{2,1,0:T(8,128)(2,1)} %bitcast.76), calls=%async_computation.4 | async-start | bytes 1441792 | tf_op jit(solution)/shard_map/all_to_all | solution.py:333
  138.6 30.3 %collective-permute-start.12 = (bf16[32,176,128]{2,1,0:T(8,128)(2,1)}, bf16[32,176,128]{2,1,0:T(8,128)(2,1)}, u32[]{:S(2)}, u32[]{:S(2)}) collective-permute-start(bf16[32,176,128]{2,1,0:T(8,128)(2,1)} %bitcast.25.refs_3_), channel_id=1, source_target_pairs={{0,1},{1,0},{2,3},{3,2},{4,7},{5,6},{6,5},{7,4},{8,9},{9,8},{10,11... | collective-permute-start | bytes 4325384 | tf_op jit(solution)/shard_map/ppermute | solution.py:336
  147.9 21.0 %collective-permute-start.13 = (bf16[16,176,128]{2,1,0:T(8,128)(2,1)}, bf16[16,176,128]{2,1,0:T(8,128)(2,1)}, u32[]{:S(2)}, u32[]{:S(2)}) collective-permute-start(bf16[16,176,128]{2,1,0:T(8,128)(2,1)} %bitcast.28.refs_4_), channel_id=1, source_target_pairs={{0,1},{1,0},{2,3},{3,2},{4,7},{5,6},{6,5},{7,4},{8,9},{9,8},{10,11... | collective-permute-start | bytes 2162696 | tf_op jit(solution)/shard_map/ppermute | solution.py:336
  149.3 1.2 copy-start.6
  158.1 9.6 %collective-permute-start.20 = (f32[64,128]{0,1:T(8,128)}, f32[64,128]{0,1:T(8,128)S(1)}, u32[]{:S(2)}, u32[]{:S(2)}) collective-permute-start(f32[64,128]{0,1:T(8,128)} %bitcast.36), channel_id=1, source_target_pairs={{0,3},{1,0},{2,1},{3,2},{4,7},{5,4},{6,5},{7,6},{8,11},{9,8},{10,9... | collective-permute-start | bytes 98312 | tf_op jit(solution)/shard_map/ppermute | solution.py:369
  160.0 8.8 %collective-permute-start.19 = (f32[64,128]{0,1:T(8,128)}, f32[64,128]{0,1:T(8,128)S(1)}, u32[]{:S(2)}, u32[]{:S(2)}) collective-permute-start(f32[64,128]{0,1:T(8,128)} %bitcast.34), channel_id=1, source_target_pairs={{0,2},{1,3},{2,0},{3,1},{4,6},{5,7},{6,4},{7,5},{8,10},{9,11},{10,... | collective-permute-start | bytes 98312 | tf_op jit(solution)/shard_map/ppermute | solution.py:369
  162.4 6.4 %collective-permute-start.18 = (f32[64,128]{0,1:T(8,128)}, f32[64,128]{0,1:T(8,128)S(1)}, u32[]{:S(2)}, u32[]{:S(2)}) collective-permute-start(f32[64,128]{0,1:T(8,128)} %bitcast.32), channel_id=1, source_target_pairs={{0,1},{1,2},{2,3},{3,0},{4,5},{5,6},{6,7},{7,4},{8,9},{9,10},{10,1... | collective-permute-start | bytes 98312 | tf_op jit(solution)/shard_map/ppermute | solution.py:369
  201.4 1.2 copy-start.4
  202.6 28.8 %collective-permute-start.15 = (bf16[48,32,512]{2,1,0:T(8,128)(2,1)}, bf16[48,32,512]{2,1,0:T(8,128)(2,1)}, u32[]{:S(2)}, u32[]{:S(2)}) collective-permute-start(bf16[48,32,512]{2,1,0:T(8,128)(2,1)} %get-tuple-element.29), channel_id=1, source_target_pairs={{0,3},{1,2},{2,1},{3,0},{4,5},{5,4},{6,7},{7,6},{8,11},{9,10},{10,... | collective-permute-start | bytes 4718600 | tf_op jit(solution)/shard_map/ppermute | solution.py:386
  220.0 11.1 %collective-permute-start.17 = (bf16[16,32,512]{2,1,0:T(8,128)(2,1)}, bf16[16,32,512]{2,1,0:T(8,128)(2,1)S(1)}, u32[]{:S(2)}, u32[]{:S(2)}) collective-permute-start(bf16[16,32,512]{2,1,0:T(8,128)(2,1)} %get-tuple-element.32), channel_id=1, source_target_pairs={{0,3},{1,2},{2,1},{3,0},{4,5},{5,4},{6,7},{7,6},{8,11},{9,10},{10,... | collective-permute-start | bytes 1572872 | tf_op jit(solution)/shard_map/ppermute | solution.py:386
  221.1 9.7 %collective-permute-start.16 = (f32[16,32]{1,0:T(8,128)S(1)}, f32[16,32]{1,0:T(8,128)S(1)}, u32[]{:S(2)}, u32[]{:S(2)}) collective-permute-start(f32[16,32]{1,0:T(8,128)S(1)} %slice.75), channel_id=1, source_target_pairs={{0,3},{1,2},{2,1},{3,0},{4,5},{5,4},{6,7},{7,6},{8,11},{9,10},{10,... | collective-permute-start | bytes 6152 | tf_op jit(solution)/shard_map/ppermute | solution.py:387
  223.4 8.0 %copy-start.5 = (bf16[48,32,512]{2,1,0:T(8,128)(2,1)S(1)}, bf16[48,32,512]{2,1,0:T(8,128)(2,1)}, u32[]{:S(2)}) copy-start(bf16[48,32,512]{2,1,0:T(8,128)(2,1)} %copy-done.4) | copy-start | bytes 4718596
  224.3 6.7 %collective-permute-start.14 = (f32[48,32]{1,0:T(8,128)S(1)}, f32[48,32]{1,0:T(8,128)S(1)}, u32[]{:S(2)}, u32[]{:S(2)}) collective-permute-start(f32[48,32]{1,0:T(8,128)S(1)} %slice.71), channel_id=1, source_target_pairs={{0,3},{1,2},{2,1},{3,0},{4,5},{5,4},{6,7},{7,6},{8,11},{9,10},{10,... | collective-permute-start | bytes 18440 | tf_op jit(solution)/shard_map/ppermute | solution.py:387
Sparse Core Ops, SparseCore 0:
  115.0 22.6 all-gather.2

commit v4 on v3

v4 whole, which is shorter than its diff:
```python
import functools

import jax
import jax.numpy as jnp
from jax import lax
from jax.experimental import pallas as pl
from jax.experimental.pallas import tpu as pltpu
from jax.sharding import Mesh, PartitionSpec as P

KEY_VALUE_RANK = 512
LANES = 128
COLUMNS = KEY_VALUE_RANK // LANES
TILE = 128
CAP = 2
PART = 32
GROUP = 8
BATCH = 8
SCALE = 192.0 ** -0.5
LOG2_E = 1.4426950408889634
MASKED = -1e30


def lines_of(part):
    latent = COLUMNS * part
    return latent, latent + part // 2, latent + part // 2 + part


def attend_kernel(sel, lim, quarter, q_own, q_pair, *refs, merge, fetched_count):
    refs = list(refs)
    earlier, earlier_lse = (refs.pop(0), refs.pop(0)) if merge else (None, None)
    fetched, outs, (rows, sems) = refs[:fetched_count], refs[fetched_count:-2], refs[-2:]
    lse = outs[-1]
    step = pl.program_id(0)
    picks = sel.shape[1]
    half_heads = q_own.shape[1]
    heads = 2 * half_heads
    part = PART
    low = part // 2

    @pl.when(step == 0)
    def _():
        copies, at = [], 0
        for ref in fetched:
            size = ref.shape[0]
            copies.append(
                pltpu.make_async_copy(
                    ref.at[:, pl.ds(0, rows.shape[1])], rows.at[pl.ds(at, size)], sems.at[len(copies)]
                )
            )
            at += size
        for copy in copies:
            copy.start()
        for copy in copies:
            copy.wait()

    row = lax.broadcasted_iota(jnp.int32, (low, 2 * heads), 0)
    lane = lax.broadcasted_iota(jnp.int32, (low, 2 * heads), 1)
    place = jnp.where(lane < heads, row, row + low) + quarter[0] * part
    head = lax.broadcasted_iota(jnp.int32, (heads, 2 * heads), 0)
    own_lane = lax.broadcasted_iota(jnp.int32, (heads, 2 * heads), 1) == head

    def half_rows(slot, upper):
        return jnp.concatenate(
            [rows[slot, pl.ds(j * part + upper * low, low), :] for j in range(COLUMNS)], axis=1
        )

    def scores_of(i):
        query = step * GROUP + i
        here = jnp.concatenate([q_own[i], q_pair[i]], axis=0)
        value, rotary = here[:, :KEY_VALUE_RANK], here[:, KEY_VALUE_RANK:]
        no_value, no_rotary = jnp.zeros_like(value), jnp.zeros_like(rotary)
        weights = jnp.concatenate(
            [
                jnp.concatenate([value, no_value, rotary, no_rotary], axis=1),
                jnp.concatenate([no_value, value, no_rotary, rotary], axis=1),
            ],
            axis=0,
        )
        lines = []
        for k in range(picks):
            slot = sel[query, k]
            lines.append(
                jnp.concatenate(
                    [half_rows(slot, 0), half_rows(slot, 1), rows[slot, pl.ds(COLUMNS * part, low), :]], axis=1
                )
            )
        scores = lax.dot_general(
            jnp.concatenate(lines, axis=0),
            weights,
            (((1,), (1,)), ((), ())),
            preferred_element_type=jnp.float32,
        )
        scores = scores * (SCALE * LOG2_E)
        return jnp.concatenate(
            [
                jnp.where(place <= lim[query, k], scores[k * low : (k + 1) * low], MASKED)
                for k in range(picks)
            ],
            axis=0,
        )

    def both(row, op):
        return op(row, jnp.concatenate([row[:, heads:], row[:, :heads]], axis=1))

    for first in range(0, GROUP, BATCH):
        batch = range(first, first + BATCH)
        scores = [scores_of(i) for i in batch]
        probs, kept = [], []
        for i, s in zip(batch, scores):
            peak = both(jnp.max(s, axis=0, keepdims=True), jnp.maximum)
            p = jnp.exp2(s - peak)
            total = both(jnp.sum(p, axis=0, keepdims=True), jnp.add)
            level = peak + jnp.log2(total)
            if merge:
                before = earlier_lse[pl.ds(i, 1), :]
                top = jnp.maximum(before, level)
                old, new = jnp.exp2(before - top), jnp.exp2(level - top)
                share = 1.0 / (old + new)
                level = top + jnp.log2(old + new)
                kept.append(jnp.sum(jnp.where(own_lane, old * share, 0.0), axis=1, keepdims=True))
                p = p * (new * share / total)
            else:
                p = p * (1.0 / total)
            lse[pl.ds(i, 1), :] = level
            probs.append(jnp.transpose(p.astype(jnp.bfloat16)))
        for j, (i, p) in enumerate(zip(batch, probs)):
            query = step * GROUP + i
            summed = earlier[i].astype(jnp.float32) * kept[j] if merge else 0.0
            for upper in range(2):
                values = jnp.concatenate([half_rows(sel[query, k], upper) for k in range(picks)], axis=0)
                summed = summed + jnp.dot(
                    p[upper * heads : (upper + 1) * heads], values, preferred_element_type=jnp.float32
                )
            summed = summed.astype(jnp.bfloat16)
            if merge:
                outs[0][i] = summed[:half_heads]
                outs[1][i] = summed[half_heads:]
            else:
                outs[0][i] = summed


def attend(sel, lim, quarter, q_own, q_pair, fetched, first, count, earlier=None):
    _, heads, width = q_own.shape
    slots = sum(f.shape[0] for f in fetched)
    at = first // GROUP
    merge = earlier is not None
    lse_spec = pl.BlockSpec((GROUP, LANES), lambda i, *_: (i, 0))
    heads_out = [heads, heads] if merge else [2 * heads]
    before = [
        pl.BlockSpec((GROUP, 2 * heads, KEY_VALUE_RANK), lambda i, *_: (at + i, 0, 0)),
        pl.BlockSpec((GROUP, LANES), lambda i, *_: (at + i, 0)),
    ]
    spec = pltpu.PrefetchScalarGridSpec(
        num_scalar_prefetch=3,
        grid=(count // GROUP,),
        in_specs=[pl.BlockSpec((GROUP, heads, width), lambda i, *_: (at + i, 0, 0))] * 2
        + (before if merge else [])
        + [pl.BlockSpec(memory_space=pl.ANY)] * len(fetched),
        out_specs=[pl.BlockSpec((GROUP, n, KEY_VALUE_RANK), lambda i, *_: (i, 0, 0)) for n in heads_out]
        + [lse_spec],
        scratch_shapes=[
            pltpu.VMEM((slots, lines_of(PART)[1], LANES), jnp.bfloat16),
            pltpu.SemaphoreType.DMA((len(fetched),)),
        ],
    )
    return pl.pallas_call(
        functools.partial(attend_kernel, merge=merge, fetched_count=len(fetched)),
        grid_spec=spec,
        out_shape=[jax.ShapeDtypeStruct((count, n, KEY_VALUE_RANK), jnp.bfloat16) for n in heads_out]
        + [jax.ShapeDtypeStruct((count, LANES), jnp.float32)],
        compiler_params=pltpu.CompilerParams(vmem_limit_bytes=56 * 1024 * 1024),
        cost_estimate=pl.CostEstimate(
            flops=count * 400_000_000, bytes_accessed=12_000_000, transcendentals=count * 32768
        ),
        name="attend_merge" if merge else "attend_own",
    )(
        sel[first : first + count],
        lim[first : first + count],
        quarter,
        q_own,
        q_pair,
        *(earlier if merge else ()),
        *fetched,
    )


def take_kernel(asked, *refs):
    blocks, found = refs[:-1], refs[-1]
    for to in range(found.shape[0]):
        for p, block in enumerate(blocks):
            for slot in range(CAP):
                found[to, p * CAP + slot] = block[asked[p, to, slot]]


def take(asked, blocks):
    count, plane, _ = asked.shape
    tile = blocks[0].shape[1:]
    return pl.pallas_call(
        take_kernel,
        in_specs=[pl.BlockSpec(memory_space=pltpu.SMEM)] + [pl.BlockSpec(memory_space=pltpu.VMEM)] * count,
        out_specs=pl.BlockSpec(memory_space=pltpu.VMEM),
        out_shape=jax.ShapeDtypeStruct((plane, count * CAP) + tile, blocks[0].dtype),
        compiler_params=pltpu.CompilerParams(vmem_limit_bytes=16 * 1024 * 1024),
        cost_estimate=pl.CostEstimate(flops=0, bytes_accessed=count * 1_500_000, transcendentals=0),
        name="take",
    )(asked, *blocks)


def index_kernel(sel, quarter, iq, weight_t, lim, *refs):
    fetched, (index_out, keys, sems) = refs[:-3], refs[-3:]
    step = pl.program_id(0)
    part = keys.shape[1]
    _, packed, lines = lines_of(part)
    picks = sel.shape[1]
    heads = iq.shape[0] * iq.shape[2]

    @pl.when(step == 0)
    def _():
        copies, at = [], 0
        for i, ref in enumerate(fetched):
            count = ref.shape[0]
            copies.append(
                pltpu.make_async_copy(
                    ref.at[:, pl.ds(packed, lines - packed), :], keys.at[pl.ds(at, count)], sems.at[i]
                )
            )
            at += count
        for copy in copies:
            copy.start()
        for copy in copies:
            copy.wait()

    weight_lane = lax.broadcasted_iota(jnp.int32, weight_t.shape, 1)
    all_dots = []
    for i in range(GROUP):
        picked = jnp.concatenate([keys[sel[step * GROUP + i, k]] for k in range(picks)], axis=0)
        all_dots.append(
            lax.dot_general(
                iq[:, i].reshape(heads, iq.shape[3]),
                picked,
                (((1,), (1,)), ((), ())),
                preferred_element_type=jnp.float32,
            )
        )
    sums = []
    for i, dots in enumerate(all_dots):
        here = weight_lane == step * GROUP + i
        weight = jnp.sum(jnp.where(here, weight_t[...], 0.0), axis=1, keepdims=True)
        sums.append(jnp.sum(jnp.maximum(dots, 0.0) * weight, axis=0, keepdims=True))
    sums = jnp.where(lim[...] >= 0, jnp.concatenate(sums, axis=0), 0.0)
    lane = lax.broadcasted_iota(jnp.int32, (GROUP, TILE), 1)
    mine = lane // part == quarter[0]
    for k in range(picks):
        at = k * part // TILE * TILE
        turn = (quarter[0] * part - (k * part - at) + TILE) % TILE
        piece = pltpu.roll(sums[:, at : at + TILE], turn, 1)
        index_out[:, pl.ds(k * TILE, TILE)] = jnp.where(mine, piece, 0.0)


def index(sel, quarter, iq, weight_t, lim, fetched):
    queries, picks = sel.shape
    part = lim.shape[1] // picks
    slots = sum(f.shape[0] for f in fetched)
    spec = pltpu.PrefetchScalarGridSpec(
        num_scalar_prefetch=2,
        grid=(queries // GROUP,),
        in_specs=[
            pl.BlockSpec((iq.shape[0], GROUP) + iq.shape[2:], lambda i, *_: (0, i, 0, 0)),
            pl.BlockSpec(weight_t.shape, lambda i, *_: (0, 0)),
            pl.BlockSpec((GROUP, lim.shape[1]), lambda i, *_: (i, 0)),
        ]
        + [pl.BlockSpec(memory_space=pl.ANY)] * len(fetched),
        out_specs=pl.BlockSpec((GROUP, picks * TILE), lambda i, *_: (i, 0)),
        scratch_shapes=[
            pltpu.VMEM((slots, part, LANES), jnp.bfloat16),
            pltpu.SemaphoreType.DMA((len(fetched),)),
        ],
    )
    return pl.pallas_call(
        index_kernel,
        grid_spec=spec,
        out_shape=jax.ShapeDtypeStruct((queries, picks * TILE), jnp.float32),
        compiler_params=pltpu.CompilerParams(vmem_limit_bytes=16 * 1024 * 1024),
        name="index",
    )(sel, quarter, iq, weight_t, lim, *fetched)


def ring_blocks(block, axis, size):
    forward = [(i, (i + 1) % size) for i in range(size)]
    backward = [(i, (i - 1) % size) for i in range(size)]
    up = down = block
    got = {0: block}
    for d in range(1, size // 2):
        up = lax.ppermute(up, axis, forward)
        down = lax.ppermute(down, axis, backward)
        got[size - d], got[d] = up, down
    half = block.shape[0] // 2
    got[size // 2] = jnp.concatenate(
        [lax.ppermute(up[:half], axis, forward), lax.ppermute(down[half:], axis, backward)]
    )
    return got


def rounds_of(size):
    near = size // 4
    return [
        [0],
        [e for d in range(1, near + 1) for e in (d, size - d)],
        [e for d in range(near + 1, size // 2) for e in (d, size - d)] + [size // 2],
    ]


def pairings():
    near, far = (lambda y: y ^ 1), (lambda y: 3 - y)
    rows = [(4 * c + y, 4 * c + (near, far)[c](y)) for c in range(2) for y in range(4)]
    heads = [(4 * c + y, 4 * c + (far, near)[c](y)) for c in range(2) for y in range(4)]
    return rows, heads


def shards(queries, latent, index_queries, index_weights, index_keys, request_tiles, selection):
    z_count, x_count, c_count, y_count = (lax.axis_size(a) for a in ("z", "x", "c", "y"))
    z, x, c, y = (lax.axis_index(a) for a in ("z", "x", "c", "y"))
    plane = x_count * c_count
    here = x * c_count + c
    query_count, local_heads, _ = queries.shape
    index_heads = index_queries.shape[1]
    tile_count = latent.shape[0] // TILE
    part = TILE // y_count
    picks = selection.shape[1]
    _, packed, lines = lines_of(part)
    row_pairs, head_pairs = pairings()

    def quarter(a):
        return lax.dynamic_index_in_dim(a.reshape(tile_count, y_count, part, a.shape[1]), y, 1, False)

    own_rows, own_keys = quarter(latent), quarter(index_keys)
    rotary = own_rows[:, :, KEY_VALUE_RANK:]
    own = jnp.concatenate(
        [own_rows[:, :, j * LANES : (j + 1) * LANES] for j in range(COLUMNS)]
        + [jnp.concatenate([rotary[:, : part // 2], rotary[:, part // 2 :]], axis=2), own_keys],
        axis=1,
    )

    q_pair = lax.ppermute(queries, ("c", "y"), head_pairs)
    weight_rows = jnp.pad(index_weights, ((0, 0), (0, LANES - index_heads)))
    joined = jnp.concatenate([index_queries, weight_rows.reshape(-1, index_heads, LANES)], axis=0)
    joined = lax.all_gather(joined, "y")
    weights = joined[:, query_count:].reshape(y_count, query_count, LANES)[:, :, :index_heads]
    key_scale = index_keys.shape[1] ** -0.5
    weight_t = jnp.transpose(weights.astype(jnp.float32), (0, 2, 1)).reshape(-1, query_count) * key_scale

    wanted = request_tiles[0]
    plans = lax.all_gather(wanted, ("x", "c")).reshape(plane, z_count, plane, CAP)
    plans = lax.dynamic_index_in_dim(plans, here, 2, False)

    place = {}
    base = 0
    for distances in rounds_of(z_count):
        for p, d in enumerate(distances):
            place[d] = (base + p * CAP, len(distances) * CAP)
        base += plane * len(distances) * CAP
    owner = selection // CAP
    distance = (owner // plane - z) % z_count
    first = sum(jnp.where(distance == d, place[d][0], 0) for d in place)
    stride = sum(jnp.where(distance == d, place[d][1], 0) for d in place)
    rows_at = first + (owner % plane) * stride + selection % CAP

    flat_wanted = wanted.reshape(-1)
    matches = selection[:, :, None] == jnp.arange(flat_wanted.shape[0], dtype=jnp.int32)
    local_tile = jnp.sum(jnp.where(matches, flat_wanted, 0), axis=2)
    tile_start = (owner * tile_count + local_tile) * TILE
    ctx_count = z_count * plane
    context = ctx_count * tile_count * TILE
    query_pos = (
        context
        - ctx_count * query_count
        + (z * plane + here) * query_count
        + jnp.arange(query_count, dtype=jnp.int32)
    )
    lim = query_pos[:, None] - tile_start
    own_lim = (lim - y * part)[:, :, None] - jnp.arange(part, dtype=jnp.int32)
    own_lim = own_lim.reshape(query_count, picks * part)
    partner = jnp.where(c == 0, y ^ 1, 3 - y).astype(jnp.int32)

    blocks = ring_blocks(own, "z", z_count)
    own_fetched, pair_fetched = [], []
    for r, distances in enumerate(rounds_of(z_count)):
        asked = jnp.stack(
            [lax.dynamic_index_in_dim(plans, (z + d) % z_count, 1, False) for d in distances]
        )
        found = take(asked, [blocks[d] for d in distances])
        if r == 1:
            found, q_pair, own_fetched[0] = lax.optimization_barrier((found, q_pair, own_fetched[0]))
        if r == 2:
            found, joined, weight_t, own_lim, lim, rows_at = lax.optimization_barrier(
                (found, joined, weight_t, own_lim, lim, rows_at)
            )
        moved = lax.all_to_all(found.reshape(plane, -1, LANES), ("x", "c"), split_axis=0, concat_axis=0, tiled=True)
        moved = moved.reshape(-1, lines, LANES)
        own_fetched.append(moved)
        pair_fetched.append(lax.ppermute(moved[:, :packed], ("c", "y"), row_pairs))

    lim, *pair_fetched[:2] = lax.optimization_barrier((lim, *pair_fetched[:2]))
    quarter_here = jnp.reshape(y, (1,)).astype(jnp.int32)
    earlier = list(
        attend(rows_at, lim, quarter_here, queries, q_pair, own_fetched, 0, query_count)
    )
    rows_at, earlier[0] = lax.optimization_barrier((rows_at, earlier[0]))
    index_part = index(rows_at, quarter_here, joined, weight_t, own_lim, own_fetched)
    rows_at, index_part = lax.optimization_barrier((rows_at, index_part))
    index_scores = lax.psum_scatter(index_part, "y", scatter_dimension=1, tiled=True)
    split = query_count * 5 // 8
    halves = []
    for first_query, count in ((0, split), (split, query_count - split)):
        mine, other, lse = attend(
            rows_at,
            lim,
            jnp.reshape(partner, (1,)),
            queries,
            q_pair,
            pair_fetched,
            first_query,
            count,
            earlier,
        )
        if not first_query:
            rows_at, lse, index_scores = lax.optimization_barrier((rows_at, lse, index_scores))
        other = lax.ppermute(other, ("c", "y"), head_pairs)
        halves.append([mine, other, lse])
    all_lse = jnp.concatenate([lse[:, local_heads : 2 * local_heads] for _, _, lse in halves], axis=0)
    all_lse = lax.ppermute(all_lse, ("c", "y"), head_pairs)
    attended = []
    for first_query, (mine, other, lse) in zip((0, split), halves):
        lse, other_lse = lse[:, :local_heads], all_lse[first_query : first_query + lse.shape[0]]
        share = 1.0 / (1.0 + jnp.exp2(other_lse - lse))[..., None]
        other_share = 1.0 / (1.0 + jnp.exp2(lse - other_lse))[..., None]
        merged = mine.astype(jnp.float32) * share + other.astype(jnp.float32) * other_share
        attended.append(merged.astype(jnp.bfloat16))
    return jnp.concatenate(attended, axis=0), index_scores


def solution(mesh):
    ctx, head = mesh.devices.shape
    x_count, c_count = 4, 2
    grid = Mesh(
        mesh.devices.reshape(ctx // (x_count * c_count), x_count, c_count, head), ("z", "x", "c", "y")
    )
    ctx_axes = ("z", "x", "c")
    return jax.shard_map(
        shards,
        mesh=grid,
        in_specs=(
            P(ctx_axes, "y", None),
            P(ctx_axes, None),
            P(ctx_axes, "y", None),
            P(ctx_axes, "y"),
            P(ctx_axes, None),
            P(ctx_axes, None, None),
            P(ctx_axes, None),
        ),
        out_specs=(P(ctx_axes, "y", None), P(ctx_axes, "y")),
        check_vma=False,
    )
```

time: 243 us -> 236 us (0.971)
  starting transfers between devices: 56 us -> 44.6 us
  Pallas kernels: 60.2 us -> 64.8 us
    ppermute x3, waiting for transfers between devices: 4.18 us -> 17.3 us  [ring_blocks(): up = lax.ppermute(up, axis, forward)]
    all_to_all x5 -> x3, starting transfers between devices: 26.7 us -> 16.2 us  [shards(): lax.all_to_all(found.reshape(plane, -1, LANES), ('x', 'c'), split_axis=0,...]
    pallas_call x2 -> x3, Pallas kernels: 47.5 us -> 53.5 us  [attend(): pl.pallas_call(functools.partial(attend_kernel, merge=merge, fetched_coun...]
    unnamed x41 -> x51, local copies, waits for them, and re-layouts: 15 us -> 9.59 us
    ppermute x1, waiting for transfers between devices: 5.07 us -> 0.01 us  [ring_blocks(): lax.ppermute(down[half:], axis, backward)]
    ppermute x3, waiting for transfers between devices: 15.5 us -> 11 us  [ring_blocks(): down = lax.ppermute(down, axis, backward)]
    ppermute x10 -> x4, starting transfers between devices: 9.55 us -> 5.08 us  [the longest x1 2.63 us: shards(): all_lse = lax.ppermute(all_lse, ('c', 'y'), head_pairs)]
    slice x0 -> x3, local copies, waits for them, and re-layouts: none -> 3.94 us  [shards(): pair_fetched.append(lax.ppermute(moved[:, :packed], ('c', 'y'), row_pairs))]
  transfers between devices with their start and end apart: 27 -> 20, of which waited for: 14 -> 8; matrix products, arithmetic and copies ran while one was open for 7% -> 10% of each run, Pallas kernels for 11% -> 28%
where the time goes in v4:
time: 236 us; the launch traced here: 235 us
  waiting for transfers between devices  71.6 us (30%)
  Pallas kernels  64.8 us (27%)
  starting transfers between devices  44.6 us (19%)
  local copies, waits for them, and re-layouts  23.3 us (10%)
  between operations  14.5 us (6%)
  blocking collectives  8.67 us (4%)
  other arithmetic  7.33 us (3%)
    pallas_call x3, Pallas kernels, attend(): pl.pallas_call(functools.partial(attend_kernel, merge=merge, fetched_coun...  53.5 us
    all_to_all x3, waiting for transfers between devices, shards(): lax.all_to_all(found.reshape(plane, -1, LANES), ('x', 'c'), split_axis=0,...  31.4 us
    ppermute x3, waiting for transfers between devices, ring_blocks(): up = lax.ppermute(up, axis, forward)  17.3 us
    all_to_all x3, starting transfers between devices, shards(): lax.all_to_all(found.reshape(plane, -1, LANES), ('x', 'c'), split_axis=0,...  16.2 us
    ppermute x3, starting transfers between devices, ring_blocks(): down = lax.ppermute(down, axis, backward)  12.8 us
    ppermute x3, waiting for transfers between devices, ring_blocks(): down = lax.ppermute(down, axis, backward)  11 us
    ppermute x1, waiting for transfers between devices, shards(): all_lse = lax.ppermute(all_lse, ('c', 'y'), head_pairs)  10.5 us
    unnamed x51, local copies, waits for them, and re-layouts  9.59 us
  transfers between devices with their start and end apart: 20, of which 8 were waited for; matrix products, arithmetic and copies ran while one was open for 10% of the time, Pallas kernels for 28%

profile of v4, /device:TPU:2, one launch (start us, length us, event | category | flops | bytes accessed | tf_op | source)
XLA Modules:
  0.0 234.7 jit_solution(7361253995813355310)
XLA Ops:
  7.2 3.1 %collective-permute-start.9 = (bf16[64,32,576]{2,1,0:T(8,128)(2,1)}, bf16[64,32,576]{2,1,0:T(8,128)(2,1)}, u32[]{:S(2)}, u32[]{:S(2)}) collective-permute-start(bf16[64,32,576]{2,1,0:T(8,128)(2,1)} %q_own.5), channel_id=1, source_target_pairs={{0,3},{1,2},{2,1},{3,0},{4,5},{5,4},{6,7},{7,6},{8,11},{9,10},{10,... | collective-permute-start | bytes 7077896 | tf_op jit(solution)/shard_map/ppermute | solution.py:344
  10.3 3.1 %copy.93 = bf16[2048,576]{1,0:T(8,128)(2,1)S(1)} copy(bf16[2048,576]{0,1:T(8,128)(2,1)} %param.8) | data formatting | bytes 4718592 | tf_op args[1]
  13.6 0.1 maximum_dynamic-update-slice_fusion
  13.7 0.9 bitcast_dynamic-update-slice_fusion.refs_0_
  14.7 5.9 %collective-permute-start = (bf16[16,176,128]{2,1,0:T(8,128)(2,1)S(1)}, bf16[16,176,128]{2,1,0:T(8,128)(2,1)S(1)}, u32[]{:S(2)}, u32[]{:S(2)}) collective-permute-start(bf16[16,176,128]{2,1,0:T(8,128)(2,1)S(1)} %bitcast_dynamic-update-slice_fusion.refs_0_), channel_id=1, source_target_pairs={{0,224},{32,0},{64,32},{96,64},{128,96},{160,128},{192,160},{224,1... | collective-permute-start | bytes 2162696 | tf_op jit(solution)/shard_map/ppermute | solution.py:295
  20.6 8.7 %all_gather.9 = s32[8,64,2]{1,2,0:T(2,128)S(1)} all-gather(s32[1,64,2]{1,2,0:T(2,128)S(1)} %copy-done.19), channel_id=1, replica_groups=mesh['z'=8,'x'=4,'c'=2,'y'=4] {'x','c'}, dimensions={0}, use_global_device_ids=true | all-gather | bytes 4608 | tf_op jit(solution)/shard_map/all_gather | solution.py:353
  29.3 0.1 copy.116
  29.4 4.9 %collective-permute-done.refs_0_ = bf16[16,176,128]{2,1,0:T(8,128)(2,1)S(1)} collective-permute-done((bf16[16,176,128]{2,1,0:T(8,128)(2,1)S(1)}, bf16[16,176,128]{2,1,0:T(8,128)(2,1)S(1)}, u32[]{:S(2)}, u32[]{:S(2)}) %collective-permute-start) | collective-permute-done | bytes 720928 | tf_op jit(solution)/shard_map/ppermute | solution.py:295
  34.3 3.7 %collective-permute-start.1 = (bf16[16,176,128]{2,1,0:T(8,128)(2,1)S(1)}, bf16[16,176,128]{2,1,0:T(8,128)(2,1)S(1)}, u32[]{:S(2)}, u32[]{:S(2)}) collective-permute-start(bf16[16,176,128]{2,1,0:T(8,128)(2,1)S(1)} %collective-permute-done.refs_0_), channel_id=1, source_target_pairs={{0,224},{32,0},{64,32},{96,64},{128,96},{160,128},{192,160},{224,1... | collective-permute-start | bytes 2162696 | tf_op jit(solution)/shard_map/ppermute | solution.py:295
  38.1 1.5 take.4
  39.6 4.8 %all-to-all-start = ((bf16[8,352,128]{2,1,0:T(8,128)(2,1)}), bf16[8,352,128]{2,1,0:T(8,128)(2,1)S(1)}, u32[]{:S(2)}, u32[]{:S(2)}) async-start(bf16[8,352,128]{2,1,0:T(8,128)(2,1)} %bitcast.15), calls=%async_computation | async-start | bytes 1441792 | tf_op jit(solution)/shard_map/all_to_all | solution.py:398
  44.8 6.1 %collective-permute-done.1.refs_2_ = bf16[16,176,128]{2,1,0:T(8,128)(2,1)S(1)} collective-permute-done((bf16[16,176,128]{2,1,0:T(8,128)(2,1)S(1)}, bf16[16,176,128]{2,1,0:T(8,128)(2,1)S(1)}, u32[]{:S(2)}, u32[]{:S(2)}) %collective-permute-start.1) | collective-permute-done | bytes 720928 | tf_op jit(solution)/shard_map/ppermute | solution.py:295
  50.8 3.5 %collective-permute-done.4.refs_3_ = bf16[16,176,128]{2,1,0:T(8,128)(2,1)} collective-permute-done((bf16[16,176,128]{2,1,0:T(8,128)(2,1)S(1)}, bf16[16,176,128]{2,1,0:T(8,128)(2,1)}, u32[]{:S(2)}, u32[]{:S(2)}) %collective-permute-start.4) | collective-permute-done | bytes 720928 | tf_op jit(solution)/shard_map/ppermute | solution.py:294
  54.4 1.3 take.5
  55.7 1.5 copy-done.4
  57.3 0.8 copy-done.6
  58.1 4.8 %all-to-all-start.1 = ((bf16[8,1408,128]{2,1,0:T(8,128)(2,1)}), bf16[8,1408,128]{2,1,0:T(8,128)(2,1)S(1)}, u32[]{:S(2)}, u32[]{:S(2)}) async-start(bf16[8,1408,128]{2,1,0:T(8,128)(2,1)} %bitcast.47), calls=%async_computation.1 | async-start | bytes 5767168 | tf_op jit(solution)/shard_map/all_to_all | solution.py:398
  63.0 0.1 copy.96
  63.1 0.7 pad_maximum_fusion.2
  64.0 3.2 %collective-permute-start.2 = (bf16[16,176,128]{2,1,0:T(8,128)(2,1)}, bf16[16,176,128]{2,1,0:T(8,128)(2,1)}, u32[]{:S(2)}, u32[]{:S(2)}) collective-permute-start(bf16[16,176,128]{2,1,0:T(8,128)(2,1)} %copy-done.10), channel_id=1, source_target_pairs={{0,224},{32,0},{64,32},{96,64},{128,96},{160,128},{192,160},{224,1... | collective-permute-start | bytes 2162696 | tf_op jit(solution)/shard_map/ppermute | solution.py:295
  67.2 0.1 copy.103
  67.4 0.1 reshape_squeeze.3
  67.5 1.3 select_reduce_fusion
  68.8 0.7 broadcast_subtract_fusion.1
  69.7 0.1 copy.105
  69.9 13.8 %collective-permute-done.5.refs_1_ = bf16[16,176,128]{2,1,0:T(8,128)(2,1)} collective-permute-done((bf16[16,176,128]{2,1,0:T(8,128)(2,1)}, bf16[16,176,128]{2,1,0:T(8,128)(2,1)}, u32[]{:S(2)}, u32[]{:S(2)}) %collective-permute-start.5) | collective-permute-done | bytes 720928 | tf_op jit(solution)/shard_map/ppermute | solution.py:294
  83.7 1.8 slice.101
  85.4 1.7 slice.102
  87.2 3.2 %collective-permute-start.7 = (bf16[8,176,128]{2,1,0:T(8,128)(2,1)}, bf16[8,176,128]{2,1,0:T(8,128)(2,1)}, u32[]{:S(2)}, u32[]{:S(2)}) collective-permute-start(bf16[8,176,128]{2,1,0:T(8,128)(2,1)} %slice.102), channel_id=1, source_target_pairs={{0,224},{32,0},{64,32},{96,64},{128,96},{160,128},{192,160},{224,1... | collective-permute-start | bytes 1081352 | tf_op jit(solution)/shard_map/ppermute | solution.py:299
  90.4 6.7 %all-to-all-done.1 = bf16[8,1408,128]{2,1,0:T(8,128)(2,1)S(1)} async-done(((bf16[8,1408,128]{2,1,0:T(8,128)(2,1)}), bf16[8,1408,128]{2,1,0:T(8,128)(2,1)S(1)}, u32[]{:S(2)}, u32[]{:S(2)}) %all-to-all-start.1) | async-done | bytes 2883616 | tf_op jit(solution)/shard_map/all_to_all | solution.py:398
  97.2 1.7 slice.106
  98.8 0.6 copy-done
  99.4 0.7 collective-permute-start.10
  100.1 0.1 copy.95.asked
  100.2 0.8 slice.103
  101.0 0.1 copy.118
  101.1 1.2 pad_maximum_fusion.1.refs_2_
  102.3 1.5 take.3
  103.8 1.3 copy-done.5
  105.2 6.6 %all-to-all-start.2 = ((bf16[8,1056,128]{2,1,0:T(8,128)(2,1)}), bf16[8,1056,128]{2,1,0:T(8,128)(2,1)S(1)}, u32[]{:S(2)}, u32[]{:S(2)}) async-start(bf16[8,1056,128]{2,1,0:T(8,128)(2,1)} %bitcast.48), calls=%async_computation.2 | async-start | bytes 4325376 | tf_op jit(solution)/shard_map/all_to_all | solution.py:398
  111.7 0.8 slice.105
  112.6 0.9 collective-permute-start.8
  113.5 24.7 %all-to-all-done.2 = bf16[8,1056,128]{2,1,0:T(8,128)(2,1)S(1)} async-done(((bf16[8,1056,128]{2,1,0:T(8,128)(2,1)}), bf16[8,1056,128]{2,1,0:T(8,128)(2,1)S(1)}, u32[]{:S(2)}, u32[]{:S(2)}) %all-to-all-start.2) | async-done | bytes 2162720 | tf_op jit(solution)/shard_map/all_to_all | solution.py:398
  138.2 1.4 slice.107
  139.6 0.9 collective-permute-start.11
  140.5 0.7 slice.85.lim
  141.2 0.6 slice.89.lim
  141.8 23.9 %attend_own.1 = (bf16[64,64,512]{2,1,0:T(8,128)(2,1)}, f32[64,128]{1,0:T(8,128)}) custom-call(s32[64,16]{1,0:T(8,128)} %get-tuple-element.50.sel, s32[64,16]{1,0:T(8,128)} %copy-done.15, s32[1]{0:T(128)} %bitcast.23.quarter, bf16[64,32,576]{2,1,0:T(8,128)(2,1)} %q_own.5, bf16[64,32,576]{2,1,0:T(8,128)(2,1)} %collective-permute-done.9.q_pair, ...), custom_call_target="tpu_custom_call" | custom-call | flops 25600000000 | bytes 12000000 | tf_op jit(solution)/shard_map/attend_own/pallas_call | solution.py:166
  165.8 1.6 copy-done.3
  167.4 7.0 %index.1 = f32[64,2048]{1,0:T(8,128)} custom-call(s32[64,16]{1,0:T(8,128)S(1)} %copy-done.11, s32[1]{0:T(128)} %bitcast.23.quarter, bf16[4,68,16,128]{3,2,1,0:T(8,128)(2,1)S(1)} %bitcast.53, f32[64,64]{1,0:T(8,128)S(1)} %bitcast.54, s32[64,512]{1,0:T(8,128)S(1)} %broadcast_subtract_fusion.lim, bf16[16,176,128]{2,1,0:T(8,128)(2,1)S(1)} %bitcast.51, ...), custom_call_target="tpu_custom_call" | custom-call | tf_op jit(solution)/shard_map/index/pallas_call | solution.py:279
  174.3 0.6 slice.84.sel
  175.0 17.1 %attend_merge.2 = (bf16[40,32,512]{2,1,0:T(8,128)(2,1)}, bf16[40,32,512]{2,1,0:T(8,128)(2,1)}, f32[40,128]{1,0:T(8,128)}) custom-call(s32[40,16]{1,0:T(8,128)} %slice.84.sel, s32[40,16]{1,0:T(8,128)} %slice.85.lim, s32[1]{0:T(128)} %bitcast.26.quarter, bf16[64,32,576]{2,1,0:T(8,128)(2,1)} %q_own.5, bf16[64,32,576]{2,1,0:T(8,128)(2,1)} %collective-permute-done.9.q_pair, ...), custom_call_target="tpu_custom_call" | custom-call | flops 16000000000 | bytes 12000000 | tf_op jit(solution)/shard_map/attend_merge/pallas_call | solution.py:166
  192.1 3.4 %collective-permute-start.13 = (bf16[40,32,512]{2,1,0:T(8,128)(2,1)}, bf16[40,32,512]{2,1,0:T(8,128)(2,1)S(1)}, u32[]{:S(2)}, u32[]{:S(2)}) collective-permute-start(bf16[40,32,512]{2,1,0:T(8,128)(2,1)} %get-tuple-element.52), channel_id=1, source_target_pairs={{0,3},{1,2},{2,1},{3,0},{4,5},{5,4},{6,7},{7,6},{8,11},{9,10},{10,... | collective-permute-start | bytes 3932168 | tf_op jit(solution)/shard_map/ppermute | solution.py:428
  195.4 1.3 reduce-scatter.2.cloned.1.call-done
  196.8 0.6 slice.88.sel
  197.4 12.5 %attend_merge.3 = (bf16[24,32,512]{2,1,0:T(8,128)(2,1)}, bf16[24,32,512]{2,1,0:T(8,128)(2,1)}, f32[24,128]{1,0:T(8,128)}) custom-call(s32[24,16]{1,0:T(8,128)} %slice.88.sel, s32[24,16]{1,0:T(8,128)} %slice.89.lim, s32[1]{0:T(128)} %bitcast.26.quarter, bf16[64,32,576]{2,1,0:T(8,128)(2,1)} %q_own.5, bf16[64,32,576]{2,1,0:T(8,128)(2,1)} %collective-permute-done.9.q_pair, ...), custom_call_target="tpu_custom_call" | custom-call | flops 9600000000 | bytes 12000000 | tf_op jit(solution)/shard_map/attend_merge/pallas_call | solution.py:166
  209.9 0.8 slice.90
  210.7 0.6 collective-permute-start.14
  211.4 2.6 %collective-permute-start.12 = (f32[64,32]{1,0:T(8,128)S(1)}, f32[64,32]{1,0:T(8,128)S(1)}, u32[]{:S(2)}, u32[]{:S(2)}) collective-permute-start(f32[64,32]{1,0:T(8,128)S(1)} %pad_maximum_fusion.3), channel_id=1, source_target_pairs={{0,3},{1,2},{2,1},{3,0},{4,5},{5,4},{6,7},{7,6},{8,11},{9,10},{10,... | collective-permute-start | bytes 24584 | tf_op jit(solution)/shard_map/ppermute | solution.py:431
  214.0 10.5 %collective-permute-done.12 = f32[64,32]{1,0:T(8,128)S(1)} collective-permute-done((f32[64,32]{1,0:T(8,128)S(1)}, f32[64,32]{1,0:T(8,128)S(1)}, u32[]{:S(2)}, u32[]{:S(2)}) %collective-permute-start.12) | collective-permute-done | bytes 8224 | tf_op jit(solution)/shard_map/ppermute | solution.py:431
  224.5 0.7 add_divide_fusion.3
  225.3 0.6 add_convert_fusion
  225.9 0.4 add_convert_fusion.1
  226.3 1.5 pad_maximum_fusion
  (83 shorter events, 1.3 us)
Async XLA Ops:
  7.2 50.1 %collective-permute-start.9 = (bf16[64,32,576]{2,1,0:T(8,128)(2,1)}, bf16[64,32,576]{2,1,0:T(8,128)(2,1)}, u32[]{:S(2)}, u32[]{:S(2)}) collective-permute-start(bf16[64,32,576]{2,1,0:T(8,128)(2,1)} %q_own.5), channel_id=1, source_target_pairs={{0,3},{1,2},{2,1},{3,0},{4,5},{5,4},{6,7},{7,6},{8,11},{9,10},{10,... | collective-permute-start | bytes 7077896 | tf_op jit(solution)/shard_map/ppermute | solution.py:344
  13.4 7.3 %copy-start.19 = (s32[1,64,2]{1,2,0:T(2,128)S(1)}, s32[1,64,2]{1,2,0:T(2,128)}, u32[]{:S(2)}) copy-start(s32[1,64,2]{1,2,0:T(2,128)} %param.12) | copy-start | bytes 1540
  14.7 19.6 %collective-permute-start = (bf16[16,176,128]{2,1,0:T(8,128)(2,1)S(1)}, bf16[16,176,128]{2,1,0:T(8,128)(2,1)S(1)}, u32[]{:S(2)}, u32[]{:S(2)}) collective-permute-start(bf16[16,176,128]{2,1,0:T(8,128)(2,1)S(1)} %bitcast_dynamic-update-slice_fusion.refs_0_), channel_id=1, source_target_pairs={{0,224},{32,0},{64,32},{96,64},{128,96},{160,128},{192,160},{224,1... | collective-permute-start | bytes 2162696 | tf_op jit(solution)/shard_map/ppermute | solution.py:295
  20.6 17.4 %collective-permute-start.3 = (bf16[16,176,128]{2,1,0:T(8,128)(2,1)S(1)}, bf16[16,176,128]{2,1,0:T(8,128)(2,1)S(1)}, u32[]{:S(2)}, u32[]{:S(2)}) collective-permute-start(bf16[16,176,128]{2,1,0:T(8,128)(2,1)S(1)} %bitcast_dynamic-update-slice_fusion.refs_0_), channel_id=1, source_target_pairs={{0,32},{32,64},{64,96},{96,128},{128,160},{160,192},{192,224},{224... | collective-permute-start | bytes 2162696 | tf_op jit(solution)/shard_map/ppermute | solution.py:294
  34.3 16.5 %collective-permute-start.1 = (bf16[16,176,128]{2,1,0:T(8,128)(2,1)S(1)}, bf16[16,176,128]{2,1,0:T(8,128)(2,1)S(1)}, u32[]{:S(2)}, u32[]{:S(2)}) collective-permute-start(bf16[16,176,128]{2,1,0:T(8,128)(2,1)S(1)} %collective-permute-done.refs_0_), channel_id=1, source_target_pairs={{0,224},{32,0},{64,32},{96,64},{128,96},{160,128},{192,160},{224,1... | collective-permute-start | bytes 2162696 | tf_op jit(solution)/shard_map/ppermute | solution.py:295
  38.0 16.4 %collective-permute-start.4 = (bf16[16,176,128]{2,1,0:T(8,128)(2,1)S(1)}, bf16[16,176,128]{2,1,0:T(8,128)(2,1)}, u32[]{:S(2)}, u32[]{:S(2)}) collective-permute-start(bf16[16,176,128]{2,1,0:T(8,128)(2,1)S(1)} %collective-permute-done.3.refs_1_), channel_id=1, source_target_pairs={{0,32},{32,64},{64,96},{96,128},{128,160},{160,192},{192,224},{224... | collective-permute-start | bytes 2162696 | tf_op jit(solution)/shard_map/ppermute | solution.py:294
  39.6 17.7 %all-to-all-start = ((bf16[8,352,128]{2,1,0:T(8,128)(2,1)}), bf16[8,352,128]{2,1,0:T(8,128)(2,1)S(1)}, u32[]{:S(2)}, u32[]{:S(2)}) async-start(bf16[8,352,128]{2,1,0:T(8,128)(2,1)} %bitcast.15), calls=%async_computation | async-start | bytes 1441792 | tf_op jit(solution)/shard_map/all_to_all | solution.py:398
  50.8 4.8 %copy-start.10 = (bf16[16,176,128]{2,1,0:T(8,128)(2,1)}, bf16[16,176,128]{2,1,0:T(8,128)(2,1)S(1)}, u32[]{:S(2)}) copy-start(bf16[16,176,128]{2,1,0:T(8,128)(2,1)S(1)} %collective-permute-done.1.refs_2_) | copy-start | bytes 2162692
  55.7 1.6 copy-start.4
  57.3 0.9 copy-start.6
  57.3 5.7 %copy-start.18 = (bf16[64,16]{0,1:T(8,128)(2,1)S(1)}, bf16[64,16]{0,1:T(8,128)(2,1)}, u32[]{:S(2)}) copy-start(bf16[64,16]{0,1:T(8,128)(2,1)} %param.10) | copy-start | bytes 6148
  57.3 5.8 %copy-start.14 = (bf16[64,16,128]{2,1,0:T(8,128)(2,1)S(1)}, bf16[64,16,128]{2,1,0:T(8,128)(2,1)}, u32[]{:S(2)}) copy-start(bf16[64,16,128]{2,1,0:T(8,128)(2,1)} %param.9) | copy-start | bytes 786436
  57.3 10.0 %copy-start.17 = (s32[64,16]{0,1:T(8,128)S(1)}, s32[64,16]{0,1:T(8,128)}, u32[]{:S(2)}) copy-start(s32[64,16]{0,1:T(8,128)} %param.13) | copy-start | bytes 12292
  58.1 39.0 %all-to-all-start.1 = ((bf16[8,1408,128]{2,1,0:T(8,128)(2,1)}), bf16[8,1408,128]{2,1,0:T(8,128)(2,1)S(1)}, u32[]{:S(2)}, u32[]{:S(2)}) async-start(bf16[8,1408,128]{2,1,0:T(8,128)(2,1)} %bitcast.47), calls=%async_computation.1 | async-start | bytes 5767168 | tf_op jit(solution)/shard_map/all_to_all | solution.py:398
  63.0 37.2 %all-gather.3.cloned.1.call-start = ((), (), s32[]{:S(2)}) async-start(), calls=%async_computation.5 | async-start | bytes 1392640 | tf_op jit(solution)/shard_map/all_gather | solution.py:347
  63.9 19.8 %collective-permute-start.5 = (bf16[16,176,128]{2,1,0:T(8,128)(2,1)}, bf16[16,176,128]{2,1,0:T(8,128)(2,1)}, u32[]{:S(2)}, u32[]{:S(2)}) collective-permute-start(bf16[16,176,128]{2,1,0:T(8,128)(2,1)} %collective-permute-done.4.refs_3_), channel_id=1, source_target_pairs={{0,32},{32,64},{64,96},{96,128},{128,160},{160,192},{192,224},{224... | collective-permute-start | bytes 2162696 | tf_op jit(solution)/shard_map/ppermute | solution.py:294
  64.0 21.5 %collective-permute-start.2 = (bf16[16,176,128]{2,1,0:T(8,128)(2,1)}, bf16[16,176,128]{2,1,0:T(8,128)(2,1)}, u32[]{:S(2)}, u32[]{:S(2)}) collective-permute-start(bf16[16,176,128]{2,1,0:T(8,128)(2,1)} %copy-done.10), channel_id=1, source_target_pairs={{0,224},{32,0},{64,32},{96,64},{128,96},{160,128},{192,160},{224,1... | collective-permute-start | bytes 2162696 | tf_op jit(solution)/shard_map/ppermute | solution.py:295
  69.6 71.6 %copy-start.15 = (s32[64,16]{1,0:T(8,128)}, s32[64,16]{1,0:T(8,128)S(1)}, u32[]{:S(2)}) copy-start(s32[64,16]{1,0:T(8,128)S(1)} %get-tuple-element.32.lim) | copy-start | bytes 12292
  85.4 15.7 %collective-permute-start.6 = (bf16[8,176,128]{2,1,0:T(8,128)(2,1)}, bf16[8,176,128]{2,1,0:T(8,128)(2,1)}, u32[]{:S(2)}, u32[]{:S(2)}) collective-permute-start(bf16[8,176,128]{2,1,0:T(8,128)(2,1)} %slice.101), channel_id=1, source_target_pairs={{0,32},{32,64},{64,96},{96,128},{128,160},{160,192},{192,224},{224... | collective-permute-start | bytes 1081352 | tf_op jit(solution)/shard_map/ppermute | solution.py:299
  87.2 13.9 %collective-permute-start.7 = (bf16[8,176,128]{2,1,0:T(8,128)(2,1)}, bf16[8,176,128]{2,1,0:T(8,128)(2,1)}, u32[]{:S(2)}, u32[]{:S(2)}) collective-permute-start(bf16[8,176,128]{2,1,0:T(8,128)(2,1)} %slice.102), channel_id=1, source_target_pairs={{0,224},{32,0},{64,32},{96,64},{128,96},{160,128},{192,160},{224,1... | collective-permute-start | bytes 1081352 | tf_op jit(solution)/shard_map/ppermute | solution.py:299
  97.1 2.3 copy-start
  99.4 41.1 %collective-permute-start.10 = (bf16[64,144,128]{2,1,0:T(8,128)(2,1)}, bf16[64,144,128]{2,1,0:T(8,128)(2,1)}, u32[]{:S(2)}, u32[]{:S(2)}) collective-permute-start(bf16[64,144,128]{2,1,0:T(8,128)(2,1)} %slice.106), channel_id=1, source_target_pairs={{0,1},{1,0},{2,3},{3,2},{4,7},{5,6},{6,5},{7,4},{8,9},{9,8},{10,11... | collective-permute-start | bytes 7077896 | tf_op jit(solution)/shard_map/ppermute | solution.py:401
  103.8 1.4 copy-start.5
  105.1 6.6 %copy-start.7 = (bf16[8,352,128]{2,1,0:T(8,128)(2,1)S(1)}, bf16[8,352,128]{2,1,0:T(8,128)(2,1)}, u32[]{:S(2)}) copy-start(bf16[8,352,128]{2,1,0:T(8,128)(2,1)} %copy-done.6) | copy-start | bytes 2162692
  105.2 33.0 %all-to-all-start.2 = ((bf16[8,1056,128]{2,1,0:T(8,128)(2,1)}), bf16[8,1056,128]{2,1,0:T(8,128)(2,1)S(1)}, u32[]{:S(2)}, u32[]{:S(2)}) async-start(bf16[8,1056,128]{2,1,0:T(8,128)(2,1)} %bitcast.48), calls=%async_computation.2 | async-start | bytes 4325376 | tf_op jit(solution)/shard_map/all_to_all | solution.py:398
  111.7 85.1 %reduce-scatter.2.cloned.1.call-start = ((), (), s32[]{:S(2)}) async-start(), calls=%async_computation.4 | async-start | bytes 655360 | tf_op jit(solution)/shard_map/reduce_scatter | solution.py:411
  112.6 27.9 %collective-permute-start.8 = (bf16[16,144,128]{2,1,0:T(8,128)(2,1)}, bf16[16,144,128]{2,1,0:T(8,128)(2,1)S(1)}, u32[]{:S(2)}, u32[]{:S(2)}) collective-permute-start(bf16[16,144,128]{2,1,0:T(8,128)(2,1)} %slice.105), channel_id=1, source_target_pairs={{0,1},{1,0},{2,3},{3,2},{4,7},{5,6},{6,5},{7,4},{8,9},{9,8},{10,11... | collective-permute-start | bytes 1769480 | tf_op jit(solution)/shard_map/ppermute | solution.py:401
  138.2 3.6 %copy-start.2 = (bf16[8,1056,128]{2,1,0:T(8,128)(2,1)}, bf16[8,1056,128]{2,1,0:T(8,128)(2,1)S(1)}, u32[]{:S(2)}) copy-start(bf16[8,1056,128]{2,1,0:T(8,128)(2,1)S(1)} %all-to-all-done.2) | copy-start | bytes 6488068
  139.6 35.4 %collective-permute-start.11 = (bf16[48,144,128]{2,1,0:T(8,128)(2,1)}, bf16[48,144,128]{2,1,0:T(8,128)(2,1)}, u32[]{:S(2)}, u32[]{:S(2)}) collective-permute-start(bf16[48,144,128]{2,1,0:T(8,128)(2,1)} %slice.107), channel_id=1, source_target_pairs={{0,1},{1,0},{2,3},{3,2},{4,7},{5,6},{6,5},{7,4},{8,9},{9,8},{10,11... | collective-permute-start | bytes 5308424 | tf_op jit(solution)/shard_map/ppermute | solution.py:401
  140.5 25.2 %copy-start.20 = (bf16[16,144,128]{2,1,0:T(8,128)(2,1)}, bf16[16,144,128]{2,1,0:T(8,128)(2,1)S(1)}, u32[]{:S(2)}) copy-start(bf16[16,144,128]{2,1,0:T(8,128)(2,1)S(1)} %collective-permute-done.8.refs_2_) | copy-start | bytes 1769476
  141.8 23.9 %copy-start.1 = (bf16[8,1408,128]{2,1,0:T(8,128)(2,1)S(1)}, bf16[8,1408,128]{2,1,0:T(8,128)(2,1)}, u32[]{:S(2)}) copy-start(bf16[8,1408,128]{2,1,0:T(8,128)(2,1)} %copy-done) | copy-start | bytes 8650756
  141.8 23.9 %copy-start.8 = (bf16[8,352,128]{2,1,0:T(8,128)(2,1)S(1)}, bf16[8,352,128]{2,1,0:T(8,128)(2,1)}, u32[]{:S(2)}) copy-start(bf16[8,352,128]{2,1,0:T(8,128)(2,1)} %copy-done.6) | copy-start | bytes 2162692
  141.8 23.9 %copy-start.9 = (bf16[272,16,128]{2,1,0:T(8,128)(2,1)S(1)}, bf16[272,16,128]{2,1,0:T(8,128)(2,1)}, u32[]{:S(2)}) copy-start(bf16[272,16,128]{2,1,0:T(8,128)(2,1)} %all-gather.3.cloned.1.call-done) | copy-start | bytes 3342340
  141.8 24.0 %copy-start.11 = (s32[64,16]{1,0:T(8,128)S(1)}, s32[64,16]{1,0:T(8,128)}, u32[]{:S(2)}) copy-start(s32[64,16]{1,0:T(8,128)} %get-tuple-element.50.sel) | copy-start | bytes 12292
  165.7 1.6 copy-start.3
  192.1 33.2 %collective-permute-start.13 = (bf16[40,32,512]{2,1,0:T(8,128)(2,1)}, bf16[40,32,512]{2,1,0:T(8,128)(2,1)S(1)}, u32[]{:S(2)}, u32[]{:S(2)}) collective-permute-start(bf16[40,32,512]{2,1,0:T(8,128)(2,1)} %get-tuple-element.52), channel_id=1, source_target_pairs={{0,3},{1,2},{2,1},{3,0},{4,5},{5,4},{6,7},{7,6},{8,11},{9,10},{10,... | collective-permute-start | bytes 3932168 | tf_op jit(solution)/shard_map/ppermute | solution.py:428
  197.4 13.3 %copy-start.16 = (f32[40,128]{1,0:T(8,128)S(1)}, f32[40,128]{1,0:T(8,128)}, u32[]{:S(2)}) copy-start(f32[40,128]{1,0:T(8,128)} %get-tuple-element.49) | copy-start | bytes 61444
  197.4 27.9 %copy-start.12 = (bf16[40,32,512]{2,1,0:T(8,128)(2,1)S(1)}, bf16[40,32,512]{2,1,0:T(8,128)(2,1)}, u32[]{:S(2)}) copy-start(bf16[40,32,512]{2,1,0:T(8,128)(2,1)} %get-tuple-element.46) | copy-start | bytes 3932164
  210.7 15.2 %copy-start.13 = (bf16[24,32,512]{2,1,0:T(8,128)(2,1)S(1)}, bf16[24,32,512]{2,1,0:T(8,128)(2,1)}, u32[]{:S(2)}) copy-start(bf16[24,32,512]{2,1,0:T(8,128)(2,1)} %get-tuple-element.53) | copy-start | bytes 2359300
  210.7 15.2 %collective-permute-start.14 = (bf16[24,32,512]{2,1,0:T(8,128)(2,1)}, bf16[24,32,512]{2,1,0:T(8,128)(2,1)S(1)}, u32[]{:S(2)}, u32[]{:S(2)}) collective-permute-start(bf16[24,32,512]{2,1,0:T(8,128)(2,1)} %get-tuple-element.54), channel_id=1, source_target_pairs={{0,3},{1,2},{2,1},{3,0},{4,5},{5,4},{6,7},{7,6},{8,11},{9,10},{10,... | collective-permute-start | bytes 2359304 | tf_op jit(solution)/shard_map/ppermute | solution.py:428
  211.4 13.1 %collective-permute-start.12 = (f32[64,32]{1,0:T(8,128)S(1)}, f32[64,32]{1,0:T(8,128)S(1)}, u32[]{:S(2)}, u32[]{:S(2)}) collective-permute-start(f32[64,32]{1,0:T(8,128)S(1)} %pad_maximum_fusion.3), channel_id=1, source_target_pairs={{0,3},{1,2},{2,1},{3,0},{4,5},{5,4},{6,7},{7,6},{8,11},{9,10},{10,... | collective-permute-start | bytes 24584 | tf_op jit(solution)/shard_map/ppermute | solution.py:431
Sparse Core Ops, SparseCore 0:
  65.6 26.2 all-gather.2
  175.1 21.6 reduce-scatter.1

commit v5 on v4

--- a/solution.py
+++ b/solution.py
@@ -25,7 +25,7 @@
     return latent, latent + part // 2, latent + part // 2 + part
 
 
-def attend_kernel(sel, lim, quarter, q_own, q_pair, *refs, merge, fetched_count):
+def attend_kernel(sel, lim, quarter, q_own, q_pair, *refs, merge, fetched_count, first_query):
     refs = list(refs)
     earlier, earlier_lse = (refs.pop(0), refs.pop(0)) if merge else (None, None)
     fetched, outs, (rows, sems) = refs[:fetched_count], refs[fetched_count:-2], refs[-2:]
@@ -65,7 +65,7 @@
         )
 
     def scores_of(i):
-        query = step * GROUP + i
+        query = first_query + step * GROUP + i
         here = jnp.concatenate([q_own[i], q_pair[i]], axis=0)
         value, rotary = here[:, :KEY_VALUE_RANK], here[:, KEY_VALUE_RANK:]
         no_value, no_rotary = jnp.zeros_like(value), jnp.zeros_like(rotary)
@@ -124,7 +124,7 @@
             lse[pl.ds(i, 1), :] = level
             probs.append(jnp.transpose(p.astype(jnp.bfloat16)))
         for j, (i, p) in enumerate(zip(batch, probs)):
-            query = step * GROUP + i
+            query = first_query + step * GROUP + i
             summed = earlier[i].astype(jnp.float32) * kept[j] if merge else 0.0
             for upper in range(2):
                 values = jnp.concatenate([half_rows(sel[query, k], upper) for k in range(picks)], axis=0)
@@ -164,7 +164,7 @@
         ],
     )
     return pl.pallas_call(
-        functools.partial(attend_kernel, merge=merge, fetched_count=len(fetched)),
+        functools.partial(attend_kernel, merge=merge, fetched_count=len(fetched), first_query=first),
         grid_spec=spec,
         out_shape=[jax.ShapeDtypeStruct((count, n, KEY_VALUE_RANK), jnp.bfloat16) for n in heads_out]
         + [jax.ShapeDtypeStruct((count, LANES), jnp.float32)],
@@ -174,8 +174,8 @@
         ),
         name="attend_merge" if merge else "attend_own",
     )(
-        sel[first : first + count],
-        lim[first : first + count],
+        sel,
+        lim,
         quarter,
         q_own,
         q_pair,
@@ -184,20 +184,32 @@
     )
 
 
-def take_kernel(asked, *refs):
+def take_kernel(asked, *refs, halves):
     blocks, found = refs[:-1], refs[-1]
+    whole = blocks[: len(blocks) - 2 * halves]
     for to in range(found.shape[0]):
-        for p, block in enumerate(blocks):
+        for p in range(len(whole) + halves):
             for slot in range(CAP):
-                found[to, p * CAP + slot] = block[asked[p, to, slot]]
+                at, tile = p * CAP + slot, asked[p, to, slot]
+                if p < len(whole):
+                    found[to, at] = whole[p][tile]
+                else:
+                    low, high = blocks[-2:]
+                    count = low.shape[0]
+                    found[to, at] = jnp.where(
+                        tile < count, low[jnp.minimum(tile, count - 1)], high[jnp.maximum(tile - count, 0)]
+                    )
 
 
 def take(asked, blocks):
     count, plane, _ = asked.shape
+    halves = isinstance(blocks[-1], tuple)
+    if halves:
+        blocks = [*blocks[:-1], *blocks[-1]]
     tile = blocks[0].shape[1:]
     return pl.pallas_call(
-        take_kernel,
-        in_specs=[pl.BlockSpec(memory_space=pltpu.SMEM)] + [pl.BlockSpec(memory_space=pltpu.VMEM)] * count,
+        functools.partial(take_kernel, halves=halves),
+        in_specs=[pl.BlockSpec(memory_space=pltpu.SMEM)] + [pl.BlockSpec(memory_space=pltpu.VMEM)] * len(blocks),
         out_specs=pl.BlockSpec(memory_space=pltpu.VMEM),
         out_shape=jax.ShapeDtypeStruct((plane, count * CAP) + tile, blocks[0].dtype),
         compiler_params=pltpu.CompilerParams(vmem_limit_bytes=16 * 1024 * 1024),
@@ -295,9 +307,7 @@
         down = lax.ppermute(down, axis, backward)
         got[size - d], got[d] = up, down
     half = block.shape[0] // 2
-    got[size // 2] = jnp.concatenate(
-        [lax.ppermute(up[:half], axis, forward), lax.ppermute(down[half:], axis, backward)]
-    )
+    got[size // 2] = lax.ppermute(up[:half], axis, forward), lax.ppermute(down[half:], axis, backward)
     return got
 
 
@@ -327,7 +337,7 @@
     tile_count = latent.shape[0] // TILE
     part = TILE // y_count
     picks = selection.shape[1]
-    _, packed, lines = lines_of(part)
+    lines = lines_of(part)[2]
     row_pairs, head_pairs = pairings()
 
     def quarter(a):
@@ -345,10 +355,6 @@
     weight_rows = jnp.pad(index_weights, ((0, 0), (0, LANES - index_heads)))
     joined = jnp.concatenate([index_queries, weight_rows.reshape(-1, index_heads, LANES)], axis=0)
     joined = lax.all_gather(joined, "y")
-    weights = joined[:, query_count:].reshape(y_count, query_count, LANES)[:, :, :index_heads]
-    key_scale = index_keys.shape[1] ** -0.5
-    weight_t = jnp.transpose(weights.astype(jnp.float32), (0, 2, 1)).reshape(-1, query_count) * key_scale
-
     wanted = request_tiles[0]
     plans = lax.all_gather(wanted, ("x", "c")).reshape(plane, z_count, plane, CAP)
     plans = lax.dynamic_index_in_dim(plans, here, 2, False)
@@ -392,24 +398,29 @@
         if r == 1:
             found, q_pair, own_fetched[0] = lax.optimization_barrier((found, q_pair, own_fetched[0]))
         if r == 2:
-            found, joined, weight_t, own_lim, lim, rows_at = lax.optimization_barrier(
-                (found, joined, weight_t, own_lim, lim, rows_at)
+            found, own_fetched[1], joined, own_lim, lim, rows_at = lax.optimization_barrier(
+                (found, own_fetched[1], joined, own_lim, lim, rows_at)
             )
+            pair_fetched.append(lax.ppermute(own_fetched[1], ("c", "y"), row_pairs))
+            weights = joined[:, query_count:].reshape(y_count, query_count, LANES)[:, :, :index_heads]
+            key_scale = index_keys.shape[1] ** -0.5
+            weight_t = jnp.transpose(weights.astype(jnp.float32), (0, 2, 1)).reshape(-1, query_count) * key_scale
         moved = lax.all_to_all(found.reshape(plane, -1, LANES), ("x", "c"), split_axis=0, concat_axis=0, tiled=True)
         moved = moved.reshape(-1, lines, LANES)
         own_fetched.append(moved)
-        pair_fetched.append(lax.ppermute(moved[:, :packed], ("c", "y"), row_pairs))
-
-    lim, *pair_fetched[:2] = lax.optimization_barrier((lim, *pair_fetched[:2]))
+        if r != 1:
+            pair_fetched.append(lax.ppermute(moved, ("c", "y"), row_pairs))
+
+    lim, weight_t, pair_fetched[1] = lax.optimization_barrier((lim, weight_t, pair_fetched[1]))
     quarter_here = jnp.reshape(y, (1,)).astype(jnp.int32)
     earlier = list(
         attend(rows_at, lim, quarter_here, queries, q_pair, own_fetched, 0, query_count)
     )
-    rows_at, earlier[0] = lax.optimization_barrier((rows_at, earlier[0]))
+    rows_at, earlier[0], pair_fetched[0] = lax.optimization_barrier((rows_at, earlier[0], pair_fetched[0]))
     index_part = index(rows_at, quarter_here, joined, weight_t, own_lim, own_fetched)
     rows_at, index_part = lax.optimization_barrier((rows_at, index_part))
     index_scores = lax.psum_scatter(index_part, "y", scatter_dimension=1, tiled=True)
-    split = query_count * 5 // 8
+    split = query_count * 3 // 4
     halves = []
     for first_query, count in ((0, split), (split, query_count - split)):
         mine, other, lse = attend(

time: 236 us -> 231 us (0.979)
  local copies, waits for them, and re-layouts: 23.3 us -> 16.6 us
  Pallas kernels: 64.8 us -> 68.6 us
  waiting for transfers between devices: 71.6 us -> 68.6 us
    all_to_all x3, waiting for transfers between devices: 31.4 us -> 24.7 us  [shards(): lax.all_to_all(found.reshape(plane, -1, LANES), ('x', 'c'), split_axis=0,...]
    slice x7 -> x0, local copies, waits for them, and re-layouts: 6.41 us -> none  [the longest x3 3.94 us: shards(): pair_fetched.append(lax.ppermute(moved[:, :packed], ('c', 'y'), row_pairs))]
    ppermute x1, waiting for transfers between devices: 0.01 us -> 3.37 us  [ring_blocks(): lax.ppermute(up[:half], axis, forward)]
    ppermute x1, waiting for transfers between devices: 10.5 us -> 7.99 us  [shards(): all_lse = lax.ppermute(all_lse, ('c', 'y'), head_pairs)]
    unnamed x51 -> x37, local copies, waits for them, and re-layouts: 9.59 us -> 7.55 us
  transfers between devices with their start and end apart: 20 -> 20, of which waited for: 8 -> 10; matrix products, arithmetic and copies ran while one was open for 10% -> 8% of each run, Pallas kernels for 28% -> 30%
where the time goes in v5:
time: 231 us; the launch traced here: 229 us
  waiting for transfers between devices  68.6 us (30%)
  Pallas kernels  68.6 us (30%)
  starting transfers between devices  44.8 us (19%)
  local copies, waits for them, and re-layouts  16.6 us (7%)
  between operations  14.4 us (6%)
  blocking collectives  8.67 us (4%)
  other arithmetic  7.23 us (3%)
    pallas_call x3, Pallas kernels, attend(): pl.pallas_call(functools.partial(attend_kernel, merge=merge, fetched_coun...  54.5 us
    all_to_all x3, waiting for transfers between devices, shards(): lax.all_to_all(found.reshape(plane, -1, LANES), ('x', 'c'), split_axis=0,...  24.7 us
    ppermute x3, waiting for transfers between devices, ring_blocks(): up = lax.ppermute(up, axis, forward)  18.3 us
    all_to_all x3, starting transfers between devices, shards(): lax.all_to_all(found.reshape(plane, -1, LANES), ('x', 'c'), split_axis=0,...  15.5 us
    ppermute x3, starting transfers between devices, ring_blocks(): down = lax.ppermute(down, axis, backward)  12.8 us
    ppermute x3, waiting for transfers between devices, ring_blocks(): down = lax.ppermute(down, axis, backward)  11 us
    all_gather x1, blocking collectives, shards(): lax.all_gather(wanted, ('x', 'c')).reshape(plane, z_count, plane, CAP)  8.67 us
    ppermute x1, waiting for transfers between devices, shards(): all_lse = lax.ppermute(all_lse, ('c', 'y'), head_pairs)  7.99 us
  transfers between devices with their start and end apart: 20, of which 10 were waited for; matrix products, arithmetic and copies ran while one was open for 8% of the time, Pallas kernels for 30%

profile of v5, /device:TPU:2, one launch (start us, length us, event | category | flops | bytes accessed | tf_op | source)
XLA Modules:
  0.0 228.8 jit_solution(4470273607622608516)
XLA Ops:
  7.2 3.1 %collective-permute-start.8 = (bf16[64,32,576]{2,1,0:T(8,128)(2,1)}, bf16[64,32,576]{2,1,0:T(8,128)(2,1)}, u32[]{:S(2)}, u32[]{:S(2)}) collective-permute-start(bf16[64,32,576]{2,1,0:T(8,128)(2,1)} %q_own.5), channel_id=1, source_target_pairs={{0,3},{1,2},{2,1},{3,0},{4,5},{5,4},{6,7},{7,6},{8,11},{9,10},{10,... | collective-permute-start | bytes 7077896 | tf_op jit(solution)/shard_map/ppermute | solution.py:354
  10.3 3.1 %copy.93 = bf16[2048,576]{1,0:T(8,128)(2,1)S(1)} copy(bf16[2048,576]{0,1:T(8,128)(2,1)} %param.8) | data formatting | bytes 4718592 | tf_op args[1]
  13.6 0.1 maximum_dynamic-update-slice_fusion
  13.7 0.9 bitcast_dynamic-update-slice_fusion.refs_0_
  14.7 5.9 %collective-permute-start = (bf16[16,176,128]{2,1,0:T(8,128)(2,1)S(1)}, bf16[16,176,128]{2,1,0:T(8,128)(2,1)S(1)}, u32[]{:S(2)}, u32[]{:S(2)}) collective-permute-start(bf16[16,176,128]{2,1,0:T(8,128)(2,1)S(1)} %bitcast_dynamic-update-slice_fusion.refs_0_), channel_id=1, source_target_pairs={{0,224},{32,0},{64,32},{96,64},{128,96},{160,128},{192,160},{224,1... | collective-permute-start | bytes 2162696 | tf_op jit(solution)/shard_map/ppermute | solution.py:307
  20.6 8.7 %all_gather.9 = s32[8,64,2]{1,2,0:T(2,128)S(1)} all-gather(s32[1,64,2]{1,2,0:T(2,128)S(1)} %copy-done.13), channel_id=1, replica_groups=mesh['z'=8,'x'=4,'c'=2,'y'=4] {'x','c'}, dimensions={0}, use_global_device_ids=true | all-gather | bytes 4608 | tf_op jit(solution)/shard_map/all_gather | solution.py:359
  29.3 0.1 copy.116
  29.4 4.9 %collective-permute-done.refs_0_ = bf16[16,176,128]{2,1,0:T(8,128)(2,1)S(1)} collective-permute-done((bf16[16,176,128]{2,1,0:T(8,128)(2,1)S(1)}, bf16[16,176,128]{2,1,0:T(8,128)(2,1)S(1)}, u32[]{:S(2)}, u32[]{:S(2)}) %collective-permute-start) | collective-permute-done | bytes 720928 | tf_op jit(solution)/shard_map/ppermute | solution.py:307
  34.3 3.7 %collective-permute-start.1 = (bf16[16,176,128]{2,1,0:T(8,128)(2,1)S(1)}, bf16[16,176,128]{2,1,0:T(8,128)(2,1)S(1)}, u32[]{:S(2)}, u32[]{:S(2)}) collective-permute-start(bf16[16,176,128]{2,1,0:T(8,128)(2,1)S(1)} %collective-permute-done.refs_0_), channel_id=1, source_target_pairs={{0,224},{32,0},{64,32},{96,64},{128,96},{160,128},{192,160},{224,1... | collective-permute-start | bytes 2162696 | tf_op jit(solution)/shard_map/ppermute | solution.py:307
  38.0 0.1 copy.105.asked
  38.1 1.5 take.5
  39.6 4.8 %all-to-all-start = ((bf16[8,352,128]{2,1,0:T(8,128)(2,1)}), bf16[8,352,128]{2,1,0:T(8,128)(2,1)S(1)}, u32[]{:S(2)}, u32[]{:S(2)}) async-start(bf16[8,352,128]{2,1,0:T(8,128)(2,1)} %bitcast.13), calls=%async_computation | async-start | bytes 1441792 | tf_op jit(solution)/shard_map/all_to_all | solution.py:408
  44.4 0.1 copy.100
  44.5 0.1 copy.101
  44.6 0.1 copy.102
  44.7 0.1 copy.103
  44.8 6.1 %collective-permute-done.1.refs_2_ = bf16[16,176,128]{2,1,0:T(8,128)(2,1)S(1)} collective-permute-done((bf16[16,176,128]{2,1,0:T(8,128)(2,1)S(1)}, bf16[16,176,128]{2,1,0:T(8,128)(2,1)S(1)}, u32[]{:S(2)}, u32[]{:S(2)}) %collective-permute-start.1) | collective-permute-done | bytes 720928 | tf_op jit(solution)/shard_map/ppermute | solution.py:307
  50.8 3.5 %collective-permute-done.4.refs_3_ = bf16[16,176,128]{2,1,0:T(8,128)(2,1)} collective-permute-done((bf16[16,176,128]{2,1,0:T(8,128)(2,1)S(1)}, bf16[16,176,128]{2,1,0:T(8,128)(2,1)}, u32[]{:S(2)}, u32[]{:S(2)}) %collective-permute-start.4) | collective-permute-done | bytes 720928 | tf_op jit(solution)/shard_map/ppermute | solution.py:306
  54.4 2.9 %take.4 = bf16[8,8,176,128]{3,2,1,0:T(8,128)(2,1)} custom-call(s32[4,8,2]{2,1,0:T(8,128)S(1)} %pad_add_fusion.asked, bf16[16,176,128]{2,1,0:T(8,128)(2,1)S(1)} %collective-permute-done.refs_0_, bf16[16,176,128]{2,1,0:T(8,128)(2,1)S(1)} %collective-permute-done.3.refs_1_, bf16[16,176,128]{2,1,0:T(8,128)(2,1)S(1)} %collective-permute-done.1.refs_2_, ...), custom_call_target="tpu_custom_call" | custom-call | bytes 6000000 | tf_op jit(solution)/shard_map/take/pallas_call | solution.py:210
  57.3 0.8 copy-done.3
  58.1 4.8 %all-to-all-start.1 = ((bf16[8,1408,128]{2,1,0:T(8,128)(2,1)}), bf16[8,1408,128]{2,1,0:T(8,128)(2,1)S(1)}, u32[]{:S(2)}, u32[]{:S(2)}) async-start(bf16[8,1408,128]{2,1,0:T(8,128)(2,1)} %bitcast.15), calls=%async_computation.1 | async-start | bytes 5767168 | tf_op jit(solution)/shard_map/all_to_all | solution.py:408
  62.9 0.1 copy.106
  63.1 0.8 pad_maximum_fusion.1
  63.8 0.1 collective-permute-start.5
  63.9 3.2 %collective-permute-start.2 = (bf16[16,176,128]{2,1,0:T(8,128)(2,1)}, bf16[16,176,128]{2,1,0:T(8,128)(2,1)}, u32[]{:S(2)}, u32[]{:S(2)}) collective-permute-start(bf16[16,176,128]{2,1,0:T(8,128)(2,1)} %copy-done.6), channel_id=1, source_target_pairs={{0,224},{32,0},{64,32},{96,64},{128,96},{160,128},{192,160},{224,1... | collective-permute-start | bytes 2162696 | tf_op jit(solution)/shard_map/ppermute | solution.py:307
  67.2 0.1 copy.112
  67.3 0.1 copy.95.asked
  67.4 0.1 copy.107
  67.4 0.1 reshape_squeeze.3
  67.6 1.3 select_reduce_fusion
  68.9 14.7 %collective-permute-done.5.refs_1_ = bf16[16,176,128]{2,1,0:T(8,128)(2,1)} collective-permute-done((bf16[16,176,128]{2,1,0:T(8,128)(2,1)}, bf16[16,176,128]{2,1,0:T(8,128)(2,1)}, u32[]{:S(2)}, u32[]{:S(2)}) %collective-permute-start.5) | collective-permute-done | bytes 720928 | tf_op jit(solution)/shard_map/ppermute | solution.py:306
  83.6 1.8 slice.73
  85.4 1.8 slice.74
  87.2 3.2 %collective-permute-start.7 = (bf16[8,176,128]{2,1,0:T(8,128)(2,1)}, bf16[8,176,128]{2,1,0:T(8,128)(2,1)}, u32[]{:S(2)}, u32[]{:S(2)}) collective-permute-start(bf16[8,176,128]{2,1,0:T(8,128)(2,1)} %slice.74), channel_id=1, source_target_pairs={{0,224},{32,0},{64,32},{96,64},{128,96},{160,128},{192,160},{224,1... | collective-permute-start | bytes 1081352 | tf_op jit(solution)/shard_map/ppermute | solution.py:310
  90.4 0.7 broadcast_subtract_fusion.1
  91.2 0.7 sub.70
  91.9 1.1 copy.114
  93.1 3.4 %collective-permute-done.6.refs_2_ = bf16[8,176,128]{2,1,0:T(8,128)(2,1)S(1)} collective-permute-done((bf16[8,176,128]{2,1,0:T(8,128)(2,1)}, bf16[8,176,128]{2,1,0:T(8,128)(2,1)S(1)}, u32[]{:S(2)}, u32[]{:S(2)}) %collective-permute-start.6) | collective-permute-done | bytes 360480 | tf_op jit(solution)/shard_map/ppermute | solution.py:310
  96.5 1.1 collective-permute-done.7.refs_3_
  97.6 1.7 take.3
  99.3 1.3 copy-done.2
  100.6 0.6 collective-permute-start.9
  101.3 5.8 %all-to-all-start.2 = ((bf16[8,1056,128]{2,1,0:T(8,128)(2,1)}), bf16[8,1056,128]{2,1,0:T(8,128)(2,1)}, u32[]{:S(2)}, u32[]{:S(2)}) async-start(bf16[8,1056,128]{2,1,0:T(8,128)(2,1)} %bitcast.44), calls=%async_computation.2 | async-start | bytes 4325376 | tf_op jit(solution)/shard_map/all_to_all | solution.py:408
  107.1 0.9 collective-permute-start.10
  108.0 0.8 slice.59
  108.9 0.1 copy.118
  109.0 24.7 %all-to-all-done.2 = bf16[8,1056,128]{2,1,0:T(8,128)(2,1)} async-done(((bf16[8,1056,128]{2,1,0:T(8,128)(2,1)}), bf16[8,1056,128]{2,1,0:T(8,128)(2,1)}, u32[]{:S(2)}, u32[]{:S(2)}) %all-to-all-start.2) | async-done | bytes 2162720 | tf_op jit(solution)/shard_map/all_to_all | solution.py:408
  133.7 0.9 collective-permute-start.11
  134.6 0.6 collective-permute-done.9.refs_3_
  135.2 23.9 %attend_own.1 = (bf16[64,64,512]{2,1,0:T(8,128)(2,1)}, f32[64,128]{1,0:T(8,128)}) custom-call(s32[64,16]{1,0:T(8,128)} %get-tuple-element.52.sel, s32[64,16]{1,0:T(8,128)} %get-tuple-element.35.lim, s32[1]{0:T(128)} %bitcast.23.quarter, bf16[64,32,576]{2,1,0:T(8,128)(2,1)} %q_own.5, bf16[64,32,576]{2,1,0:T(8,128)(2,1)} %collective-permute-done.8.q_pair, ...), custom_call_target="tpu_custom_call" | custom-call | flops 25600000000 | bytes 12000000 | tf_op jit(solution)/shard_map/attend_own/pallas_call | solution.py:166
  159.1 1.8 copy-done.1
  161.0 7.9 %index.1 = f32[64,2048]{1,0:T(8,128)} custom-call(s32[64,16]{1,0:T(8,128)S(1)} %copy-done.7, s32[1]{0:T(128)} %bitcast.23.quarter, bf16[4,68,16,128]{3,2,1,0:T(8,128)(2,1)S(1)} %bitcast.49, f32[64,64]{1,0:T(8,128)S(1)} %bitcast.50, s32[64,512]{1,0:T(8,128)S(1)} %broadcast_subtract_fusion.lim, bf16[16,176,128]{2,1,0:T(8,128)(2,1)S(1)} %bitcast.47, ...), custom_call_target="tpu_custom_call" | custom-call | tf_op jit(solution)/shard_map/index/pallas_call | solution.py:291
  168.9 19.8 %attend_merge.2 = (bf16[48,32,512]{2,1,0:T(8,128)(2,1)}, bf16[48,32,512]{2,1,0:T(8,128)(2,1)}, f32[48,128]{1,0:T(8,128)}) custom-call(s32[64,16]{1,0:T(8,128)} %get-tuple-element.52.sel, s32[64,16]{1,0:T(8,128)} %get-tuple-element.35.lim, s32[1]{0:T(128)} %bitcast.26.quarter, bf16[64,32,576]{2,1,0:T(8,128)(2,1)} %q_own.5, ...), custom_call_target="tpu_custom_call" | custom-call | flops 19200000000 | bytes 12000000 | tf_op jit(solution)/shard_map/attend_merge/pallas_call | solution.py:166
  188.7 4.3 %collective-permute-start.13 = (bf16[48,32,512]{2,1,0:T(8,128)(2,1)}, bf16[48,32,512]{2,1,0:T(8,128)(2,1)S(1)}, u32[]{:S(2)}, u32[]{:S(2)}) collective-permute-start(bf16[48,32,512]{2,1,0:T(8,128)(2,1)} %get-tuple-element.54), channel_id=1, source_target_pairs={{0,3},{1,2},{2,1},{3,0},{4,5},{5,4},{6,7},{7,6},{8,11},{9,10},{10,... | collective-permute-start | bytes 4718600 | tf_op jit(solution)/shard_map/ppermute | solution.py:439
  193.0 1.5 reduce-scatter.2.cloned.1.call-done
  194.5 10.9 %attend_merge.3 = (bf16[16,32,512]{2,1,0:T(8,128)(2,1)}, bf16[16,32,512]{2,1,0:T(8,128)(2,1)}, f32[16,128]{1,0:T(8,128)}) custom-call(s32[64,16]{1,0:T(8,128)} %get-tuple-element.52.sel, s32[64,16]{1,0:T(8,128)} %get-tuple-element.35.lim, s32[1]{0:T(128)} %bitcast.26.quarter, bf16[64,32,576]{2,1,0:T(8,128)(2,1)} %q_own.5, ...), custom_call_target="tpu_custom_call" | custom-call | flops 6400000000 | bytes 12000000 | tf_op jit(solution)/shard_map/attend_merge/pallas_call | solution.py:166
  205.4 0.9 slice.62
  206.4 0.6 collective-permute-start.14
  207.0 2.6 %collective-permute-start.12 = (f32[64,32]{1,0:T(8,128)S(1)}, f32[64,32]{1,0:T(8,128)S(1)}, u32[]{:S(2)}, u32[]{:S(2)}) collective-permute-start(f32[64,32]{1,0:T(8,128)S(1)} %pad_maximum_fusion.2), channel_id=1, source_target_pairs={{0,3},{1,2},{2,1},{3,0},{4,5},{5,4},{6,7},{7,6},{8,11},{9,10},{10,... | collective-permute-start | bytes 24584 | tf_op jit(solution)/shard_map/ppermute | solution.py:442
  209.6 8.0 %collective-permute-done.12 = f32[64,32]{1,0:T(8,128)S(1)} collective-permute-done((f32[64,32]{1,0:T(8,128)S(1)}, f32[64,32]{1,0:T(8,128)S(1)}, u32[]{:S(2)}, u32[]{:S(2)}) %collective-permute-start.12) | collective-permute-done | bytes 8224 | tf_op jit(solution)/shard_map/ppermute | solution.py:442
  217.6 0.7 add_divide_fusion.3
  218.4 1.3 add_convert_fusion.1
  219.7 0.7 add_convert_fusion
  220.4 1.5 pad_maximum_fusion
  (61 shorter events, 0.7 us)
Async XLA Ops:
  7.2 50.1 %collective-permute-start.8 = (bf16[64,32,576]{2,1,0:T(8,128)(2,1)}, bf16[64,32,576]{2,1,0:T(8,128)(2,1)}, u32[]{:S(2)}, u32[]{:S(2)}) collective-permute-start(bf16[64,32,576]{2,1,0:T(8,128)(2,1)} %q_own.5), channel_id=1, source_target_pairs={{0,3},{1,2},{2,1},{3,0},{4,5},{5,4},{6,7},{7,6},{8,11},{9,10},{10,... | collective-permute-start | bytes 7077896 | tf_op jit(solution)/shard_map/ppermute | solution.py:354
  13.4 7.3 %copy-start.13 = (s32[1,64,2]{1,2,0:T(2,128)S(1)}, s32[1,64,2]{1,2,0:T(2,128)}, u32[]{:S(2)}) copy-start(s32[1,64,2]{1,2,0:T(2,128)} %param.12) | copy-start | bytes 1540
  14.7 19.6 %collective-permute-start = (bf16[16,176,128]{2,1,0:T(8,128)(2,1)S(1)}, bf16[16,176,128]{2,1,0:T(8,128)(2,1)S(1)}, u32[]{:S(2)}, u32[]{:S(2)}) collective-permute-start(bf16[16,176,128]{2,1,0:T(8,128)(2,1)S(1)} %bitcast_dynamic-update-slice_fusion.refs_0_), channel_id=1, source_target_pairs={{0,224},{32,0},{64,32},{96,64},{128,96},{160,128},{192,160},{224,1... | collective-permute-start | bytes 2162696 | tf_op jit(solution)/shard_map/ppermute | solution.py:307
  20.6 17.4 %collective-permute-start.3 = (bf16[16,176,128]{2,1,0:T(8,128)(2,1)S(1)}, bf16[16,176,128]{2,1,0:T(8,128)(2,1)S(1)}, u32[]{:S(2)}, u32[]{:S(2)}) collective-permute-start(bf16[16,176,128]{2,1,0:T(8,128)(2,1)S(1)} %bitcast_dynamic-update-slice_fusion.refs_0_), channel_id=1, source_target_pairs={{0,32},{32,64},{64,96},{96,128},{128,160},{160,192},{192,224},{224... | collective-permute-start | bytes 2162696 | tf_op jit(solution)/shard_map/ppermute | solution.py:306
  34.3 16.5 %collective-permute-start.1 = (bf16[16,176,128]{2,1,0:T(8,128)(2,1)S(1)}, bf16[16,176,128]{2,1,0:T(8,128)(2,1)S(1)}, u32[]{:S(2)}, u32[]{:S(2)}) collective-permute-start(bf16[16,176,128]{2,1,0:T(8,128)(2,1)S(1)} %collective-permute-done.refs_0_), channel_id=1, source_target_pairs={{0,224},{32,0},{64,32},{96,64},{128,96},{160,128},{192,160},{224,1... | collective-permute-start | bytes 2162696 | tf_op jit(solution)/shard_map/ppermute | solution.py:307
  38.0 16.4 %collective-permute-start.4 = (bf16[16,176,128]{2,1,0:T(8,128)(2,1)S(1)}, bf16[16,176,128]{2,1,0:T(8,128)(2,1)}, u32[]{:S(2)}, u32[]{:S(2)}) collective-permute-start(bf16[16,176,128]{2,1,0:T(8,128)(2,1)S(1)} %collective-permute-done.3.refs_1_), channel_id=1, source_target_pairs={{0,32},{32,64},{64,96},{96,128},{128,160},{160,192},{192,224},{224... | collective-permute-start | bytes 2162696 | tf_op jit(solution)/shard_map/ppermute | solution.py:306
  39.6 17.6 %all-to-all-start = ((bf16[8,352,128]{2,1,0:T(8,128)(2,1)}), bf16[8,352,128]{2,1,0:T(8,128)(2,1)S(1)}, u32[]{:S(2)}, u32[]{:S(2)}) async-start(bf16[8,352,128]{2,1,0:T(8,128)(2,1)} %bitcast.13), calls=%async_computation | async-start | bytes 1441792 | tf_op jit(solution)/shard_map/all_to_all | solution.py:408
  50.8 6.4 %copy-start.6 = (bf16[16,176,128]{2,1,0:T(8,128)(2,1)}, bf16[16,176,128]{2,1,0:T(8,128)(2,1)S(1)}, u32[]{:S(2)}) copy-start(bf16[16,176,128]{2,1,0:T(8,128)(2,1)S(1)} %collective-permute-done.1.refs_2_) | copy-start | bytes 2162692
  57.2 0.9 copy-start.3
  57.3 5.7 %copy-start.12 = (bf16[64,16]{0,1:T(8,128)(2,1)S(1)}, bf16[64,16]{0,1:T(8,128)(2,1)}, u32[]{:S(2)}) copy-start(bf16[64,16]{0,1:T(8,128)(2,1)} %param.10) | copy-start | bytes 6148
  57.3 5.8 %copy-start.9 = (bf16[64,16,128]{2,1,0:T(8,128)(2,1)S(1)}, bf16[64,16,128]{2,1,0:T(8,128)(2,1)}, u32[]{:S(2)}) copy-start(bf16[64,16,128]{2,1,0:T(8,128)(2,1)} %param.9) | copy-start | bytes 786436
  57.3 10.1 %copy-start.11 = (s32[64,16]{0,1:T(8,128)S(1)}, s32[64,16]{0,1:T(8,128)}, u32[]{:S(2)}) copy-start(s32[64,16]{0,1:T(8,128)} %param.13) | copy-start | bytes 12292
  58.1 42.6 %all-to-all-start.1 = ((bf16[8,1408,128]{2,1,0:T(8,128)(2,1)}), bf16[8,1408,128]{2,1,0:T(8,128)(2,1)S(1)}, u32[]{:S(2)}, u32[]{:S(2)}) async-start(bf16[8,1408,128]{2,1,0:T(8,128)(2,1)} %bitcast.15), calls=%async_computation.1 | async-start | bytes 5767168 | tf_op jit(solution)/shard_map/all_to_all | solution.py:408
  62.9 37.7 %all-gather.3.cloned.1.call-start = ((), (), s32[]{:S(2)}) async-start(), calls=%async_computation.5 | async-start | bytes 1392640 | tf_op jit(solution)/shard_map/all_gather | solution.py:357
  63.8 19.8 %collective-permute-start.5 = (bf16[16,176,128]{2,1,0:T(8,128)(2,1)}, bf16[16,176,128]{2,1,0:T(8,128)(2,1)}, u32[]{:S(2)}, u32[]{:S(2)}) collective-permute-start(bf16[16,176,128]{2,1,0:T(8,128)(2,1)} %collective-permute-done.4.refs_3_), channel_id=1, source_target_pairs={{0,32},{32,64},{64,96},{96,128},{128,160},{160,192},{192,224},{224... | collective-permute-start | bytes 2162696 | tf_op jit(solution)/shard_map/ppermute | solution.py:306
  63.9 21.5 %collective-permute-start.2 = (bf16[16,176,128]{2,1,0:T(8,128)(2,1)}, bf16[16,176,128]{2,1,0:T(8,128)(2,1)}, u32[]{:S(2)}, u32[]{:S(2)}) collective-permute-start(bf16[16,176,128]{2,1,0:T(8,128)(2,1)} %copy-done.6), channel_id=1, source_target_pairs={{0,224},{32,0},{64,32},{96,64},{128,96},{160,128},{192,160},{224,1... | collective-permute-start | bytes 2162696 | tf_op jit(solution)/shard_map/ppermute | solution.py:307
  85.4 11.1 %collective-permute-start.6 = (bf16[8,176,128]{2,1,0:T(8,128)(2,1)}, bf16[8,176,128]{2,1,0:T(8,128)(2,1)S(1)}, u32[]{:S(2)}, u32[]{:S(2)}) collective-permute-start(bf16[8,176,128]{2,1,0:T(8,128)(2,1)} %slice.73), channel_id=1, source_target_pairs={{0,32},{32,64},{64,96},{96,128},{128,160},{160,192},{192,224},{224... | collective-permute-start | bytes 1081352 | tf_op jit(solution)/shard_map/ppermute | solution.py:310
  87.2 10.4 %collective-permute-start.7 = (bf16[8,176,128]{2,1,0:T(8,128)(2,1)}, bf16[8,176,128]{2,1,0:T(8,128)(2,1)}, u32[]{:S(2)}, u32[]{:S(2)}) collective-permute-start(bf16[8,176,128]{2,1,0:T(8,128)(2,1)} %slice.74), channel_id=1, source_target_pairs={{0,224},{32,0},{64,32},{96,64},{128,96},{160,128},{192,160},{224,1... | collective-permute-start | bytes 1081352 | tf_op jit(solution)/shard_map/ppermute | solution.py:310
  99.3 1.3 copy-start.2
  100.6 34.6 %copy-start = (bf16[8,1408,128]{2,1,0:T(8,128)(2,1)}, bf16[8,1408,128]{2,1,0:T(8,128)(2,1)S(1)}, u32[]{:S(2)}) copy-start(bf16[8,1408,128]{2,1,0:T(8,128)(2,1)S(1)} %all-to-all-done.1) | copy-start | bytes 8650756
  100.6 34.6 %collective-permute-start.9 = (bf16[64,176,128]{2,1,0:T(8,128)(2,1)S(1)}, bf16[64,176,128]{2,1,0:T(8,128)(2,1)}, u32[]{:S(2)}, u32[]{:S(2)}) collective-permute-start(bf16[64,176,128]{2,1,0:T(8,128)(2,1)S(1)} %bitcast.41), channel_id=1, source_target_pairs={{0,1},{1,0},{2,3},{3,2},{4,7},{5,6},{6,5},{7,4},{8,9},{9,8},{10,11... | collective-permute-start | bytes 8650760 | tf_op jit(solution)/shard_map/ppermute | solution.py:404
  101.3 32.4 %all-to-all-start.2 = ((bf16[8,1056,128]{2,1,0:T(8,128)(2,1)}), bf16[8,1056,128]{2,1,0:T(8,128)(2,1)}, u32[]{:S(2)}, u32[]{:S(2)}) async-start(bf16[8,1056,128]{2,1,0:T(8,128)(2,1)} %bitcast.44), calls=%async_computation.2 | async-start | bytes 4325376 | tf_op jit(solution)/shard_map/all_to_all | solution.py:408
  107.1 87.4 %reduce-scatter.2.cloned.1.call-start = ((), (), s32[]{:S(2)}) async-start(), calls=%async_computation.4 | async-start | bytes 655360 | tf_op jit(solution)/shard_map/reduce_scatter | solution.py:422
  107.1 52.0 %collective-permute-start.10 = (bf16[16,176,128]{2,1,0:T(8,128)(2,1)}, bf16[16,176,128]{2,1,0:T(8,128)(2,1)}, u32[]{:S(2)}, u32[]{:S(2)}) collective-permute-start(bf16[16,176,128]{2,1,0:T(8,128)(2,1)} %bitcast.45), channel_id=1, source_target_pairs={{0,1},{1,0},{2,3},{3,2},{4,7},{5,6},{6,5},{7,4},{8,9},{9,8},{10,11... | collective-permute-start | bytes 2162696 | tf_op jit(solution)/shard_map/ppermute | solution.py:412
  133.7 35.3 %collective-permute-start.11 = (bf16[48,176,128]{2,1,0:T(8,128)(2,1)}, bf16[48,176,128]{2,1,0:T(8,128)(2,1)}, u32[]{:S(2)}, u32[]{:S(2)}) collective-permute-start(bf16[48,176,128]{2,1,0:T(8,128)(2,1)} %bitcast.25.refs_2_), channel_id=1, source_target_pairs={{0,1},{1,0},{2,3},{3,2},{4,7},{5,6},{6,5},{7,4},{8,9},{9,8},{10,11... | collective-permute-start | bytes 6488072 | tf_op jit(solution)/shard_map/ppermute | solution.py:412
  135.2 23.9 %copy-start.4 = (bf16[8,352,128]{2,1,0:T(8,128)(2,1)S(1)}, bf16[8,352,128]{2,1,0:T(8,128)(2,1)}, u32[]{:S(2)}) copy-start(bf16[8,352,128]{2,1,0:T(8,128)(2,1)} %copy-done.3) | copy-start | bytes 2162692
  135.2 23.9 %copy-start.5 = (bf16[272,16,128]{2,1,0:T(8,128)(2,1)S(1)}, bf16[272,16,128]{2,1,0:T(8,128)(2,1)}, u32[]{:S(2)}) copy-start(bf16[272,16,128]{2,1,0:T(8,128)(2,1)} %all-gather.3.cloned.1.call-done) | copy-start | bytes 3342340
  135.2 23.9 %copy-start.7 = (s32[64,16]{1,0:T(8,128)S(1)}, s32[64,16]{1,0:T(8,128)}, u32[]{:S(2)}) copy-start(s32[64,16]{1,0:T(8,128)} %get-tuple-element.52.sel) | copy-start | bytes 12292
  159.1 1.8 copy-start.1
  188.7 31.0 %collective-permute-start.13 = (bf16[48,32,512]{2,1,0:T(8,128)(2,1)}, bf16[48,32,512]{2,1,0:T(8,128)(2,1)S(1)}, u32[]{:S(2)}, u32[]{:S(2)}) collective-permute-start(bf16[48,32,512]{2,1,0:T(8,128)(2,1)} %get-tuple-element.54), channel_id=1, source_target_pairs={{0,3},{1,2},{2,1},{3,0},{4,5},{5,4},{6,7},{7,6},{8,11},{9,10},{10,... | collective-permute-start | bytes 4718600 | tf_op jit(solution)/shard_map/ppermute | solution.py:439
  194.5 11.8 %copy-start.10 = (f32[48,128]{1,0:T(8,128)S(1)}, f32[48,128]{1,0:T(8,128)}, u32[]{:S(2)}) copy-start(f32[48,128]{1,0:T(8,128)} %get-tuple-element.51) | copy-start | bytes 73732
  205.4 14.4 %copy-start.8 = (bf16[48,32,512]{2,1,0:T(8,128)(2,1)S(1)}, bf16[48,32,512]{2,1,0:T(8,128)(2,1)}, u32[]{:S(2)}) copy-start(bf16[48,32,512]{2,1,0:T(8,128)(2,1)} %get-tuple-element.48) | copy-start | bytes 4718596
  206.4 12.0 %collective-permute-start.14 = (bf16[16,32,512]{2,1,0:T(8,128)(2,1)}, bf16[16,32,512]{2,1,0:T(8,128)(2,1)S(1)}, u32[]{:S(2)}, u32[]{:S(2)}) collective-permute-start(bf16[16,32,512]{2,1,0:T(8,128)(2,1)} %get-tuple-element.56), channel_id=1, source_target_pairs={{0,3},{1,2},{2,1},{3,0},{4,5},{5,4},{6,7},{7,6},{8,11},{9,10},{10,... | collective-permute-start | bytes 1572872 | tf_op jit(solution)/shard_map/ppermute | solution.py:439
  207.0 10.6 %collective-permute-start.12 = (f32[64,32]{1,0:T(8,128)S(1)}, f32[64,32]{1,0:T(8,128)S(1)}, u32[]{:S(2)}, u32[]{:S(2)}) collective-permute-start(f32[64,32]{1,0:T(8,128)S(1)} %pad_maximum_fusion.2), channel_id=1, source_target_pairs={{0,3},{1,2},{2,1},{3,0},{4,5},{5,4},{6,7},{7,6},{8,11},{9,10},{10,... | collective-permute-start | bytes 24584 | tf_op jit(solution)/shard_map/ppermute | solution.py:442
Sparse Core Ops, SparseCore 0:
  65.6 26.2 all-gather.2
  169.0 25.4 reduce-scatter.1

commit v6 on v5

--- a/solution.py
+++ b/solution.py
@@ -13,7 +13,7 @@
 TILE = 128
 CAP = 2
 PART = 32
-GROUP = 8
+GROUP = 16
 BATCH = 8
 SCALE = 192.0 ** -0.5
 LOG2_E = 1.4426950408889634

time: 231 us -> 229 us (level)
  transfers between devices with their start and end apart: 20 -> 20, of which waited for: 10 -> 10; matrix products, arithmetic and copies ran while one was open for 8% -> 8% of each run, Pallas kernels for 30% -> 29%
where the time goes in v6:
time: 229 us; the launch traced here: 227 us
  waiting for transfers between devices  68.5 us (30%)
  Pallas kernels  66.4 us (29%)
  starting transfers between devices  45 us (20%)
  local copies, waits for them, and re-layouts  16.6 us (7%)
  between operations  14.4 us (6%)
  blocking collectives  8.67 us (4%)
  other arithmetic  7.23 us (3%)
    pallas_call x3, Pallas kernels, attend(): pl.pallas_call(functools.partial(attend_kernel, merge=merge, fetched_coun...  53.3 us
    all_to_all x3, waiting for transfers between devices, shards(): lax.all_to_all(found.reshape(plane, -1, LANES), ('x', 'c'), split_axis=0,...  24.7 us
    ppermute x3, waiting for transfers between devices, ring_blocks(): up = lax.ppermute(up, axis, forward)  18.3 us
    all_to_all x3, starting transfers between devices, shards(): lax.all_to_all(found.reshape(plane, -1, LANES), ('x', 'c'), split_axis=0,...  15.5 us
    ppermute x3, starting transfers between devices, ring_blocks(): down = lax.ppermute(down, axis, backward)  12.8 us
    ppermute x3, waiting for transfers between devices, ring_blocks(): down = lax.ppermute(down, axis, backward)  11 us
    all_gather x1, blocking collectives, shards(): lax.all_gather(wanted, ('x', 'c')).reshape(plane, z_count, plane, CAP)  8.67 us
    ppermute x1, waiting for transfers between devices, shards(): all_lse = lax.ppermute(all_lse, ('c', 'y'), head_pairs)  7.77 us
  transfers between devices with their start and end apart: 20, of which 10 were waited for; matrix products, arithmetic and copies ran while one was open for 8% of the time, Pallas kernels for 29%

profile of v6, /device:TPU:2, one launch (start us, length us, event | category | flops | bytes accessed | tf_op | source)
XLA Modules:
  0.0 226.7 jit_solution(12357132585067354219)
XLA Ops:
  7.2 3.1 %collective-permute-start.8 = (bf16[64,32,576]{2,1,0:T(8,128)(2,1)}, bf16[64,32,576]{2,1,0:T(8,128)(2,1)}, u32[]{:S(2)}, u32[]{:S(2)}) collective-permute-start(bf16[64,32,576]{2,1,0:T(8,128)(2,1)} %q_own.5), channel_id=1, source_target_pairs={{0,3},{1,2},{2,1},{3,0},{4,5},{5,4},{6,7},{7,6},{8,11},{9,10},{10,... | collective-permute-start | bytes 7077896 | tf_op jit(solution)/shard_map/ppermute | solution.py:354
  10.3 3.1 %copy.93 = bf16[2048,576]{1,0:T(8,128)(2,1)S(1)} copy(bf16[2048,576]{0,1:T(8,128)(2,1)} %param.8) | data formatting | bytes 4718592 | tf_op args[1]
  13.6 0.1 maximum_dynamic-update-slice_fusion
  13.7 0.9 bitcast_dynamic-update-slice_fusion.refs_0_
  14.7 5.9 %collective-permute-start = (bf16[16,176,128]{2,1,0:T(8,128)(2,1)S(1)}, bf16[16,176,128]{2,1,0:T(8,128)(2,1)S(1)}, u32[]{:S(2)}, u32[]{:S(2)}) collective-permute-start(bf16[16,176,128]{2,1,0:T(8,128)(2,1)S(1)} %bitcast_dynamic-update-slice_fusion.refs_0_), channel_id=1, source_target_pairs={{0,224},{32,0},{64,32},{96,64},{128,96},{160,128},{192,160},{224,1... | collective-permute-start | bytes 2162696 | tf_op jit(solution)/shard_map/ppermute | solution.py:307
  20.6 8.7 %all_gather.9 = s32[8,64,2]{1,2,0:T(2,128)S(1)} all-gather(s32[1,64,2]{1,2,0:T(2,128)S(1)} %copy-done.13), channel_id=1, replica_groups=mesh['z'=8,'x'=4,'c'=2,'y'=4] {'x','c'}, dimensions={0}, use_global_device_ids=true | all-gather | bytes 4608 | tf_op jit(solution)/shard_map/all_gather | solution.py:359
  29.3 0.1 copy.116
  29.4 4.9 %collective-permute-done.refs_0_ = bf16[16,176,128]{2,1,0:T(8,128)(2,1)S(1)} collective-permute-done((bf16[16,176,128]{2,1,0:T(8,128)(2,1)S(1)}, bf16[16,176,128]{2,1,0:T(8,128)(2,1)S(1)}, u32[]{:S(2)}, u32[]{:S(2)}) %collective-permute-start) | collective-permute-done | bytes 720928 | tf_op jit(solution)/shard_map/ppermute | solution.py:307
  34.3 3.7 %collective-permute-start.1 = (bf16[16,176,128]{2,1,0:T(8,128)(2,1)S(1)}, bf16[16,176,128]{2,1,0:T(8,128)(2,1)S(1)}, u32[]{:S(2)}, u32[]{:S(2)}) collective-permute-start(bf16[16,176,128]{2,1,0:T(8,128)(2,1)S(1)} %collective-permute-done.refs_0_), channel_id=1, source_target_pairs={{0,224},{32,0},{64,32},{96,64},{128,96},{160,128},{192,160},{224,1... | collective-permute-start | bytes 2162696 | tf_op jit(solution)/shard_map/ppermute | solution.py:307
  38.0 0.1 copy.105.asked
  38.1 1.5 take.5
  39.6 4.8 %all-to-all-start = ((bf16[8,352,128]{2,1,0:T(8,128)(2,1)}), bf16[8,352,128]{2,1,0:T(8,128)(2,1)S(1)}, u32[]{:S(2)}, u32[]{:S(2)}) async-start(bf16[8,352,128]{2,1,0:T(8,128)(2,1)} %bitcast.13), calls=%async_computation | async-start | bytes 1441792 | tf_op jit(solution)/shard_map/all_to_all | solution.py:408
  44.4 0.1 copy.100
  44.5 0.1 copy.101
  44.6 0.1 copy.102
  44.7 0.1 copy.103
  44.8 6.1 %collective-permute-done.1.refs_2_ = bf16[16,176,128]{2,1,0:T(8,128)(2,1)S(1)} collective-permute-done((bf16[16,176,128]{2,1,0:T(8,128)(2,1)S(1)}, bf16[16,176,128]{2,1,0:T(8,128)(2,1)S(1)}, u32[]{:S(2)}, u32[]{:S(2)}) %collective-permute-start.1) | collective-permute-done | bytes 720928 | tf_op jit(solution)/shard_map/ppermute | solution.py:307
  50.8 3.5 %collective-permute-done.4.refs_3_ = bf16[16,176,128]{2,1,0:T(8,128)(2,1)} collective-permute-done((bf16[16,176,128]{2,1,0:T(8,128)(2,1)S(1)}, bf16[16,176,128]{2,1,0:T(8,128)(2,1)}, u32[]{:S(2)}, u32[]{:S(2)}) %collective-permute-start.4) | collective-permute-done | bytes 720928 | tf_op jit(solution)/shard_map/ppermute | solution.py:306
  54.4 2.9 %take.4 = bf16[8,8,176,128]{3,2,1,0:T(8,128)(2,1)} custom-call(s32[4,8,2]{2,1,0:T(8,128)S(1)} %pad_add_fusion.asked, bf16[16,176,128]{2,1,0:T(8,128)(2,1)S(1)} %collective-permute-done.refs_0_, bf16[16,176,128]{2,1,0:T(8,128)(2,1)S(1)} %collective-permute-done.3.refs_1_, bf16[16,176,128]{2,1,0:T(8,128)(2,1)S(1)} %collective-permute-done.1.refs_2_, ...), custom_call_target="tpu_custom_call" | custom-call | bytes 6000000 | tf_op jit(solution)/shard_map/take/pallas_call | solution.py:210
  57.3 0.8 copy-done.3
  58.1 4.8 %all-to-all-start.1 = ((bf16[8,1408,128]{2,1,0:T(8,128)(2,1)}), bf16[8,1408,128]{2,1,0:T(8,128)(2,1)S(1)}, u32[]{:S(2)}, u32[]{:S(2)}) async-start(bf16[8,1408,128]{2,1,0:T(8,128)(2,1)} %bitcast.15), calls=%async_computation.1 | async-start | bytes 5767168 | tf_op jit(solution)/shard_map/all_to_all | solution.py:408
  62.9 0.1 copy.106
  63.1 0.8 pad_maximum_fusion.1
  63.8 0.1 collective-permute-start.5
  63.9 3.2 %collective-permute-start.2 = (bf16[16,176,128]{2,1,0:T(8,128)(2,1)}, bf16[16,176,128]{2,1,0:T(8,128)(2,1)}, u32[]{:S(2)}, u32[]{:S(2)}) collective-permute-start(bf16[16,176,128]{2,1,0:T(8,128)(2,1)} %copy-done.6), channel_id=1, source_target_pairs={{0,224},{32,0},{64,32},{96,64},{128,96},{160,128},{192,160},{224,1... | collective-permute-start | bytes 2162696 | tf_op jit(solution)/shard_map/ppermute | solution.py:307
  67.2 0.1 copy.112
  67.3 0.1 copy.95.asked
  67.4 0.1 copy.107
  67.4 0.1 reshape_squeeze.3
  67.6 1.3 select_reduce_fusion
  68.9 14.7 %collective-permute-done.5.refs_1_ = bf16[16,176,128]{2,1,0:T(8,128)(2,1)} collective-permute-done((bf16[16,176,128]{2,1,0:T(8,128)(2,1)}, bf16[16,176,128]{2,1,0:T(8,128)(2,1)}, u32[]{:S(2)}, u32[]{:S(2)}) %collective-permute-start.5) | collective-permute-done | bytes 720928 | tf_op jit(solution)/shard_map/ppermute | solution.py:306
  83.6 1.8 slice.73
  85.4 1.8 slice.74
  87.2 3.2 %collective-permute-start.7 = (bf16[8,176,128]{2,1,0:T(8,128)(2,1)}, bf16[8,176,128]{2,1,0:T(8,128)(2,1)}, u32[]{:S(2)}, u32[]{:S(2)}) collective-permute-start(bf16[8,176,128]{2,1,0:T(8,128)(2,1)} %slice.74), channel_id=1, source_target_pairs={{0,224},{32,0},{64,32},{96,64},{128,96},{160,128},{192,160},{224,1... | collective-permute-start | bytes 1081352 | tf_op jit(solution)/shard_map/ppermute | solution.py:310
  90.4 0.7 broadcast_subtract_fusion.1
  91.2 0.7 sub.70
  91.9 1.1 copy.114
  93.1 3.4 %collective-permute-done.6.refs_2_ = bf16[8,176,128]{2,1,0:T(8,128)(2,1)S(1)} collective-permute-done((bf16[8,176,128]{2,1,0:T(8,128)(2,1)}, bf16[8,176,128]{2,1,0:T(8,128)(2,1)S(1)}, u32[]{:S(2)}, u32[]{:S(2)}) %collective-permute-start.6) | collective-permute-done | bytes 360480 | tf_op jit(solution)/shard_map/ppermute | solution.py:310
  96.5 1.1 collective-permute-done.7.refs_3_
  97.6 1.7 take.3
  99.3 1.3 copy-done.2
  100.6 0.6 collective-permute-start.9
  101.3 5.8 %all-to-all-start.2 = ((bf16[8,1056,128]{2,1,0:T(8,128)(2,1)}), bf16[8,1056,128]{2,1,0:T(8,128)(2,1)}, u32[]{:S(2)}, u32[]{:S(2)}) async-start(bf16[8,1056,128]{2,1,0:T(8,128)(2,1)} %bitcast.44), calls=%async_computation.2 | async-start | bytes 4325376 | tf_op jit(solution)/shard_map/all_to_all | solution.py:408
  107.1 0.9 collective-permute-start.10
  108.0 0.8 slice.59
  108.9 0.1 copy.118
  109.0 24.7 %all-to-all-done.2 = bf16[8,1056,128]{2,1,0:T(8,128)(2,1)} async-done(((bf16[8,1056,128]{2,1,0:T(8,128)(2,1)}), bf16[8,1056,128]{2,1,0:T(8,128)(2,1)}, u32[]{:S(2)}, u32[]{:S(2)}) %all-to-all-start.2) | async-done | bytes 2162720 | tf_op jit(solution)/shard_map/all_to_all | solution.py:408
  133.7 0.9 collective-permute-start.11
  134.6 0.6 collective-permute-done.9.refs_3_
  135.2 22.9 %attend_own.1 = (bf16[64,64,512]{2,1,0:T(8,128)(2,1)}, f32[64,128]{1,0:T(8,128)}) custom-call(s32[64,16]{1,0:T(8,128)} %get-tuple-element.52.sel, s32[64,16]{1,0:T(8,128)} %get-tuple-element.35.lim, s32[1]{0:T(128)} %bitcast.23.quarter, bf16[64,32,576]{2,1,0:T(8,128)(2,1)} %q_own.5, bf16[64,32,576]{2,1,0:T(8,128)(2,1)} %collective-permute-done.8.q_pair, ...), custom_call_target="tpu_custom_call" | custom-call | flops 25600000000 | bytes 12000000 | tf_op jit(solution)/shard_map/attend_own/pallas_call | solution.py:166
  158.2 1.8 copy-done.1
  160.0 7.0 %index.1 = f32[64,2048]{1,0:T(8,128)} custom-call(s32[64,16]{1,0:T(8,128)S(1)} %copy-done.7, s32[1]{0:T(128)} %bitcast.23.quarter, bf16[4,68,16,128]{3,2,1,0:T(8,128)(2,1)S(1)} %bitcast.49, f32[64,64]{1,0:T(8,128)S(1)} %bitcast.50, s32[64,512]{1,0:T(8,128)S(1)} %broadcast_subtract_fusion.lim, bf16[16,176,128]{2,1,0:T(8,128)(2,1)S(1)} %bitcast.47, ...), custom_call_target="tpu_custom_call" | custom-call | tf_op jit(solution)/shard_map/index/pallas_call | solution.py:291
  167.1 19.4 %attend_merge.2 = (bf16[48,32,512]{2,1,0:T(8,128)(2,1)}, bf16[48,32,512]{2,1,0:T(8,128)(2,1)}, f32[48,128]{1,0:T(8,128)}) custom-call(s32[64,16]{1,0:T(8,128)} %get-tuple-element.52.sel, s32[64,16]{1,0:T(8,128)} %get-tuple-element.35.lim, s32[1]{0:T(128)} %bitcast.26.quarter, bf16[64,32,576]{2,1,0:T(8,128)(2,1)} %q_own.5, ...), custom_call_target="tpu_custom_call" | custom-call | flops 19200000000 | bytes 12000000 | tf_op jit(solution)/shard_map/attend_merge/pallas_call | solution.py:166
  186.5 4.5 %collective-permute-start.13 = (bf16[48,32,512]{2,1,0:T(8,128)(2,1)}, bf16[48,32,512]{2,1,0:T(8,128)(2,1)S(1)}, u32[]{:S(2)}, u32[]{:S(2)}) collective-permute-start(bf16[48,32,512]{2,1,0:T(8,128)(2,1)} %get-tuple-element.54), channel_id=1, source_target_pairs={{0,3},{1,2},{2,1},{3,0},{4,5},{5,4},{6,7},{7,6},{8,11},{9,10},{10,... | collective-permute-start | bytes 4718600 | tf_op jit(solution)/shard_map/ppermute | solution.py:439
  191.0 1.6 reduce-scatter.2.cloned.1.call-done
  192.6 11.0 %attend_merge.3 = (bf16[16,32,512]{2,1,0:T(8,128)(2,1)}, bf16[16,32,512]{2,1,0:T(8,128)(2,1)}, f32[16,128]{1,0:T(8,128)}) custom-call(s32[64,16]{1,0:T(8,128)} %get-tuple-element.52.sel, s32[64,16]{1,0:T(8,128)} %get-tuple-element.35.lim, s32[1]{0:T(128)} %bitcast.26.quarter, bf16[64,32,576]{2,1,0:T(8,128)(2,1)} %q_own.5, ...), custom_call_target="tpu_custom_call" | custom-call | flops 6400000000 | bytes 12000000 | tf_op jit(solution)/shard_map/attend_merge/pallas_call | solution.py:166
  203.6 0.9 slice.62
  204.5 0.6 collective-permute-start.14
  205.2 2.6 %collective-permute-start.12 = (f32[64,32]{1,0:T(8,128)S(1)}, f32[64,32]{1,0:T(8,128)S(1)}, u32[]{:S(2)}, u32[]{:S(2)}) collective-permute-start(f32[64,32]{1,0:T(8,128)S(1)} %pad_maximum_fusion.2), channel_id=1, source_target_pairs={{0,3},{1,2},{2,1},{3,0},{4,5},{5,4},{6,7},{7,6},{8,11},{9,10},{10,... | collective-permute-start | bytes 24584 | tf_op jit(solution)/shard_map/ppermute | solution.py:442
  207.8 7.8 %collective-permute-done.12 = f32[64,32]{1,0:T(8,128)S(1)} collective-permute-done((f32[64,32]{1,0:T(8,128)S(1)}, f32[64,32]{1,0:T(8,128)S(1)}, u32[]{:S(2)}, u32[]{:S(2)}) %collective-permute-start.12) | collective-permute-done | bytes 8224 | tf_op jit(solution)/shard_map/ppermute | solution.py:442
  215.6 0.7 add_divide_fusion.3
  216.3 1.3 add_convert_fusion.1
  217.7 0.7 add_convert_fusion
  218.4 1.5 pad_maximum_fusion
  (61 shorter events, 0.7 us)
Async XLA Ops:
  7.2 50.1 %collective-permute-start.8 = (bf16[64,32,576]{2,1,0:T(8,128)(2,1)}, bf16[64,32,576]{2,1,0:T(8,128)(2,1)}, u32[]{:S(2)}, u32[]{:S(2)}) collective-permute-start(bf16[64,32,576]{2,1,0:T(8,128)(2,1)} %q_own.5), channel_id=1, source_target_pairs={{0,3},{1,2},{2,1},{3,0},{4,5},{5,4},{6,7},{7,6},{8,11},{9,10},{10,... | collective-permute-start | bytes 7077896 | tf_op jit(solution)/shard_map/ppermute | solution.py:354
  13.4 7.3 %copy-start.13 = (s32[1,64,2]{1,2,0:T(2,128)S(1)}, s32[1,64,2]{1,2,0:T(2,128)}, u32[]{:S(2)}) copy-start(s32[1,64,2]{1,2,0:T(2,128)} %param.12) | copy-start | bytes 1540
  14.7 19.6 %collective-permute-start = (bf16[16,176,128]{2,1,0:T(8,128)(2,1)S(1)}, bf16[16,176,128]{2,1,0:T(8,128)(2,1)S(1)}, u32[]{:S(2)}, u32[]{:S(2)}) collective-permute-start(bf16[16,176,128]{2,1,0:T(8,128)(2,1)S(1)} %bitcast_dynamic-update-slice_fusion.refs_0_), channel_id=1, source_target_pairs={{0,224},{32,0},{64,32},{96,64},{128,96},{160,128},{192,160},{224,1... | collective-permute-start | bytes 2162696 | tf_op jit(solution)/shard_map/ppermute | solution.py:307
  20.6 17.4 %collective-permute-start.3 = (bf16[16,176,128]{2,1,0:T(8,128)(2,1)S(1)}, bf16[16,176,128]{2,1,0:T(8,128)(2,1)S(1)}, u32[]{:S(2)}, u32[]{:S(2)}) collective-permute-start(bf16[16,176,128]{2,1,0:T(8,128)(2,1)S(1)} %bitcast_dynamic-update-slice_fusion.refs_0_), channel_id=1, source_target_pairs={{0,32},{32,64},{64,96},{96,128},{128,160},{160,192},{192,224},{224... | collective-permute-start | bytes 2162696 | tf_op jit(solution)/shard_map/ppermute | solution.py:306
  34.3 16.5 %collective-permute-start.1 = (bf16[16,176,128]{2,1,0:T(8,128)(2,1)S(1)}, bf16[16,176,128]{2,1,0:T(8,128)(2,1)S(1)}, u32[]{:S(2)}, u32[]{:S(2)}) collective-permute-start(bf16[16,176,128]{2,1,0:T(8,128)(2,1)S(1)} %collective-permute-done.refs_0_), channel_id=1, source_target_pairs={{0,224},{32,0},{64,32},{96,64},{128,96},{160,128},{192,160},{224,1... | collective-permute-start | bytes 2162696 | tf_op jit(solution)/shard_map/ppermute | solution.py:307
  38.0 16.4 %collective-permute-start.4 = (bf16[16,176,128]{2,1,0:T(8,128)(2,1)S(1)}, bf16[16,176,128]{2,1,0:T(8,128)(2,1)}, u32[]{:S(2)}, u32[]{:S(2)}) collective-permute-start(bf16[16,176,128]{2,1,0:T(8,128)(2,1)S(1)} %collective-permute-done.3.refs_1_), channel_id=1, source_target_pairs={{0,32},{32,64},{64,96},{96,128},{128,160},{160,192},{192,224},{224... | collective-permute-start | bytes 2162696 | tf_op jit(solution)/shard_map/ppermute | solution.py:306
  39.6 17.6 %all-to-all-start = ((bf16[8,352,128]{2,1,0:T(8,128)(2,1)}), bf16[8,352,128]{2,1,0:T(8,128)(2,1)S(1)}, u32[]{:S(2)}, u32[]{:S(2)}) async-start(bf16[8,352,128]{2,1,0:T(8,128)(2,1)} %bitcast.13), calls=%async_computation | async-start | bytes 1441792 | tf_op jit(solution)/shard_map/all_to_all | solution.py:408
  50.8 6.4 %copy-start.6 = (bf16[16,176,128]{2,1,0:T(8,128)(2,1)}, bf16[16,176,128]{2,1,0:T(8,128)(2,1)S(1)}, u32[]{:S(2)}) copy-start(bf16[16,176,128]{2,1,0:T(8,128)(2,1)S(1)} %collective-permute-done.1.refs_2_) | copy-start | bytes 2162692
  57.2 0.9 copy-start.3
  57.2 5.7 %copy-start.12 = (bf16[64,16]{0,1:T(8,128)(2,1)S(1)}, bf16[64,16]{0,1:T(8,128)(2,1)}, u32[]{:S(2)}) copy-start(bf16[64,16]{0,1:T(8,128)(2,1)} %param.10) | copy-start | bytes 6148
  57.3 5.8 %copy-start.9 = (bf16[64,16,128]{2,1,0:T(8,128)(2,1)S(1)}, bf16[64,16,128]{2,1,0:T(8,128)(2,1)}, u32[]{:S(2)}) copy-start(bf16[64,16,128]{2,1,0:T(8,128)(2,1)} %param.9) | copy-start | bytes 786436
  57.3 10.1 %copy-start.11 = (s32[64,16]{0,1:T(8,128)S(1)}, s32[64,16]{0,1:T(8,128)}, u32[]{:S(2)}) copy-start(s32[64,16]{0,1:T(8,128)} %param.13) | copy-start | bytes 12292
  58.1 42.6 %all-to-all-start.1 = ((bf16[8,1408,128]{2,1,0:T(8,128)(2,1)}), bf16[8,1408,128]{2,1,0:T(8,128)(2,1)S(1)}, u32[]{:S(2)}, u32[]{:S(2)}) async-start(bf16[8,1408,128]{2,1,0:T(8,128)(2,1)} %bitcast.15), calls=%async_computation.1 | async-start | bytes 5767168 | tf_op jit(solution)/shard_map/all_to_all | solution.py:408
  62.9 37.7 %all-gather.3.cloned.1.call-start = ((), (), s32[]{:S(2)}) async-start(), calls=%async_computation.5 | async-start | bytes 1392640 | tf_op jit(solution)/shard_map/all_gather | solution.py:357
  63.8 19.8 %collective-permute-start.5 = (bf16[16,176,128]{2,1,0:T(8,128)(2,1)}, bf16[16,176,128]{2,1,0:T(8,128)(2,1)}, u32[]{:S(2)}, u32[]{:S(2)}) collective-permute-start(bf16[16,176,128]{2,1,0:T(8,128)(2,1)} %collective-permute-done.4.refs_3_), channel_id=1, source_target_pairs={{0,32},{32,64},{64,96},{96,128},{128,160},{160,192},{192,224},{224... | collective-permute-start | bytes 2162696 | tf_op jit(solution)/shard_map/ppermute | solution.py:306
  63.9 21.5 %collective-permute-start.2 = (bf16[16,176,128]{2,1,0:T(8,128)(2,1)}, bf16[16,176,128]{2,1,0:T(8,128)(2,1)}, u32[]{:S(2)}, u32[]{:S(2)}) collective-permute-start(bf16[16,176,128]{2,1,0:T(8,128)(2,1)} %copy-done.6), channel_id=1, source_target_pairs={{0,224},{32,0},{64,32},{96,64},{128,96},{160,128},{192,160},{224,1... | collective-permute-start | bytes 2162696 | tf_op jit(solution)/shard_map/ppermute | solution.py:307
  85.4 11.1 %collective-permute-start.6 = (bf16[8,176,128]{2,1,0:T(8,128)(2,1)}, bf16[8,176,128]{2,1,0:T(8,128)(2,1)S(1)}, u32[]{:S(2)}, u32[]{:S(2)}) collective-permute-start(bf16[8,176,128]{2,1,0:T(8,128)(2,1)} %slice.73), channel_id=1, source_target_pairs={{0,32},{32,64},{64,96},{96,128},{128,160},{160,192},{192,224},{224... | collective-permute-start | bytes 1081352 | tf_op jit(solution)/shard_map/ppermute | solution.py:310
  87.2 10.4 %collective-permute-start.7 = (bf16[8,176,128]{2,1,0:T(8,128)(2,1)}, bf16[8,176,128]{2,1,0:T(8,128)(2,1)}, u32[]{:S(2)}, u32[]{:S(2)}) collective-permute-start(bf16[8,176,128]{2,1,0:T(8,128)(2,1)} %slice.74), channel_id=1, source_target_pairs={{0,224},{32,0},{64,32},{96,64},{128,96},{160,128},{192,160},{224,1... | collective-permute-start | bytes 1081352 | tf_op jit(solution)/shard_map/ppermute | solution.py:310
  99.3 1.3 copy-start.2
  100.6 34.6 %copy-start = (bf16[8,1408,128]{2,1,0:T(8,128)(2,1)}, bf16[8,1408,128]{2,1,0:T(8,128)(2,1)S(1)}, u32[]{:S(2)}) copy-start(bf16[8,1408,128]{2,1,0:T(8,128)(2,1)S(1)} %all-to-all-done.1) | copy-start | bytes 8650756
  100.6 34.6 %collective-permute-start.9 = (bf16[64,176,128]{2,1,0:T(8,128)(2,1)S(1)}, bf16[64,176,128]{2,1,0:T(8,128)(2,1)}, u32[]{:S(2)}, u32[]{:S(2)}) collective-permute-start(bf16[64,176,128]{2,1,0:T(8,128)(2,1)S(1)} %bitcast.41), channel_id=1, source_target_pairs={{0,1},{1,0},{2,3},{3,2},{4,7},{5,6},{6,5},{7,4},{8,9},{9,8},{10,11... | collective-permute-start | bytes 8650760 | tf_op jit(solution)/shard_map/ppermute | solution.py:404
  101.3 32.4 %all-to-all-start.2 = ((bf16[8,1056,128]{2,1,0:T(8,128)(2,1)}), bf16[8,1056,128]{2,1,0:T(8,128)(2,1)}, u32[]{:S(2)}, u32[]{:S(2)}) async-start(bf16[8,1056,128]{2,1,0:T(8,128)(2,1)} %bitcast.44), calls=%async_computation.2 | async-start | bytes 4325376 | tf_op jit(solution)/shard_map/all_to_all | solution.py:408
  107.1 85.5 %reduce-scatter.2.cloned.1.call-start = ((), (), s32[]{:S(2)}) async-start(), calls=%async_computation.4 | async-start | bytes 655360 | tf_op jit(solution)/shard_map/reduce_scatter | solution.py:422
  107.1 51.1 %collective-permute-start.10 = (bf16[16,176,128]{2,1,0:T(8,128)(2,1)}, bf16[16,176,128]{2,1,0:T(8,128)(2,1)}, u32[]{:S(2)}, u32[]{:S(2)}) collective-permute-start(bf16[16,176,128]{2,1,0:T(8,128)(2,1)} %bitcast.45), channel_id=1, source_target_pairs={{0,1},{1,0},{2,3},{3,2},{4,7},{5,6},{6,5},{7,4},{8,9},{9,8},{10,11... | collective-permute-start | bytes 2162696 | tf_op jit(solution)/shard_map/ppermute | solution.py:412
  133.7 33.4 %collective-permute-start.11 = (bf16[48,176,128]{2,1,0:T(8,128)(2,1)}, bf16[48,176,128]{2,1,0:T(8,128)(2,1)}, u32[]{:S(2)}, u32[]{:S(2)}) collective-permute-start(bf16[48,176,128]{2,1,0:T(8,128)(2,1)} %bitcast.25.refs_2_), channel_id=1, source_target_pairs={{0,1},{1,0},{2,3},{3,2},{4,7},{5,6},{6,5},{7,4},{8,9},{9,8},{10,11... | collective-permute-start | bytes 6488072 | tf_op jit(solution)/shard_map/ppermute | solution.py:412
  135.2 23.0 %copy-start.4 = (bf16[8,352,128]{2,1,0:T(8,128)(2,1)S(1)}, bf16[8,352,128]{2,1,0:T(8,128)(2,1)}, u32[]{:S(2)}) copy-start(bf16[8,352,128]{2,1,0:T(8,128)(2,1)} %copy-done.3) | copy-start | bytes 2162692
  135.2 23.0 %copy-start.5 = (bf16[272,16,128]{2,1,0:T(8,128)(2,1)S(1)}, bf16[272,16,128]{2,1,0:T(8,128)(2,1)}, u32[]{:S(2)}) copy-start(bf16[272,16,128]{2,1,0:T(8,128)(2,1)} %all-gather.3.cloned.1.call-done) | copy-start | bytes 3342340
  135.2 23.0 %copy-start.7 = (s32[64,16]{1,0:T(8,128)S(1)}, s32[64,16]{1,0:T(8,128)}, u32[]{:S(2)}) copy-start(s32[64,16]{1,0:T(8,128)} %get-tuple-element.52.sel) | copy-start | bytes 12292
  158.2 1.8 copy-start.1
  186.5 31.2 %collective-permute-start.13 = (bf16[48,32,512]{2,1,0:T(8,128)(2,1)}, bf16[48,32,512]{2,1,0:T(8,128)(2,1)S(1)}, u32[]{:S(2)}, u32[]{:S(2)}) collective-permute-start(bf16[48,32,512]{2,1,0:T(8,128)(2,1)} %get-tuple-element.54), channel_id=1, source_target_pairs={{0,3},{1,2},{2,1},{3,0},{4,5},{5,4},{6,7},{7,6},{8,11},{9,10},{10,... | collective-permute-start | bytes 4718600 | tf_op jit(solution)/shard_map/ppermute | solution.py:439
  192.6 11.9 %copy-start.10 = (f32[48,128]{1,0:T(8,128)S(1)}, f32[48,128]{1,0:T(8,128)}, u32[]{:S(2)}) copy-start(f32[48,128]{1,0:T(8,128)} %get-tuple-element.51) | copy-start | bytes 73732
  203.6 14.1 %copy-start.8 = (bf16[48,32,512]{2,1,0:T(8,128)(2,1)S(1)}, bf16[48,32,512]{2,1,0:T(8,128)(2,1)}, u32[]{:S(2)}) copy-start(bf16[48,32,512]{2,1,0:T(8,128)(2,1)} %get-tuple-element.48) | copy-start | bytes 4718596
  204.5 11.8 %collective-permute-start.14 = (bf16[16,32,512]{2,1,0:T(8,128)(2,1)}, bf16[16,32,512]{2,1,0:T(8,128)(2,1)S(1)}, u32[]{:S(2)}, u32[]{:S(2)}) collective-permute-start(bf16[16,32,512]{2,1,0:T(8,128)(2,1)} %get-tuple-element.56), channel_id=1, source_target_pairs={{0,3},{1,2},{2,1},{3,0},{4,5},{5,4},{6,7},{7,6},{8,11},{9,10},{10,... | collective-permute-start | bytes 1572872 | tf_op jit(solution)/shard_map/ppermute | solution.py:439
  205.2 10.4 %collective-permute-start.12 = (f32[64,32]{1,0:T(8,128)S(1)}, f32[64,32]{1,0:T(8,128)S(1)}, u32[]{:S(2)}, u32[]{:S(2)}) collective-permute-start(f32[64,32]{1,0:T(8,128)S(1)} %pad_maximum_fusion.2), channel_id=1, source_target_pairs={{0,3},{1,2},{2,1},{3,0},{4,5},{5,4},{6,7},{7,6},{8,11},{9,10},{10,... | collective-permute-start | bytes 24584 | tf_op jit(solution)/shard_map/ppermute | solution.py:442
Sparse Core Ops, SparseCore 0:
  65.6 26.2 all-gather.2
  167.2 25.3 reduce-scatter.1

commit v7 on v6

--- a/solution.py
+++ b/solution.py
@@ -14,7 +14,7 @@
 CAP = 2
 PART = 32
 GROUP = 16
-BATCH = 8
+BATCH = 16
 SCALE = 192.0 ** -0.5
 LOG2_E = 1.4426950408889634
 MASKED = -1e30

time: 229 us -> 230 us (level)
  transfers between devices with their start and end apart: 20 -> 20, of which waited for: 10 -> 10; matrix products, arithmetic and copies ran while one was open for 8% -> 8% of each run, Pallas kernels for 29% -> 30%
where the time goes in v7:
time: 230 us; the launch traced here: 228 us
  waiting for transfers between devices  68.3 us (30%)
  Pallas kernels  67.7 us (29%)
  starting transfers between devices  45 us (20%)
  local copies, waits for them, and re-layouts  16.6 us (7%)
  between operations  14.4 us (6%)
  blocking collectives  8.67 us (4%)
  other arithmetic  7.23 us (3%)
    pallas_call x3, Pallas kernels, attend(): pl.pallas_call(functools.partial(attend_kernel, merge=merge, fetched_coun...  54.6 us
    all_to_all x3, waiting for transfers between devices, shards(): lax.all_to_all(found.reshape(plane, -1, LANES), ('x', 'c'), split_axis=0,...  24.7 us
    ppermute x3, waiting for transfers between devices, ring_blocks(): up = lax.ppermute(up, axis, forward)  18.3 us
    all_to_all x3, starting transfers between devices, shards(): lax.all_to_all(found.reshape(plane, -1, LANES), ('x', 'c'), split_axis=0,...  15.5 us
    ppermute x3, starting transfers between devices, ring_blocks(): down = lax.ppermute(down, axis, backward)  12.8 us
    ppermute x3, waiting for transfers between devices, ring_blocks(): down = lax.ppermute(down, axis, backward)  11 us
    all_gather x1, blocking collectives, shards(): lax.all_gather(wanted, ('x', 'c')).reshape(plane, z_count, plane, CAP)  8.67 us
    ppermute x1, waiting for transfers between devices, shards(): all_lse = lax.ppermute(all_lse, ('c', 'y'), head_pairs)  7.99 us
  transfers between devices with their start and end apart: 20, of which 10 were waited for; matrix products, arithmetic and copies ran while one was open for 8% of the time, Pallas kernels for 30%

profile of v7, /device:TPU:2, one launch (start us, length us, event | category | flops | bytes accessed | tf_op | source)
XLA Modules:
  0.0 227.9 jit_solution(13939247302329761695)
XLA Ops:
  7.2 3.1 %collective-permute-start.8 = (bf16[64,32,576]{2,1,0:T(8,128)(2,1)}, bf16[64,32,576]{2,1,0:T(8,128)(2,1)}, u32[]{:S(2)}, u32[]{:S(2)}) collective-permute-start(bf16[64,32,576]{2,1,0:T(8,128)(2,1)} %q_own.5), channel_id=1, source_target_pairs={{0,3},{1,2},{2,1},{3,0},{4,5},{5,4},{6,7},{7,6},{8,11},{9,10},{10,... | collective-permute-start | bytes 7077896 | tf_op jit(solution)/shard_map/ppermute | solution.py:354
  10.3 3.1 %copy.93 = bf16[2048,576]{1,0:T(8,128)(2,1)S(1)} copy(bf16[2048,576]{0,1:T(8,128)(2,1)} %param.8) | data formatting | bytes 4718592 | tf_op args[1]
  13.6 0.1 maximum_dynamic-update-slice_fusion
  13.7 0.9 bitcast_dynamic-update-slice_fusion.refs_0_
  14.7 5.9 %collective-permute-start = (bf16[16,176,128]{2,1,0:T(8,128)(2,1)S(1)}, bf16[16,176,128]{2,1,0:T(8,128)(2,1)S(1)}, u32[]{:S(2)}, u32[]{:S(2)}) collective-permute-start(bf16[16,176,128]{2,1,0:T(8,128)(2,1)S(1)} %bitcast_dynamic-update-slice_fusion.refs_0_), channel_id=1, source_target_pairs={{0,224},{32,0},{64,32},{96,64},{128,96},{160,128},{192,160},{224,1... | collective-permute-start | bytes 2162696 | tf_op jit(solution)/shard_map/ppermute | solution.py:307
  20.6 8.7 %all_gather.9 = s32[8,64,2]{1,2,0:T(2,128)S(1)} all-gather(s32[1,64,2]{1,2,0:T(2,128)S(1)} %copy-done.13), channel_id=1, replica_groups=mesh['z'=8,'x'=4,'c'=2,'y'=4] {'x','c'}, dimensions={0}, use_global_device_ids=true | all-gather | bytes 4608 | tf_op jit(solution)/shard_map/all_gather | solution.py:359
  29.3 0.1 copy.116
  29.4 4.9 %collective-permute-done.refs_0_ = bf16[16,176,128]{2,1,0:T(8,128)(2,1)S(1)} collective-permute-done((bf16[16,176,128]{2,1,0:T(8,128)(2,1)S(1)}, bf16[16,176,128]{2,1,0:T(8,128)(2,1)S(1)}, u32[]{:S(2)}, u32[]{:S(2)}) %collective-permute-start) | collective-permute-done | bytes 720928 | tf_op jit(solution)/shard_map/ppermute | solution.py:307
  34.3 3.7 %collective-permute-start.1 = (bf16[16,176,128]{2,1,0:T(8,128)(2,1)S(1)}, bf16[16,176,128]{2,1,0:T(8,128)(2,1)S(1)}, u32[]{:S(2)}, u32[]{:S(2)}) collective-permute-start(bf16[16,176,128]{2,1,0:T(8,128)(2,1)S(1)} %collective-permute-done.refs_0_), channel_id=1, source_target_pairs={{0,224},{32,0},{64,32},{96,64},{128,96},{160,128},{192,160},{224,1... | collective-permute-start | bytes 2162696 | tf_op jit(solution)/shard_map/ppermute | solution.py:307
  38.0 0.1 copy.105.asked
  38.1 1.5 take.5
  39.6 4.8 %all-to-all-start = ((bf16[8,352,128]{2,1,0:T(8,128)(2,1)}), bf16[8,352,128]{2,1,0:T(8,128)(2,1)S(1)}, u32[]{:S(2)}, u32[]{:S(2)}) async-start(bf16[8,352,128]{2,1,0:T(8,128)(2,1)} %bitcast.13), calls=%async_computation | async-start | bytes 1441792 | tf_op jit(solution)/shard_map/all_to_all | solution.py:408
  44.4 0.1 copy.100
  44.5 0.1 copy.101
  44.6 0.1 copy.102
  44.7 0.1 copy.103
  44.8 6.1 %collective-permute-done.1.refs_2_ = bf16[16,176,128]{2,1,0:T(8,128)(2,1)S(1)} collective-permute-done((bf16[16,176,128]{2,1,0:T(8,128)(2,1)S(1)}, bf16[16,176,128]{2,1,0:T(8,128)(2,1)S(1)}, u32[]{:S(2)}, u32[]{:S(2)}) %collective-permute-start.1) | collective-permute-done | bytes 720928 | tf_op jit(solution)/shard_map/ppermute | solution.py:307
  50.8 3.5 %collective-permute-done.4.refs_3_ = bf16[16,176,128]{2,1,0:T(8,128)(2,1)} collective-permute-done((bf16[16,176,128]{2,1,0:T(8,128)(2,1)S(1)}, bf16[16,176,128]{2,1,0:T(8,128)(2,1)}, u32[]{:S(2)}, u32[]{:S(2)}) %collective-permute-start.4) | collective-permute-done | bytes 720928 | tf_op jit(solution)/shard_map/ppermute | solution.py:306
  54.4 2.9 %take.4 = bf16[8,8,176,128]{3,2,1,0:T(8,128)(2,1)} custom-call(s32[4,8,2]{2,1,0:T(8,128)S(1)} %pad_add_fusion.asked, bf16[16,176,128]{2,1,0:T(8,128)(2,1)S(1)} %collective-permute-done.refs_0_, bf16[16,176,128]{2,1,0:T(8,128)(2,1)S(1)} %collective-permute-done.3.refs_1_, bf16[16,176,128]{2,1,0:T(8,128)(2,1)S(1)} %collective-permute-done.1.refs_2_, ...), custom_call_target="tpu_custom_call" | custom-call | bytes 6000000 | tf_op jit(solution)/shard_map/take/pallas_call | solution.py:210
  57.3 0.8 copy-done.3
  58.1 4.8 %all-to-all-start.1 = ((bf16[8,1408,128]{2,1,0:T(8,128)(2,1)}), bf16[8,1408,128]{2,1,0:T(8,128)(2,1)S(1)}, u32[]{:S(2)}, u32[]{:S(2)}) async-start(bf16[8,1408,128]{2,1,0:T(8,128)(2,1)} %bitcast.15), calls=%async_computation.1 | async-start | bytes 5767168 | tf_op jit(solution)/shard_map/all_to_all | solution.py:408
  62.9 0.1 copy.106
  63.1 0.8 pad_maximum_fusion.1
  63.8 0.1 collective-permute-start.5
  63.9 3.2 %collective-permute-start.2 = (bf16[16,176,128]{2,1,0:T(8,128)(2,1)}, bf16[16,176,128]{2,1,0:T(8,128)(2,1)}, u32[]{:S(2)}, u32[]{:S(2)}) collective-permute-start(bf16[16,176,128]{2,1,0:T(8,128)(2,1)} %copy-done.6), channel_id=1, source_target_pairs={{0,224},{32,0},{64,32},{96,64},{128,96},{160,128},{192,160},{224,1... | collective-permute-start | bytes 2162696 | tf_op jit(solution)/shard_map/ppermute | solution.py:307
  67.2 0.1 copy.112
  67.3 0.1 copy.95.asked
  67.4 0.1 copy.107
  67.4 0.1 reshape_squeeze.3
  67.6 1.3 select_reduce_fusion
  68.9 14.7 %collective-permute-done.5.refs_1_ = bf16[16,176,128]{2,1,0:T(8,128)(2,1)} collective-permute-done((bf16[16,176,128]{2,1,0:T(8,128)(2,1)}, bf16[16,176,128]{2,1,0:T(8,128)(2,1)}, u32[]{:S(2)}, u32[]{:S(2)}) %collective-permute-start.5) | collective-permute-done | bytes 720928 | tf_op jit(solution)/shard_map/ppermute | solution.py:306
  83.6 1.8 slice.73
  85.4 1.8 slice.74
  87.2 3.2 %collective-permute-start.7 = (bf16[8,176,128]{2,1,0:T(8,128)(2,1)}, bf16[8,176,128]{2,1,0:T(8,128)(2,1)}, u32[]{:S(2)}, u32[]{:S(2)}) collective-permute-start(bf16[8,176,128]{2,1,0:T(8,128)(2,1)} %slice.74), channel_id=1, source_target_pairs={{0,224},{32,0},{64,32},{96,64},{128,96},{160,128},{192,160},{224,1... | collective-permute-start | bytes 1081352 | tf_op jit(solution)/shard_map/ppermute | solution.py:310
  90.4 0.7 broadcast_subtract_fusion.1
  91.2 0.7 sub.70
  91.9 1.1 copy.114
  93.1 3.4 %collective-permute-done.6.refs_2_ = bf16[8,176,128]{2,1,0:T(8,128)(2,1)S(1)} collective-permute-done((bf16[8,176,128]{2,1,0:T(8,128)(2,1)}, bf16[8,176,128]{2,1,0:T(8,128)(2,1)S(1)}, u32[]{:S(2)}, u32[]{:S(2)}) %collective-permute-start.6) | collective-permute-done | bytes 360480 | tf_op jit(solution)/shard_map/ppermute | solution.py:310
  96.5 1.1 collective-permute-done.7.refs_3_
  97.6 1.7 take.3
  99.3 1.3 copy-done.2
  100.7 0.6 collective-permute-start.9
  101.3 5.8 %all-to-all-start.2 = ((bf16[8,1056,128]{2,1,0:T(8,128)(2,1)}), bf16[8,1056,128]{2,1,0:T(8,128)(2,1)}, u32[]{:S(2)}, u32[]{:S(2)}) async-start(bf16[8,1056,128]{2,1,0:T(8,128)(2,1)} %bitcast.44), calls=%async_computation.2 | async-start | bytes 4325376 | tf_op jit(solution)/shard_map/all_to_all | solution.py:408
  107.1 0.9 collective-permute-start.10
  108.0 0.8 slice.59
  108.9 0.1 copy.118
  109.0 24.7 %all-to-all-done.2 = bf16[8,1056,128]{2,1,0:T(8,128)(2,1)} async-done(((bf16[8,1056,128]{2,1,0:T(8,128)(2,1)}), bf16[8,1056,128]{2,1,0:T(8,128)(2,1)}, u32[]{:S(2)}, u32[]{:S(2)}) %all-to-all-start.2) | async-done | bytes 2162720 | tf_op jit(solution)/shard_map/all_to_all | solution.py:408
  133.7 0.9 collective-permute-start.11
  134.6 0.7 collective-permute-done.9.refs_3_
  135.2 23.6 %attend_own.1 = (bf16[64,64,512]{2,1,0:T(8,128)(2,1)}, f32[64,128]{1,0:T(8,128)}) custom-call(s32[64,16]{1,0:T(8,128)} %get-tuple-element.52.sel, s32[64,16]{1,0:T(8,128)} %get-tuple-element.35.lim, s32[1]{0:T(128)} %bitcast.23.quarter, bf16[64,32,576]{2,1,0:T(8,128)(2,1)} %q_own.5, bf16[64,32,576]{2,1,0:T(8,128)(2,1)} %collective-permute-done.8.q_pair, ...), custom_call_target="tpu_custom_call" | custom-call | flops 25600000000 | bytes 12000000 | tf_op jit(solution)/shard_map/attend_own/pallas_call | solution.py:166
  158.9 1.8 copy-done.1
  160.7 7.0 %index.1 = f32[64,2048]{1,0:T(8,128)} custom-call(s32[64,16]{1,0:T(8,128)S(1)} %copy-done.7, s32[1]{0:T(128)} %bitcast.23.quarter, bf16[4,68,16,128]{3,2,1,0:T(8,128)(2,1)S(1)} %bitcast.49, f32[64,64]{1,0:T(8,128)S(1)} %bitcast.50, s32[64,512]{1,0:T(8,128)S(1)} %broadcast_subtract_fusion.lim, bf16[16,176,128]{2,1,0:T(8,128)(2,1)S(1)} %bitcast.47, ...), custom_call_target="tpu_custom_call" | custom-call | tf_op jit(solution)/shard_map/index/pallas_call | solution.py:291
  167.8 19.8 %attend_merge.2 = (bf16[48,32,512]{2,1,0:T(8,128)(2,1)}, bf16[48,32,512]{2,1,0:T(8,128)(2,1)}, f32[48,128]{1,0:T(8,128)}) custom-call(s32[64,16]{1,0:T(8,128)} %get-tuple-element.52.sel, s32[64,16]{1,0:T(8,128)} %get-tuple-element.35.lim, s32[1]{0:T(128)} %bitcast.26.quarter, bf16[64,32,576]{2,1,0:T(8,128)(2,1)} %q_own.5, ...), custom_call_target="tpu_custom_call" | custom-call | flops 19200000000 | bytes 12000000 | tf_op jit(solution)/shard_map/attend_merge/pallas_call | solution.py:166
  187.6 4.5 %collective-permute-start.13 = (bf16[48,32,512]{2,1,0:T(8,128)(2,1)}, bf16[48,32,512]{2,1,0:T(8,128)(2,1)S(1)}, u32[]{:S(2)}, u32[]{:S(2)}) collective-permute-start(bf16[48,32,512]{2,1,0:T(8,128)(2,1)} %get-tuple-element.54), channel_id=1, source_target_pairs={{0,3},{1,2},{2,1},{3,0},{4,5},{5,4},{6,7},{7,6},{8,11},{9,10},{10,... | collective-permute-start | bytes 4718600 | tf_op jit(solution)/shard_map/ppermute | solution.py:439
  192.1 1.2 reduce-scatter.2.cloned.1.call-done
  193.4 11.1 %attend_merge.3 = (bf16[16,32,512]{2,1,0:T(8,128)(2,1)}, bf16[16,32,512]{2,1,0:T(8,128)(2,1)}, f32[16,128]{1,0:T(8,128)}) custom-call(s32[64,16]{1,0:T(8,128)} %get-tuple-element.52.sel, s32[64,16]{1,0:T(8,128)} %get-tuple-element.35.lim, s32[1]{0:T(128)} %bitcast.26.quarter, bf16[64,32,576]{2,1,0:T(8,128)(2,1)} %q_own.5, ...), custom_call_target="tpu_custom_call" | custom-call | flops 6400000000 | bytes 12000000 | tf_op jit(solution)/shard_map/attend_merge/pallas_call | solution.py:166
  204.5 0.9 slice.62
  205.4 0.6 collective-permute-start.14
  206.0 2.7 %collective-permute-start.12 = (f32[64,32]{1,0:T(8,128)S(1)}, f32[64,32]{1,0:T(8,128)S(1)}, u32[]{:S(2)}, u32[]{:S(2)}) collective-permute-start(f32[64,32]{1,0:T(8,128)S(1)} %pad_maximum_fusion.2), channel_id=1, source_target_pairs={{0,3},{1,2},{2,1},{3,0},{4,5},{5,4},{6,7},{7,6},{8,11},{9,10},{10,... | collective-permute-start | bytes 24584 | tf_op jit(solution)/shard_map/ppermute | solution.py:442
  208.7 8.0 %collective-permute-done.12 = f32[64,32]{1,0:T(8,128)S(1)} collective-permute-done((f32[64,32]{1,0:T(8,128)S(1)}, f32[64,32]{1,0:T(8,128)S(1)}, u32[]{:S(2)}, u32[]{:S(2)}) %collective-permute-start.12) | collective-permute-done | bytes 8224 | tf_op jit(solution)/shard_map/ppermute | solution.py:442
  216.7 0.7 add_divide_fusion.3
  217.5 1.3 add_convert_fusion.1
  218.8 0.7 add_convert_fusion
  219.5 1.5 pad_maximum_fusion
  (61 shorter events, 0.7 us)
Async XLA Ops:
  7.2 50.1 %collective-permute-start.8 = (bf16[64,32,576]{2,1,0:T(8,128)(2,1)}, bf16[64,32,576]{2,1,0:T(8,128)(2,1)}, u32[]{:S(2)}, u32[]{:S(2)}) collective-permute-start(bf16[64,32,576]{2,1,0:T(8,128)(2,1)} %q_own.5), channel_id=1, source_target_pairs={{0,3},{1,2},{2,1},{3,0},{4,5},{5,4},{6,7},{7,6},{8,11},{9,10},{10,... | collective-permute-start | bytes 7077896 | tf_op jit(solution)/shard_map/ppermute | solution.py:354
  13.4 7.3 %copy-start.13 = (s32[1,64,2]{1,2,0:T(2,128)S(1)}, s32[1,64,2]{1,2,0:T(2,128)}, u32[]{:S(2)}) copy-start(s32[1,64,2]{1,2,0:T(2,128)} %param.12) | copy-start | bytes 1540
  14.7 19.6 %collective-permute-start = (bf16[16,176,128]{2,1,0:T(8,128)(2,1)S(1)}, bf16[16,176,128]{2,1,0:T(8,128)(2,1)S(1)}, u32[]{:S(2)}, u32[]{:S(2)}) collective-permute-start(bf16[16,176,128]{2,1,0:T(8,128)(2,1)S(1)} %bitcast_dynamic-update-slice_fusion.refs_0_), channel_id=1, source_target_pairs={{0,224},{32,0},{64,32},{96,64},{128,96},{160,128},{192,160},{224,1... | collective-permute-start | bytes 2162696 | tf_op jit(solution)/shard_map/ppermute | solution.py:307
  20.6 17.4 %collective-permute-start.3 = (bf16[16,176,128]{2,1,0:T(8,128)(2,1)S(1)}, bf16[16,176,128]{2,1,0:T(8,128)(2,1)S(1)}, u32[]{:S(2)}, u32[]{:S(2)}) collective-permute-start(bf16[16,176,128]{2,1,0:T(8,128)(2,1)S(1)} %bitcast_dynamic-update-slice_fusion.refs_0_), channel_id=1, source_target_pairs={{0,32},{32,64},{64,96},{96,128},{128,160},{160,192},{192,224},{224... | collective-permute-start | bytes 2162696 | tf_op jit(solution)/shard_map/ppermute | solution.py:306
  34.3 16.5 %collective-permute-start.1 = (bf16[16,176,128]{2,1,0:T(8,128)(2,1)S(1)}, bf16[16,176,128]{2,1,0:T(8,128)(2,1)S(1)}, u32[]{:S(2)}, u32[]{:S(2)}) collective-permute-start(bf16[16,176,128]{2,1,0:T(8,128)(2,1)S(1)} %collective-permute-done.refs_0_), channel_id=1, source_target_pairs={{0,224},{32,0},{64,32},{96,64},{128,96},{160,128},{192,160},{224,1... | collective-permute-start | bytes 2162696 | tf_op jit(solution)/shard_map/ppermute | solution.py:307
  38.0 16.4 %collective-permute-start.4 = (bf16[16,176,128]{2,1,0:T(8,128)(2,1)S(1)}, bf16[16,176,128]{2,1,0:T(8,128)(2,1)}, u32[]{:S(2)}, u32[]{:S(2)}) collective-permute-start(bf16[16,176,128]{2,1,0:T(8,128)(2,1)S(1)} %collective-permute-done.3.refs_1_), channel_id=1, source_target_pairs={{0,32},{32,64},{64,96},{96,128},{128,160},{160,192},{192,224},{224... | collective-permute-start | bytes 2162696 | tf_op jit(solution)/shard_map/ppermute | solution.py:306
  39.6 17.6 %all-to-all-start = ((bf16[8,352,128]{2,1,0:T(8,128)(2,1)}), bf16[8,352,128]{2,1,0:T(8,128)(2,1)S(1)}, u32[]{:S(2)}, u32[]{:S(2)}) async-start(bf16[8,352,128]{2,1,0:T(8,128)(2,1)} %bitcast.13), calls=%async_computation | async-start | bytes 1441792 | tf_op jit(solution)/shard_map/all_to_all | solution.py:408
  50.8 6.4 %copy-start.6 = (bf16[16,176,128]{2,1,0:T(8,128)(2,1)}, bf16[16,176,128]{2,1,0:T(8,128)(2,1)S(1)}, u32[]{:S(2)}) copy-start(bf16[16,176,128]{2,1,0:T(8,128)(2,1)S(1)} %collective-permute-done.1.refs_2_) | copy-start | bytes 2162692
  57.2 0.9 copy-start.3
  57.3 5.7 %copy-start.12 = (bf16[64,16]{0,1:T(8,128)(2,1)S(1)}, bf16[64,16]{0,1:T(8,128)(2,1)}, u32[]{:S(2)}) copy-start(bf16[64,16]{0,1:T(8,128)(2,1)} %param.10) | copy-start | bytes 6148
  57.3 5.8 %copy-start.9 = (bf16[64,16,128]{2,1,0:T(8,128)(2,1)S(1)}, bf16[64,16,128]{2,1,0:T(8,128)(2,1)}, u32[]{:S(2)}) copy-start(bf16[64,16,128]{2,1,0:T(8,128)(2,1)} %param.9) | copy-start | bytes 786436
  57.3 10.1 %copy-start.11 = (s32[64,16]{0,1:T(8,128)S(1)}, s32[64,16]{0,1:T(8,128)}, u32[]{:S(2)}) copy-start(s32[64,16]{0,1:T(8,128)} %param.13) | copy-start | bytes 12292
  58.1 42.6 %all-to-all-start.1 = ((bf16[8,1408,128]{2,1,0:T(8,128)(2,1)}), bf16[8,1408,128]{2,1,0:T(8,128)(2,1)S(1)}, u32[]{:S(2)}, u32[]{:S(2)}) async-start(bf16[8,1408,128]{2,1,0:T(8,128)(2,1)} %bitcast.15), calls=%async_computation.1 | async-start | bytes 5767168 | tf_op jit(solution)/shard_map/all_to_all | solution.py:408
  62.9 37.7 %all-gather.3.cloned.1.call-start = ((), (), s32[]{:S(2)}) async-start(), calls=%async_computation.5 | async-start | bytes 1392640 | tf_op jit(solution)/shard_map/all_gather | solution.py:357
  63.8 19.8 %collective-permute-start.5 = (bf16[16,176,128]{2,1,0:T(8,128)(2,1)}, bf16[16,176,128]{2,1,0:T(8,128)(2,1)}, u32[]{:S(2)}, u32[]{:S(2)}) collective-permute-start(bf16[16,176,128]{2,1,0:T(8,128)(2,1)} %collective-permute-done.4.refs_3_), channel_id=1, source_target_pairs={{0,32},{32,64},{64,96},{96,128},{128,160},{160,192},{192,224},{224... | collective-permute-start | bytes 2162696 | tf_op jit(solution)/shard_map/ppermute | solution.py:306
  63.9 21.5 %collective-permute-start.2 = (bf16[16,176,128]{2,1,0:T(8,128)(2,1)}, bf16[16,176,128]{2,1,0:T(8,128)(2,1)}, u32[]{:S(2)}, u32[]{:S(2)}) collective-permute-start(bf16[16,176,128]{2,1,0:T(8,128)(2,1)} %copy-done.6), channel_id=1, source_target_pairs={{0,224},{32,0},{64,32},{96,64},{128,96},{160,128},{192,160},{224,1... | collective-permute-start | bytes 2162696 | tf_op jit(solution)/shard_map/ppermute | solution.py:307
  85.4 11.1 %collective-permute-start.6 = (bf16[8,176,128]{2,1,0:T(8,128)(2,1)}, bf16[8,176,128]{2,1,0:T(8,128)(2,1)S(1)}, u32[]{:S(2)}, u32[]{:S(2)}) collective-permute-start(bf16[8,176,128]{2,1,0:T(8,128)(2,1)} %slice.73), channel_id=1, source_target_pairs={{0,32},{32,64},{64,96},{96,128},{128,160},{160,192},{192,224},{224... | collective-permute-start | bytes 1081352 | tf_op jit(solution)/shard_map/ppermute | solution.py:310
  87.2 10.4 %collective-permute-start.7 = (bf16[8,176,128]{2,1,0:T(8,128)(2,1)}, bf16[8,176,128]{2,1,0:T(8,128)(2,1)}, u32[]{:S(2)}, u32[]{:S(2)}) collective-permute-start(bf16[8,176,128]{2,1,0:T(8,128)(2,1)} %slice.74), channel_id=1, source_target_pairs={{0,224},{32,0},{64,32},{96,64},{128,96},{160,128},{192,160},{224,1... | collective-permute-start | bytes 1081352 | tf_op jit(solution)/shard_map/ppermute | solution.py:310
  99.3 1.3 copy-start.2
  100.6 34.6 %copy-start = (bf16[8,1408,128]{2,1,0:T(8,128)(2,1)}, bf16[8,1408,128]{2,1,0:T(8,128)(2,1)S(1)}, u32[]{:S(2)}) copy-start(bf16[8,1408,128]{2,1,0:T(8,128)(2,1)S(1)} %all-to-all-done.1) | copy-start | bytes 8650756
  100.7 34.6 %collective-permute-start.9 = (bf16[64,176,128]{2,1,0:T(8,128)(2,1)S(1)}, bf16[64,176,128]{2,1,0:T(8,128)(2,1)}, u32[]{:S(2)}, u32[]{:S(2)}) collective-permute-start(bf16[64,176,128]{2,1,0:T(8,128)(2,1)S(1)} %bitcast.41), channel_id=1, source_target_pairs={{0,1},{1,0},{2,3},{3,2},{4,7},{5,6},{6,5},{7,4},{8,9},{9,8},{10,11... | collective-permute-start | bytes 8650760 | tf_op jit(solution)/shard_map/ppermute | solution.py:404
  101.3 32.4 %all-to-all-start.2 = ((bf16[8,1056,128]{2,1,0:T(8,128)(2,1)}), bf16[8,1056,128]{2,1,0:T(8,128)(2,1)}, u32[]{:S(2)}, u32[]{:S(2)}) async-start(bf16[8,1056,128]{2,1,0:T(8,128)(2,1)} %bitcast.44), calls=%async_computation.2 | async-start | bytes 4325376 | tf_op jit(solution)/shard_map/all_to_all | solution.py:408
  107.1 86.2 %reduce-scatter.2.cloned.1.call-start = ((), (), s32[]{:S(2)}) async-start(), calls=%async_computation.4 | async-start | bytes 655360 | tf_op jit(solution)/shard_map/reduce_scatter | solution.py:422
  107.1 51.8 %collective-permute-start.10 = (bf16[16,176,128]{2,1,0:T(8,128)(2,1)}, bf16[16,176,128]{2,1,0:T(8,128)(2,1)}, u32[]{:S(2)}, u32[]{:S(2)}) collective-permute-start(bf16[16,176,128]{2,1,0:T(8,128)(2,1)} %bitcast.45), channel_id=1, source_target_pairs={{0,1},{1,0},{2,3},{3,2},{4,7},{5,6},{6,5},{7,4},{8,9},{9,8},{10,11... | collective-permute-start | bytes 2162696 | tf_op jit(solution)/shard_map/ppermute | solution.py:412
  133.7 34.1 %collective-permute-start.11 = (bf16[48,176,128]{2,1,0:T(8,128)(2,1)}, bf16[48,176,128]{2,1,0:T(8,128)(2,1)}, u32[]{:S(2)}, u32[]{:S(2)}) collective-permute-start(bf16[48,176,128]{2,1,0:T(8,128)(2,1)} %bitcast.25.refs_2_), channel_id=1, source_target_pairs={{0,1},{1,0},{2,3},{3,2},{4,7},{5,6},{6,5},{7,4},{8,9},{9,8},{10,11... | collective-permute-start | bytes 6488072 | tf_op jit(solution)/shard_map/ppermute | solution.py:412
  135.2 23.7 %copy-start.4 = (bf16[8,352,128]{2,1,0:T(8,128)(2,1)S(1)}, bf16[8,352,128]{2,1,0:T(8,128)(2,1)}, u32[]{:S(2)}) copy-start(bf16[8,352,128]{2,1,0:T(8,128)(2,1)} %copy-done.3) | copy-start | bytes 2162692
  135.2 23.7 %copy-start.5 = (bf16[272,16,128]{2,1,0:T(8,128)(2,1)S(1)}, bf16[272,16,128]{2,1,0:T(8,128)(2,1)}, u32[]{:S(2)}) copy-start(bf16[272,16,128]{2,1,0:T(8,128)(2,1)} %all-gather.3.cloned.1.call-done) | copy-start | bytes 3342340
  135.2 23.7 %copy-start.7 = (s32[64,16]{1,0:T(8,128)S(1)}, s32[64,16]{1,0:T(8,128)}, u32[]{:S(2)}) copy-start(s32[64,16]{1,0:T(8,128)} %get-tuple-element.52.sel) | copy-start | bytes 12292
  158.9 1.8 copy-start.1
  187.6 31.2 %collective-permute-start.13 = (bf16[48,32,512]{2,1,0:T(8,128)(2,1)}, bf16[48,32,512]{2,1,0:T(8,128)(2,1)S(1)}, u32[]{:S(2)}, u32[]{:S(2)}) collective-permute-start(bf16[48,32,512]{2,1,0:T(8,128)(2,1)} %get-tuple-element.54), channel_id=1, source_target_pairs={{0,3},{1,2},{2,1},{3,0},{4,5},{5,4},{6,7},{7,6},{8,11},{9,10},{10,... | collective-permute-start | bytes 4718600 | tf_op jit(solution)/shard_map/ppermute | solution.py:439
  193.4 12.0 %copy-start.10 = (f32[48,128]{1,0:T(8,128)S(1)}, f32[48,128]{1,0:T(8,128)}, u32[]{:S(2)}) copy-start(f32[48,128]{1,0:T(8,128)} %get-tuple-element.51) | copy-start | bytes 73732
  204.5 14.4 %copy-start.8 = (bf16[48,32,512]{2,1,0:T(8,128)(2,1)S(1)}, bf16[48,32,512]{2,1,0:T(8,128)(2,1)}, u32[]{:S(2)}) copy-start(bf16[48,32,512]{2,1,0:T(8,128)(2,1)} %get-tuple-element.48) | copy-start | bytes 4718596
  205.4 12.0 %collective-permute-start.14 = (bf16[16,32,512]{2,1,0:T(8,128)(2,1)}, bf16[16,32,512]{2,1,0:T(8,128)(2,1)S(1)}, u32[]{:S(2)}, u32[]{:S(2)}) collective-permute-start(bf16[16,32,512]{2,1,0:T(8,128)(2,1)} %get-tuple-element.56), channel_id=1, source_target_pairs={{0,3},{1,2},{2,1},{3,0},{4,5},{5,4},{6,7},{7,6},{8,11},{9,10},{10,... | collective-permute-start | bytes 1572872 | tf_op jit(solution)/shard_map/ppermute | solution.py:439
  206.0 10.7 %collective-permute-start.12 = (f32[64,32]{1,0:T(8,128)S(1)}, f32[64,32]{1,0:T(8,128)S(1)}, u32[]{:S(2)}, u32[]{:S(2)}) collective-permute-start(f32[64,32]{1,0:T(8,128)S(1)} %pad_maximum_fusion.2), channel_id=1, source_target_pairs={{0,3},{1,2},{2,1},{3,0},{4,5},{5,4},{6,7},{7,6},{8,11},{9,10},{10,... | collective-permute-start | bytes 24584 | tf_op jit(solution)/shard_map/ppermute | solution.py:442
Sparse Core Ops, SparseCore 0:
  65.6 26.2 all-gather.2
  167.9 25.4 reduce-scatter.1
